TPU v7x, 32 devices: a whole 2x2x4 slice. The times are simulated.
32 devices in a mesh: occ: 4 (over y, x), aux: 8 (over z, core).
Axes of the slice: x: 2, y: 2, z: 4, core: 2. Of those that a mesh axis runs over, the one named last changes fastest.
Arguments:
- integrals: bfloat16 [16384, 16, 256], P(('aux', 'occ')), may hold values from -0.59765625 to 0.59765625
- eps_occ: float32 [1024], replicated, may hold values from -3 to -0.5
- eps_vir: float32 [4096], replicated, may hold values from 0.5 to 4
- src_occ: int32 [4], replicated, may hold values from 0 to 15
- occ_offset: int32 [1], replicated, may hold values from 0 to 1008
- vir_offset: int32 [1], replicated, may hold values from 0 to 3840
Outputs:
- density: bfloat16 [16384, 16, 256], P('aux', 'occ')
Inputs may be any that keep to these rules, and one draw needn't show every extreme that they name: `src_occ`: each entry is an occupied index inside the window. `occ_offset`: the window of 16 occupied orbitals lies inside the occupied energies. `vir_offset`: the block of 256 virtual orbitals lies inside the virtual energies.
All inputs are finite; a program needn't handle non-finite values.
Results may differ from a plain program's by a relative error of at most 0.009.
Values may be sent and summed in bfloat16 or wider, within the bound.
No kernel may reach another device: no remote copies, remote signals or barrier semaphores. Data moves between devices by JAX's collectives and lax.ppermute only.
A program may use at most 64 MiB of HBM per device.

v0:
```python
import jax
import jax.numpy as jnp
from jax import lax
from jax.sharding import PartitionSpec as P

NSRC = 4


def spread(value, axis, source):
    kept = jnp.where(lax.axis_index(axis) == source, value, 0).astype(value.dtype)
    return lax.psum(kept, axis)


def local(integrals, eps_occ, eps_vir, src_occ, occ_offset, vir_offset):
    owned_ints = lax.all_to_all(integrals, "occ", split_axis=1, concat_axis=0, tiled=True)
    aux_rows, occ_count, virt_count = owned_ints.shape
    my_occ = lax.axis_index("occ")
    occ_energy = lax.dynamic_slice_in_dim(eps_occ, occ_offset[0] + my_occ * occ_count, occ_count)
    vir_energy = lax.dynamic_slice_in_dim(eps_vir, vir_offset[0], virt_count)
    flat_ints = owned_ints.reshape(aux_rows, occ_count * virt_count)
    local_index = src_occ % occ_count
    owner_index = src_occ // occ_count
    density_sum = jnp.zeros((aux_rows, occ_count * virt_count), jnp.float32)
    for source_step in range(NSRC):
        candidate = lax.dynamic_index_in_dim(
            owned_ints, local_index[source_step], 1, keepdims=False
        )
        source = spread(candidate, "occ", owner_index[source_step])
        partial_value = lax.dot_general(
            flat_ints, source, (((0,), (0,)), ((), ())), preferred_element_type=jnp.float32
        )
        partial_value = partial_value.reshape(occ_count, virt_count, virt_count)
        src_energy = lax.dynamic_index_in_dim(
            eps_occ, occ_offset[0] + src_occ[source_step], 0, keepdims=False
        )
        pair_sum = lax.psum(partial_value, "aux")
        denom = (
            vir_energy[None, :, None]
            + vir_energy[None, None, :]
            - occ_energy[:, None, None]
            - src_energy
        )
        scaled = (pair_sum / denom).astype(jnp.bfloat16)
        scaled_wide = scaled.astype(jnp.float32)
        amplitude = (2.0 * scaled_wide - jnp.transpose(scaled_wide, (0, 2, 1))).astype(jnp.bfloat16)
        density_sum = density_sum + lax.dot_general(
            source,
            amplitude.reshape(occ_count * virt_count, virt_count),
            (((1,), (1,)), ((), ())),
            preferred_element_type=jnp.float32,
        )
    return density_sum.astype(jnp.bfloat16).reshape(aux_rows, occ_count, virt_count)


def solution(mesh):
    in_specs = (P(("aux", "occ"), None, None), P(), P(), P(), P(), P())
    out_specs = P("aux", "occ", None)
    return jax.shard_map(local, mesh=mesh, in_specs=in_specs, out_specs=out_specs, check_vma=False)
```

profile of v0, /device:TPU:0, one launch (start us, length us, event | category | flops | bytes accessed | tf_op | source)
XLA Modules:
  0.0 351.6 jit_solution(5088492435911307812)
XLA Ops:
  6.5 5.7 %copy.26 = bf16[512,16,256]{2,0,1:T(8,128)(2,1)} copy(bf16[512,16,256]{2,1,0:T(8,128)(2,1)} %param.6) | data formatting | bytes 8388608 | tf_op args[0]
  12.2 5.3 %all-to-all-start = ((bf16[512,16,256]{2,0,1:T(8,128)(2,1)}), bf16[512,16,256]{2,0,1:T(8,128)(2,1)}, u32[]{:S(2)}, u32[]{:S(2)}) async-start(bf16[512,16,256]{2,0,1:T(8,128)(2,1)} %copy.26), calls=%async_computation | async-start | bytes 8388608 | tf_op jit(solution)/shard_map/all_to_all | solution.py:15
  28.2 37.9 %all-to-all-done = bf16[512,16,256]{2,0,1:T(8,128)(2,1)} async-done(((bf16[512,16,256]{2,0,1:T(8,128)(2,1)}), bf16[512,16,256]{2,0,1:T(8,128)(2,1)}, u32[]{:S(2)}, u32[]{:S(2)}) %all-to-all-start) | async-done | bytes 4194336 | tf_op jit(solution)/shard_map/all_to_all | solution.py:15
  66.1 2.5 copy.27
  68.6 2.1 select_bitcast_fusion
  70.9 5.4 %copy.28 = bf16[4,512,4,256]{3,2,1,0:T(4,128)(2,1)S(1)} copy(bf16[4,512,4,256]{3,1,2,0:T(8,128)(2,1)} %bitcast.2) | data formatting | bytes 8388608 | tf_op jit(solution)/shard_map/all_to_all | solution.py:15
  76.4 3.1 copy.46
  79.4 96.9 %all-reduce.7.cloned.1.call-done = (bf16[2048,256]{1,0:T(8,128)(2,1)}, bf16[2048,256]{1,0:T(8,128)(2,1)}, bf16[2048,256]{1,0:T(8,128)(2,1)}, bf16[2048,256]{1,0:T(8,128)(2,1)}) async-done(((bf16[2048,256]{1,0:T(8,128)(2,1)}, bf16[2048,256]{1,0:T(8,128)(2,1)}, bf16[2048,256]{1,0:T(8,128)(2,1)}, bf16[2048,256]{1,0:T(8,128)(2,1)}), (bf16[2048,256]{1,0:T(8,128)(2,1)}, bf16[2048,256]{1,0:T(8,128)(2,1)}, ...) | async-done | bytes 4194320 | tf_op jit(solution)/shard_map/psum | solution.py:11
  176.3 3.9 %convolution_bitcast_fusion.1 = f32[1024,256]{0,1:T(8,128)S(1)} fusion(bf16[2048,256]{1,0:T(8,128)(2,1)} %get-tuple-element.9, bf16[2048,1024]{1,0:T(8,128)(2,1)} %bitcast.95), kind=kOutput, calls=%fused_computation.6 | convolution fusion | flops 1073741824 | bytes 6291456 | tf_op jit(solution)/shard_map/dot_general | solution.py:29
  181.5 3.5 %convolution_bitcast_fusion.3 = f32[1024,256]{0,1:T(8,128)S(1)} fusion(bf16[2048,256]{1,0:T(8,128)(2,1)S(1)} %copy-done.3, bf16[2048,1024]{1,0:T(8,128)(2,1)} %bitcast.96), kind=kOutput, calls=%fused_computation.8 | convolution fusion | flops 1073741824 | bytes 6291456 | tf_op jit(solution)/shard_map/dot_general | solution.py:29
  186.3 3.6 %convolution_bitcast_fusion.2 = f32[1024,256]{0,1:T(8,128)S(1)} fusion(bf16[2048,256]{1,0:T(8,128)(2,1)S(1)} %copy-done.6, bf16[2048,1024]{1,0:T(8,128)(2,1)} %bitcast.97), kind=kOutput, calls=%fused_computation.7 | convolution fusion | flops 1073741824 | bytes 6291456 | tf_op jit(solution)/shard_map/dot_general | solution.py:29
  200.2 91.5 %all-reduce.5.cloned.1.call-done = (f32[4,256,256]{2,1,0:T(8,128)}, f32[4,256,256]{2,1,0:T(8,128)}, f32[4,256,256]{2,1,0:T(8,128)}, f32[4,256,256]{2,1,0:T(8,128)}) async-done(((f32[4,256,256]{2,1,0:T(8,128)}, f32[4,256,256]{2,1,0:T(8,128)}, f32[4,256,256]{2,1,0:T(8,128)}, f32[4,256,256]{2,1,0:T(8,128)}), (f32[4,256,256]{2,1,0:T(8,128)}, f32[4,256,256]{2,1,0:T(8,128)}, f32[4,256,256]{2,1,0:T(8,128)}, ...) | async-done | bytes 4194320 | tf_op jit(solution)/shard_map/psum | solution.py:36
  291.8 6.1 %fusion.13 = (f32[4,256,256]{2,1,0:T(8,128)S(1)}, f32[4,256,256]{2,1,0:T(8,128)S(1)}, f32[4,256,256]{2,1,0:T(8,128)S(1)}, bf16[4,256,256]{2,1,0:T(8,128)(2,1)}) fusion(f32[4,256,256]{2,1,0:T(8,128)} %get-tuple-element.8, f32[]{:T(128)} %bitcast.39, f32[4]{0:T(128)S(1)} %dynamic_slice.34, f32[256,256]{1,0:T(8,128)S(1)} %broadcast_add_fusion, ...), kind=kLoop, calls=%fused_computation.31 | loop fusion | flops 4194304 | bytes 8126496 | tf_op jit(solution)/shard_map/convert_element_type | solution.py:44
  297.9 2.0 copy.30
  300.0 2.1 convert_multiply_fusion
  302.1 2.5 copy.31
  304.6 2.3 fusion.1
  308.2 2.2 fusion.10
  310.3 2.0 copy.40
  315.9 2.6 fusion.21
  318.5 4.5 %fusion.22 = f32[2048,1024]{0,1:T(8,128)} fusion(bf16[2048,256]{1,0:T(8,128)(2,1)S(1)} %copy-done.5, bf16[1024,256]{1,0:T(8,128)(2,1)S(1)} %bitcast.104), kind=kOutput, calls=%fused_computation.46 | convolution fusion | flops 1073741824 | bytes 9961472 | tf_op jit(solution)/shard_map/dot_general | solution.py:46
  323.0 4.5 %fusion.20 = f32[2048,1024]{0,1:T(8,128)} fusion(bf16[2048,256]{1,0:T(8,128)(2,1)S(1)} %copy-done.4, bf16[1024,256]{1,0:T(8,128)(2,1)S(1)} %bitcast.106), kind=kOutput, calls=%fused_computation.44 | convolution fusion | flops 1073741824 | bytes 9961472 | tf_op jit(solution)/shard_map/dot_general | solution.py:46
  327.6 9.7 %add_convert_fusion = bf16[2048,1024]{0,1:T(8,128)(2,1)} fusion(f32[2048,1024]{0,1:T(8,128)} %fusion.22, f32[2048,1024]{0,1:T(8,128)} %fusion.20, f32[2048,1024]{0,1:T(8,128)S(1)} %fusion.21, bf16[2048,256]{1,0:T(8,128)(2,1)S(1)} %copy-done.8, bf16[1024,256]{1,0:T(8,128)(2,1)S(1)} %bitcast.103), kind=kOutput, calls=%fused_computation | convolution fusion | flops 1082130432 | bytes 30932992 | tf_op jit(solution)/shard_map/dot_general | solution.py:46
  337.3 7.4 %copy.41 = bf16[2048,4,256]{2,1,0:T(4,128)(2,1)} copy(bf16[2048,4,256]{0,2,1:T(8,128)(2,1)} %bitcast.94) | data formatting | bytes 8388608 | tf_op jit(solution)/shard_map/reshape | solution.py:52
  (45 shorter events, 14.6 us)
Async XLA Ops:
  12.2 5.3 %copy-start.9 = (s32[4]{0:T(128)S(1)}, s32[4]{0:T(128)}, u32[]{:S(2)}) copy-start(s32[4]{0:T(128)} %param.9) | copy-start | bytes 52
  12.2 53.9 %all-to-all-start = ((bf16[512,16,256]{2,0,1:T(8,128)(2,1)}), bf16[512,16,256]{2,0,1:T(8,128)(2,1)}, u32[]{:S(2)}, u32[]{:S(2)}) async-start(bf16[512,16,256]{2,0,1:T(8,128)(2,1)} %copy.26), calls=%async_computation | async-start | bytes 8388608 | tf_op jit(solution)/shard_map/all_to_all | solution.py:15
  17.5 158.8 %all-reduce.7.cloned.1.call-start = ((), (), s32[]{:S(2)}) async-start(), calls=%async_computation.2 | async-start | bytes 8388608 | tf_op jit(solution)/shard_map/psum | solution.py:11
  70.7 221.1 %all-reduce.5.cloned.1.call-start = ((), (), s32[]{:S(2)}) async-start(), calls=%async_computation.1 | async-start | bytes 8388608 | tf_op jit(solution)/shard_map/psum | solution.py:36
  176.3 5.2 %copy-start.3 = (bf16[2048,256]{1,0:T(8,128)(2,1)S(1)}, bf16[2048,256]{1,0:T(8,128)(2,1)}, u32[]{:S(2)}) copy-start(bf16[2048,256]{1,0:T(8,128)(2,1)} %get-tuple-element.10) | copy-start | bytes 3145732
  181.5 4.9 %copy-start.6 = (bf16[2048,256]{1,0:T(8,128)(2,1)S(1)}, bf16[2048,256]{1,0:T(8,128)(2,1)}, u32[]{:S(2)}) copy-start(bf16[2048,256]{1,0:T(8,128)(2,1)} %get-tuple-element.11) | copy-start | bytes 3145732
  186.3 3.6 %copy-start = (bf16[256,8,4,256]{3,1,2,0:T(8,128)(2,1)S(1)}, bf16[256,8,4,256]{3,1,2,0:T(8,128)(2,1)}, u32[]{:S(2)}) copy-start(bf16[256,8,4,256]{3,1,2,0:T(8,128)(2,1)} %copy.46) | copy-start | bytes 12582916
  186.3 3.7 %copy-start.7 = (bf16[2048,256]{1,0:T(8,128)(2,1)S(1)}, bf16[2048,256]{1,0:T(8,128)(2,1)}, u32[]{:S(2)}) copy-start(bf16[2048,256]{1,0:T(8,128)(2,1)} %get-tuple-element.12) | copy-start | bytes 3145732
  191.3 7.3 %copy-start.10 = (f32[1024]{0:T(1024)S(1)}, f32[1024]{0:T(1024)}, u32[]{:S(2)}) copy-start(f32[1024]{0:T(1024)} %param.7) | copy-start | bytes 12292
  315.8 2.6 copy-start.5
  318.5 4.6 %copy-start.2 = (bf16[4,256,256]{2,1,0:T(8,128)(2,1)S(1)}, bf16[4,256,256]{2,1,0:T(8,128)(2,1)}, u32[]{:S(2)}) copy-start(bf16[4,256,256]{2,1,0:T(8,128)(2,1)} %fusion.1) | copy-start | bytes 1572868
  318.5 4.6 %copy-start.4 = (bf16[2048,256]{1,0:T(8,128)(2,1)S(1)}, bf16[2048,256]{1,0:T(8,128)(2,1)}, u32[]{:S(2)}) copy-start(bf16[2048,256]{1,0:T(8,128)(2,1)} %get-tuple-element.10) | copy-start | bytes 3145732
  323.0 4.5 %copy-start.1 = (bf16[4,256,256]{2,1,0:T(8,128)(2,1)S(1)}, bf16[4,256,256]{2,1,0:T(8,128)(2,1)}, u32[]{:S(2)}) copy-start(bf16[4,256,256]{2,1,0:T(8,128)(2,1)} %copy.40) | copy-start | bytes 1572868
  323.0 4.5 %copy-start.8 = (bf16[2048,256]{1,0:T(8,128)(2,1)S(1)}, bf16[2048,256]{1,0:T(8,128)(2,1)}, u32[]{:S(2)}) copy-start(bf16[2048,256]{1,0:T(8,128)(2,1)} %get-tuple-element.12) | copy-start | bytes 3145732
Sparse Core Ops, SparseCore 0:
  70.8 105.3 all-reduce.6
  194.1 97.5 all-reduce.4
where the time goes:
time: 353 us; the launch traced here: 352 us
  waiting for transfers between devices  226 us (64%)
  local copies, waits for them, and re-layouts  42.6 us (12%)
  matrix products  33.7 us (10%)
  between operations  27.5 us (8%)
  other arithmetic  16 us (5%)
  starting transfers between devices  5.52 us (2%)
    psum x1, waiting for transfers between devices, spread(): return lax.psum(kept, axis)  96.9 us
    psum x1, waiting for transfers between devices, local(): pair_sum = lax.psum(partial_value, 'aux')  91.5 us
    all_to_all x1, waiting for transfers between devices, local(): lax.all_to_all(integrals, 'occ', split_axis=1, concat_axis=0, tiled=True)  37.9 us
    dot_general x4, matrix products, local(): lax.dot_general(source, amplitude.reshape(occ_count * virt_count, virt_co...  21.4 us
    dot_general x4, matrix products, local(): lax.dot_general(flat_ints, source, (((0,), (0,)), ((), ())), preferred_el...  12.3 us
    unnamed x24, local copies, waits for them, and re-layouts  8.88 us
    all_to_all x2, local copies, waits for them, and re-layouts, local(): lax.all_to_all(integrals, 'occ', split_axis=1, concat_axis=0, tiled=True)  7.88 us
    reshape x1, local copies, waits for them, and re-layouts, local(): density_sum.astype(jnp.bfloat16).reshape(aux_rows, occ_count, virt_count)  7.43 us
  transfers between devices with their start and end apart: 3, of which 3 were waited for; matrix products, arithmetic and copies ran while one was open for 3% of the time, Pallas kernels for 0%

commit v1 on v0

v1 whole, which is shorter than its diff:
```python
import functools

import jax
import jax.numpy as jnp
from jax import lax
from jax.experimental import pallas as pl
from jax.experimental.pallas import tpu as pltpu
from jax.sharding import PartitionSpec as P

F32, BF16 = jnp.float32, jnp.bfloat16
VMEM_LIMIT = 48 << 20


def swap(value, axis, size, mask):
    return lax.ppermute(value, axis, [(d, d ^ mask) for d in range(size)])


def whole(shape):
    return pl.BlockSpec(shape, lambda *_: (0,) * len(shape))


def prepare_kernel(counts, src_count, index_ref, src_ref, x_ref, *refs):
    halves, src_t, outs, turned = refs[:2], refs[2], refs[3:-1], refs[-1]
    turned[...] = jnp.swapaxes(x_ref[...], 0, 1)
    width = x_ref.shape[2]
    per_half = src_count // 2
    for s in range(src_count):
        block = turned[src_ref[s]]
        place = pl.ds((s % per_half) * width, width)
        halves[s // per_half][:, place] = block
        src_t[pl.ds(s * width, width), :] = block.T
    spot = 0
    for out, count in zip(outs, counts, strict=True):
        for j in range(count):
            out[j] = turned[index_ref[spot]]
            spot += 1


def prepare(integrals, order, src, counts):
    rows, occ_count, width = integrals.shape
    src_count = src.shape[0]
    step = min(rows, 128)
    half = src_count * width // 2
    shapes = [(rows, half)] * 2 + [(src_count * width, rows)] + [(c, rows, width) for c in counts]
    specs = (
        [pl.BlockSpec((step, half), lambda r, *_: (r, 0))] * 2
        + [pl.BlockSpec((src_count * width, step), lambda r, *_: (0, r))]
        + [pl.BlockSpec((c, step, width), lambda r, *_: (0, r, 0)) for c in counts]
    )
    return pl.pallas_call(
        functools.partial(prepare_kernel, counts, src_count),
        grid_spec=pltpu.PrefetchScalarGridSpec(
            num_scalar_prefetch=2,
            grid=(rows // step,),
            in_specs=[pl.BlockSpec((step, occ_count, width), lambda r, *_: (r, 0, 0))],
            out_specs=specs,
            scratch_shapes=[pltpu.VMEM((occ_count, step, width), BF16)],
        ),
        out_shape=[jax.ShapeDtypeStruct(s, BF16) for s in shapes],
        compiler_params=pltpu.CompilerParams(vmem_limit_bytes=VMEM_LIMIT),
        name="prepare",
    )(order, src, integrals)


def pair_kernel(counts, src_own, src_other, ints_own, ints_other, *outs):
    step = pl.program_id(0)
    total = jnp.dot(src_own[...], ints_own[0], preferred_element_type=F32)
    total += jnp.dot(src_other[...], ints_other[0], preferred_element_type=F32)
    total = total.astype(BF16)
    first = 0
    for out, count in zip(outs, counts, strict=True):

        @pl.when((step >= first) & (step < first + count))
        def _(out=out):
            out[0] = total

        first += count


def pair(src_own, src_other, ints_own, ints_other, counts):
    count, rows, width = ints_own.shape
    tall = src_own.shape[0]
    firsts = [sum(counts[:i]) for i in range(len(counts))]
    ints_spec = pl.BlockSpec((1, rows, width), lambda i: (i, 0, 0))

    def out_spec(first, size):
        return pl.BlockSpec((1, tall, width), lambda i: (jnp.clip(i - first, 0, size - 1), 0, 0))

    return pl.pallas_call(
        functools.partial(pair_kernel, counts),
        grid=(count,),
        in_specs=[whole((tall, rows))] * 2 + [ints_spec] * 2,
        out_specs=[out_spec(f, c) for f, c in zip(firsts, counts, strict=True)],
        out_shape=[jax.ShapeDtypeStruct((c, tall, width), BF16) for c in counts],
        compiler_params=pltpu.CompilerParams(vmem_limit_bytes=VMEM_LIMIT),
        name="pair",
    )(src_own, src_other, ints_own, ints_other)


def amplitude_kernel(denom, *refs):
    parts, out = refs[:-1], refs[-1]
    total = parts[0][...].astype(F32)
    for part in parts[1:]:
        total += part[...].astype(F32)
    scaled = (total / denom[...]).astype(BF16).astype(F32)
    out[...] = (2.0 * scaled - scaled.T).astype(BF16)


def amplitude_of(denom, parts):
    return pl.pallas_call(
        amplitude_kernel,
        out_shape=jax.ShapeDtypeStruct(denom.shape, BF16),
        name="amplitude",
    )(denom, *parts)


def density_kernel(n_occ, chunks, src_count, place, *refs):
    sources, amps = refs[: 2 * n_occ], refs[2 * n_occ : -2]
    out, gathered = refs[-2:]
    step = pl.program_id(0)
    width = out.shape[2]
    depth = sources[0].shape[1]

    @pl.when(step == 0)
    def _():
        spot = 0
        for core in range(2):
            for chunk in range(chunks):
                row = (place[1] if core == 0 else 1 - place[1]) * chunks + chunk
                for s in range(src_count):
                    gathered[row, pl.ds(s * width, width), :] = amps[spot][...]
                    spot += 1

    for k in range(n_occ):

        @pl.when(step == k)
        def _(k=k):
            parts = []
            for i in range(2 * chunks):
                total = jnp.dot(sources[2 * k][...], gathered[i, :depth], preferred_element_type=F32)
                total += jnp.dot(sources[2 * k + 1][...], gathered[i, depth:], preferred_element_type=F32)
                parts.append(total.astype(BF16))
            out[...] = jnp.swapaxes(jnp.stack(parts, axis=0), 0, 1)


def density_of(sources, amps, place, n_occ, chunks):
    rows, depth = sources[0].shape
    width = amps[0].shape[0]
    src_count = 2 * depth // width
    return pl.pallas_call(
        functools.partial(density_kernel, n_occ, chunks, src_count),
        grid_spec=pltpu.PrefetchScalarGridSpec(
            num_scalar_prefetch=1,
            grid=(n_occ,),
            in_specs=[whole((rows, depth))] * len(sources) + [whole((width, width))] * len(amps),
            out_specs=pl.BlockSpec((rows, 2 * chunks, width), lambda k, place: (k ^ place[0], 0, 0)),
            scratch_shapes=[pltpu.VMEM((2 * chunks, 2 * depth, width), BF16)],
        ),
        out_shape=jax.ShapeDtypeStruct((n_occ * rows, 2 * chunks, width), BF16),
        compiler_params=pltpu.CompilerParams(vmem_limit_bytes=VMEM_LIMIT),
        name="density",
    )(place, *sources, *amps)


def halving_groups(n_occ, bits):
    kept, groups = [0], [[0]]
    for bit in reversed(bits):
        sent = [k | bit for k in kept]
        groups.insert(0, sent)
        kept = sent + kept
    return groups


def solution(mesh):
    n_occ, n_aux = mesh.shape["occ"], mesh.shape["aux"]
    occ_bits = [1 << b for b in range(n_occ.bit_length() - 1)]
    n_chip = n_aux // 2

    def local(integrals, eps_occ, eps_vir, src_occ, occ_offset, vir_offset):
        rows, occ_count, width = integrals.shape
        src_count = src_occ.shape[0]
        owned = occ_count // n_occ
        chunks = owned // 2
        my_occ, my_aux = lax.axis_index("occ"), lax.axis_index("aux")
        core, chip = my_aux % 2, my_aux // 2
        src = src_occ[jnp.arange(src_count, dtype=jnp.int32) ^ (chip % src_count)]

        orders = [occ_bits if c % 2 == 0 else occ_bits[::-1] for c in range(chunks)]
        groups = [halving_groups(n_occ, order) for order in orders]
        first = [[(c, k) for k in groups[c][0]] for c in range(chunks)]
        rest = [(c, k) for c in range(chunks) for g in groups[c][1:] for k in g]
        calls = first + [rest]
        blocks = jnp.array([k * owned + c for call in calls for c, k in call], jnp.int32)
        number = (blocks // owned) ^ my_occ
        mine = number * owned + core * chunks + blocks % owned
        theirs = number * owned + (1 - core) * chunks + blocks % owned
        counts = [len(call) for call in calls]
        low, high, src_t, *ints = prepare(integrals, jnp.concatenate([theirs, mine]), src, counts * 2)
        theirs, mine = ints[: len(calls)], ints[len(calls) :]

        src_t_other = swap(src_t, "aux", n_aux, 1)
        other = [swap(v, "aux", n_aux, 1) for v in theirs]

        occ_energy = lax.dynamic_slice_in_dim(
            eps_occ, occ_offset[0] + my_occ * owned + core * chunks, chunks
        )
        vir_energy = lax.dynamic_slice_in_dim(eps_vir, vir_offset[0], width)
        src_energy = lax.dynamic_index_in_dim(eps_occ, occ_offset[0] + src[0], 0, keepdims=False)
        denoms = [
            vir_energy[None, :] + vir_energy[:, None] - occ_energy[c] - src_energy for c in range(chunks)
        ]

        sizes = [[len(g) for g in groups[c]] for c in range(chunks)]
        partial = [[None] * len(groups[c]) for c in range(chunks)]
        for c in range(chunks):
            (partial[c][0],) = pair(src_t, src_t_other, mine[c], other[c], [sizes[c][0]])
        outs = list(pair(src_t, src_t_other, mine[-1], other[-1], sum((sizes[c][1:] for c in range(chunks)), [])))
        for c in range(chunks):
            for g in range(1, len(groups[c])):
                partial[c][g] = outs.pop(0)

        received = [[] for _ in range(chunks)]
        for step in range(len(occ_bits)):
            for c in range(chunks):
                value = partial[c][step]
                if step:
                    value = value.astype(F32)
                    size = sizes[c][step]
                    for past, arrays in enumerate(received[c]):
                        start = sum(sizes[c][past + 1 : step])
                        value += arrays[start : start + size].astype(F32)
                    value = value.astype(BF16)
                received[c].append(swap(value, "occ", n_occ, orders[c][step]))

        halves = {(0, 0): low, (0, 1): high}
        bit_orders = [occ_bits, occ_bits[::-1]]
        held = lax.optimization_barrier((low, high, *[r[-1] for r in received]))
        received = [r[:-1] + [held[2 + c]] for c, r in enumerate(received)]
        for h in range(2):
            have = [0]
            for bit in bit_orders[h]:
                for k in have:
                    halves[k | bit, h] = swap(held[h] if k == 0 else halves[k, h], "occ", n_occ, bit)
                have = have + [k | bit for k in have]

        amps = [[[] for _ in range(chunks)] for _ in range(2)]
        for c in range(chunks):
            total = partial[c][-1][0].astype(F32)
            for arrays in received[c]:
                total += arrays[-1].astype(F32)
            total = total.reshape(src_count, width, width)
            parts = [total[0]]
            for s in range(1, src_count):
                parts.append(swap(total[s].astype(BF16), "aux", n_aux, 2 * s))
            for bit in range(src_count.bit_length() - 1, n_chip.bit_length() - 1):
                value = sum(part.astype(F32) for part in parts)
                parts = [value, swap(value.astype(BF16), "aux", n_aux, 2 << bit)]
            amp = amplitude_of(denoms[c], parts)
            pieces = [amp] + [swap(amp, "aux", n_aux, 2 * s) for s in range(1, src_count)]
            amps[0][c] = pieces
            amps[1][c] = [swap(v, "aux", n_aux, 1) for v in pieces]

        sources = [halves[k, h] for k in range(n_occ) for h in range(2)]
        place = jnp.stack([my_occ, core]).astype(jnp.int32)
        flat = [v for by_core in amps for by_chunk in by_core for v in by_chunk]
        return density_of(sources, flat, place, n_occ, chunks)

    in_specs = (P(("aux", "occ"), None, None), P(), P(), P(), P(), P())
    out_specs = P("aux", "occ", None)
    return jax.shard_map(local, mesh=mesh, in_specs=in_specs, out_specs=out_specs, check_vma=False)
```

time: 353 us -> 148 us (0.42)
  waiting for transfers between devices: 226 us -> 62.9 us
  matrix products: 33.7 us -> 0 us
  starting transfers between devices: 5.52 us -> 38.7 us
  local copies, waits for them, and re-layouts: 42.6 us -> 10.7 us
  between operations: 27.5 us -> 1.46 us
  Pallas kernels: 0 us -> 25.6 us
  other arithmetic: 16 us -> 8.32 us
    psum x2 -> x0, waiting for transfers between devices: 188 us -> none  [the longest x1 96.9 us: spread(): return lax.psum(kept, axis)]
    ppermute x0 -> x34, waiting for transfers between devices: none -> 62.9 us  [swap(): return lax.ppermute(value, axis, [(d, d ^ mask) for d in range(size)])]
    ppermute x0 -> x34, starting transfers between devices: none -> 38.7 us  [swap(): return lax.ppermute(value, axis, [(d, d ^ mask) for d in range(size)])]
    all_to_all x1 -> x0, waiting for transfers between devices: 37.9 us -> none  [local(): lax.all_to_all(integrals, 'occ', split_axis=1, concat_axis=0, tiled=True)]
    dot_general x8 -> x0, matrix products: 33.7 us -> none  [the longest x4 21.4 us: local(): lax.dot_general(source, amplitude.reshape(occ_count * virt_count, virt_co...]
    pallas_call x0 -> x7, Pallas kernels: none -> 25.6 us  [the longest x1 8.79 us: density_of(): pl.pallas_call(functools.partial(density_kernel, n_occ, chunks, src_count...]
    reshape x5 -> x0, local copies, waits for them, and re-layouts: 12.7 us -> none  [the longest x1 7.43 us: local(): density_sum.astype(jnp.bfloat16).reshape(aux_rows, occ_count, virt_count)]
    convert_element_type x5 -> x2, other arithmetic: 11.7 us -> 2.04 us  [local(): value = value.astype(BF16)]
  transfers between devices with their start and end apart: 3 -> 34, of which waited for: 3 -> 17; matrix products, arithmetic and copies ran while one was open for 3% -> 7% of each run, Pallas kernels for 0% -> 8%
where the time goes in v1:
time: 148 us
  waiting for transfers between devices  62.9 us (42%)
  starting transfers between devices  38.7 us (26%)
  Pallas kernels  25.6 us (17%)
  local copies, waits for them, and re-layouts  10.7 us (7%)
  other arithmetic  8.32 us (6%)
    ppermute x34, waiting for transfers between devices, swap(): return lax.ppermute(value, axis, [(d, d ^ mask) for d in range(size)])  62.9 us
    ppermute x34, starting transfers between devices, swap(): return lax.ppermute(value, axis, [(d, d ^ mask) for d in range(size)])  38.7 us
    pallas_call x1, Pallas kernels, density_of(): pl.pallas_call(functools.partial(density_kernel, n_occ, chunks, src_count...  8.79 us
    pallas_call x3, Pallas kernels, pair(): pl.pallas_call(functools.partial(pair_kernel, counts), grid=(count,), in_...  7.29 us
    pallas_call x1, Pallas kernels, prepare(): pl.pallas_call(functools.partial(prepare_kernel, counts, src_count), grid...  5.55 us
    unnamed x26, local copies, waits for them, and re-layouts  4.35 us
    pallas_call x2, Pallas kernels, amplitude_of(): pl.pallas_call(amplitude_kernel, out_shape=jax.ShapeDtypeStruct(denom.sha...  3.99 us
  transfers between devices with their start and end apart: 34, of which 17 were waited for; matrix products, arithmetic and copies ran while one was open for 7% of the time, Pallas kernels for 8%

profile of v1, /device:TPU:0, one launch (start us, length us, event | category | flops | bytes accessed | tf_op | source)
XLA Modules:
  0.0 147.8 jit_solution(12617247056129371693)
XLA Ops:
  1.4 5.5 %prepare.1 = (bf16[512,512]{1,0:T(8,128)(2,1)S(1)}, bf16[512,512]{1,0:T(8,128)(2,1)S(1)}, bf16[1024,512]{1,0:T(8,128)(2,1)S(1)}, bf16[2,512,256]{2,1,0:T(8,128)(...) custom-call(s32[16]{0:T(128)S(1)} %pad_add_fusion.1.index_ref, ...), custom_call_target="tpu_custom_call" | custom-call | tf_op jit(solution)/shard_map/prepare/pallas_call | solution.py:50
  8.0 2.5 %collective-permute-done.2.ints_other = bf16[2,512,256]{2,1,0:T(8,128)(2,1)S(1)} collective-permute-done((bf16[2,512,256]{2,1,0:T(8,128)(2,1)S(1)}, bf16[2,512,256]{2,1,0:T(8,128)(2,1)S(1)}, u32[]{:S(2)}, u32[]{:S(2)}) %collective-permute-start.2) | collective-permute-done | bytes 524320 | tf_op jit(solution)/shard_map/ppermute | solution.py:15
  12.0 2.9 %collective-permute-start.3 = (bf16[2,1024,256]{2,1,0:T(8,128)(2,1)S(1)}, bf16[2,1024,256]{2,1,0:T(8,128)(2,1)S(1)}, u32[]{:S(2)}, u32[]{:S(2)}) collective-permute-start(bf16[2,1024,256]{2,1,0:T(8,128)(2,1)S(1)} %pair.4), channel_id=1, source_target_pairs={{0,8},{8,0},{16,24},{24,16},{1,9},{9,1},{17,25},{25,17},{2,10},{10... | collective-permute-start | bytes 3145736 | tf_op jit(solution)/shard_map/ppermute | solution.py:15
  19.0 4.3 %pair.3 = (bf16[1,1024,256]{2,1,0:T(8,128)(2,1)S(1)}, bf16[1,1024,256]{2,1,0:T(8,128)(2,1)S(1)}, bf16[1,1024,256]{2,1,0:T(8,128)(2,1)S(1)}, bf16[1,1024,256]{2,1,0:T(8,128)(2,1)S(1)}) custom-call(bf16[1024,512]{1,0:T(8,128)(2,1)S(1)} %get-tuple-element.24.src_own, bf16[1024,512]{1,0:T(8,128)(2,1)S(1)} %collective-permute-done.src_other, ...), custom_call_target="tpu_custom_call" | custom-call | tf_op jit(solution)/shard_map/pair/pallas_call | solution.py:89
  23.3 15.1 %collective-permute-done.3 = bf16[2,1024,256]{2,1,0:T(8,128)(2,1)S(1)} collective-permute-done((bf16[2,1024,256]{2,1,0:T(8,128)(2,1)S(1)}, bf16[2,1024,256]{2,1,0:T(8,128)(2,1)S(1)}, u32[]{:S(2)}, u32[]{:S(2)}) %collective-permute-start.3) | collective-permute-done | bytes 1048608 | tf_op jit(solution)/shard_map/ppermute | solution.py:15
  48.4 2.7 %fusion.1 = (f32[256,256]{1,0:T(8,128)}, f32[256,256]{1,0:T(8,128)}) fusion(f32[]{:T(128)} %bitcast.12, f32[]{:T(128)} %bitcast.7, f32[256]{0:T(256)S(1)} %dynamic_slice.10, f32[]{:T(128)} %bitcast.5), kind=kLoop, calls=%fused_computation.8 | loop fusion | flops 327680 | bytes 525324 | tf_op jit(solution)/shard_map/sub | solution.py:210
  51.1 2.0 %collective-permute-done.4 = bf16[1,1024,256]{2,1,0:T(8,128)(2,1)} collective-permute-done((bf16[1,1024,256]{2,1,0:T(8,128)(2,1)}, bf16[1,1024,256]{2,1,0:T(8,128)(2,1)}, u32[]{:S(2)}, u32[]{:S(2)}) %collective-permute-start.4) | collective-permute-done | bytes 524320 | tf_op jit(solution)/shard_map/ppermute | solution.py:15
  53.1 2.6 %collective-permute-done.7 = bf16[1,1024,256]{2,1,0:T(8,128)(2,1)} collective-permute-done((bf16[1,1024,256]{2,1,0:T(8,128)(2,1)}, bf16[1,1024,256]{2,1,0:T(8,128)(2,1)}, u32[]{:S(2)}, u32[]{:S(2)}) %collective-permute-start.7) | collective-permute-done | bytes 524320 | tf_op jit(solution)/shard_map/ppermute | solution.py:15
  55.7 2.8 %fusion.3 = (bf16[1,1024,256]{2,1,0:T(8,128)(2,1)S(1)}, f32[1,1024,256]{2,1,0:T(8,128)S(1)}, bf16[1,1024,256]{2,1,0:T(8,128)(2,1)S(1)}, f32[1,1024,256]{2,1,0:T(8,128)}) fusion(bf16[1,1024,256]{2,1,0:T(8,128)(2,1)} %collective-permute-done.7, bf16[2,1024,256]{2,1,0:T(8,128)(2,1)} %copy-done.4, bf16[1,1024,256]{2,1,0:T(8,128)(2,1)S(1)} %get-tuple-element.37, ...), kind=kLoop, calls=%fused_computation.25 | loop fusion | flops 3145728 | bytes 6291456 | tf_op jit(solution)/shard_map/convert.2
  58.5 3.7 %collective-permute-start.22 = (bf16[256,256]{1,0:T(8,128)(2,1)S(1)}, bf16[256,256]{1,0:T(8,128)(2,1)S(1)}, u32[]{:S(2)}, u32[]{:S(2)}) collective-permute-start(bf16[256,256]{1,0:T(8,128)(2,1)S(1)} %get-tuple-element.43), channel_id=1, source_target_pairs={{0,6},{1,7},{2,4},{3,5},{4,2},{5,3},{6,0},{7,1},{8,14},{9,15},{10,... | collective-permute-start | bytes 393224 | tf_op jit(solution)/shard_map/ppermute | solution.py:15
  63.0 3.7 %collective-permute-start.16 = (bf16[256,256]{1,0:T(8,128)(2,1)S(1)}, bf16[256,256]{1,0:T(8,128)(2,1)S(1)}, u32[]{:S(2)}, u32[]{:S(2)}) collective-permute-start(bf16[256,256]{1,0:T(8,128)(2,1)S(1)} %get-tuple-element.46), channel_id=1, source_target_pairs={{0,6},{1,7},{2,4},{3,5},{4,2},{5,3},{6,0},{7,1},{8,14},{9,15},{10,... | collective-permute-start | bytes 393224 | tf_op jit(solution)/shard_map/ppermute | solution.py:15
  67.4 6.4 %collective-permute-start.14 = (bf16[256,256]{1,0:T(8,128)(2,1)S(1)}, bf16[256,256]{1,0:T(8,128)(2,1)S(1)}, u32[]{:S(2)}, u32[]{:S(2)}) collective-permute-start(bf16[256,256]{1,0:T(8,128)(2,1)S(1)} %get-tuple-element.48), channel_id=1, source_target_pairs={{0,2},{1,3},{2,0},{3,1},{4,6},{5,7},{6,4},{7,5},{8,10},{9,11},{10,... | collective-permute-start | bytes 393224 | tf_op jit(solution)/shard_map/ppermute | solution.py:15
  73.8 4.3 %collective-permute-done.21.refs_2_ = bf16[256,256]{1,0:T(8,128)(2,1)S(1)} collective-permute-done((bf16[256,256]{1,0:T(8,128)(2,1)S(1)}, bf16[256,256]{1,0:T(8,128)(2,1)S(1)}, u32[]{:S(2)}, u32[]{:S(2)}) %collective-permute-start.21) | collective-permute-done | bytes 131104 | tf_op jit(solution)/shard_map/ppermute | solution.py:15
  78.8 2.0 %amplitude.3.refs_12_ = bf16[256,256]{1,0:T(8,128)(2,1)} custom-call(f32[256,256]{1,0:T(8,128)} %get-tuple-element.49.denom, f32[256,256]{1,0:T(8,128)} %slice_bitcast_fusion.refs_0_, bf16[256,256]{1,0:T(8,128)(2,1)} %copy-done.12, bf16[256,256]{1,0:T(8,128)(2,1)} %copy-done.11, bf16[256,256]{1,0:T(8,128)(2,1)} %copy-done.10), custom_call_target="tpu_custom_call" | custom-call | tf_op jit(solution)/shard_map/amplitude/pallas_call | solution.py:110
  82.9 3.5 %collective-permute-start.25 = (bf16[256,256]{1,0:T(8,128)(2,1)}, bf16[256,256]{1,0:T(8,128)(2,1)S(1)}, u32[]{:S(2)}, u32[]{:S(2)}) collective-permute-start(bf16[256,256]{1,0:T(8,128)(2,1)} %amplitude.3.refs_12_), channel_id=1, source_target_pairs={{0,6},{1,7},{2,4},{3,5},{4,2},{5,3},{6,0},{7,1},{8,14},{9,15},{10,... | collective-permute-start | bytes 393224 | tf_op jit(solution)/shard_map/ppermute | solution.py:15
  89.0 2.0 %amplitude.2.refs_8_ = bf16[256,256]{1,0:T(8,128)(2,1)} custom-call(f32[256,256]{1,0:T(8,128)} %get-tuple-element.50.denom, f32[256,256]{1,0:T(8,128)} %slice_bitcast_fusion.1.refs_0_, bf16[256,256]{1,0:T(8,128)(2,1)} %copy-done.9, bf16[256,256]{1,0:T(8,128)(2,1)} %copy-done.8, bf16[256,256]{1,0:T(8,128)(2,1)} %copy-done.7), custom_call_target="tpu_custom_call" | custom-call | tf_op jit(solution)/shard_map/amplitude/pallas_call | solution.py:110
  91.3 5.7 %collective-permute-done.24.refs_14_ = bf16[256,256]{1,0:T(8,128)(2,1)S(1)} collective-permute-done((bf16[256,256]{1,0:T(8,128)(2,1)}, bf16[256,256]{1,0:T(8,128)(2,1)S(1)}, u32[]{:S(2)}, u32[]{:S(2)}) %collective-permute-start.24) | collective-permute-done | bytes 131104 | tf_op jit(solution)/shard_map/ppermute | solution.py:15
  97.0 1.9 %collective-permute-start.19 = (bf16[256,256]{1,0:T(8,128)(2,1)}, bf16[256,256]{1,0:T(8,128)(2,1)S(1)}, u32[]{:S(2)}, u32[]{:S(2)}) collective-permute-start(bf16[256,256]{1,0:T(8,128)(2,1)} %amplitude.2.refs_8_), channel_id=1, source_target_pairs={{0,6},{1,7},{2,4},{3,5},{4,2},{5,3},{6,0},{7,1},{8,14},{9,15},{10,... | collective-permute-start | bytes 393224 | tf_op jit(solution)/shard_map/ppermute | solution.py:15
  98.9 2.5 %collective-permute-start.17 = (bf16[256,256]{1,0:T(8,128)(2,1)}, bf16[256,256]{1,0:T(8,128)(2,1)S(1)}, u32[]{:S(2)}, u32[]{:S(2)}) collective-permute-start(bf16[256,256]{1,0:T(8,128)(2,1)} %amplitude.2.refs_8_), channel_id=1, source_target_pairs={{0,2},{1,3},{2,0},{3,1},{4,6},{5,7},{6,4},{7,5},{8,10},{9,11},{10,... | collective-permute-start | bytes 393224 | tf_op jit(solution)/shard_map/ppermute | solution.py:15
  101.4 4.0 %collective-permute-done.19.refs_11_ = bf16[256,256]{1,0:T(8,128)(2,1)S(1)} collective-permute-done((bf16[256,256]{1,0:T(8,128)(2,1)}, bf16[256,256]{1,0:T(8,128)(2,1)S(1)}, u32[]{:S(2)}, u32[]{:S(2)}) %collective-permute-start.19) | collective-permute-done | bytes 131104 | tf_op jit(solution)/shard_map/ppermute | solution.py:15
  105.5 4.3 %collective-permute-done.18.refs_10_ = bf16[256,256]{1,0:T(8,128)(2,1)S(1)} collective-permute-done((bf16[256,256]{1,0:T(8,128)(2,1)}, bf16[256,256]{1,0:T(8,128)(2,1)S(1)}, u32[]{:S(2)}, u32[]{:S(2)}) %collective-permute-start.18) | collective-permute-done | bytes 131104 | tf_op jit(solution)/shard_map/ppermute | solution.py:15
  118.4 6.7 %collective-permute-done.10.refs_4_ = bf16[512,512]{1,0:T(8,128)(2,1)S(1)} collective-permute-done((bf16[512,512]{1,0:T(8,128)(2,1)S(1)}, bf16[512,512]{1,0:T(8,128)(2,1)S(1)}, u32[]{:S(2)}, u32[]{:S(2)}) %collective-permute-start.10) | collective-permute-done | bytes 524320 | tf_op jit(solution)/shard_map/ppermute | solution.py:15
  126.3 9.1 %collective-permute-done.12.refs_6_ = bf16[512,512]{1,0:T(8,128)(2,1)S(1)} collective-permute-done((bf16[512,512]{1,0:T(8,128)(2,1)S(1)}, bf16[512,512]{1,0:T(8,128)(2,1)S(1)}, u32[]{:S(2)}, u32[]{:S(2)}) %collective-permute-start.12) | collective-permute-done | bytes 524320 | tf_op jit(solution)/shard_map/ppermute | solution.py:15
  139.0 8.8 %density.1 = bf16[2048,4,256]{2,1,0:T(4,128)(2,1)} custom-call(s32[2]{0:T(128)S(1)} %pad_add_fusion.place, bf16[512,512]{1,0:T(8,128)(2,1)S(1)} %get-tuple-element.33.refs_0_, bf16[512,512]{1,0:T(8,128)(2,1)S(1)} %get-tuple-element.34.refs_1_, bf16[512,512]{1,0:T(8,128)(2,1)S(1)} %collective-permute-done.8.refs_2_, ...), custom_call_target="tpu_custom_call" | custom-call | tf_op jit(solution)/shard_map/density/pallas_call | solution.py:150
  (95 shorter events, 37.3 us)
Async XLA Ops:
  7.9 10.1 %collective-permute-start.1 = (bf16[4,512,256]{2,1,0:T(8,128)(2,1)S(1)}, bf16[4,512,256]{2,1,0:T(8,128)(2,1)S(1)}, u32[]{:S(2)}, u32[]{:S(2)}) collective-permute-start(bf16[4,512,256]{2,1,0:T(8,128)(2,1)S(1)} %get-tuple-element.26), channel_id=1, source_target_pairs={{0,1},{1,0},{2,3},{3,2},{4,5},{5,4},{6,7},{7,6},{8,9},{9,8},{10,11... | collective-permute-start | bytes 3145736 | tf_op jit(solution)/shard_map/ppermute | solution.py:15
  12.0 26.4 %collective-permute-start.3 = (bf16[2,1024,256]{2,1,0:T(8,128)(2,1)S(1)}, bf16[2,1024,256]{2,1,0:T(8,128)(2,1)S(1)}, u32[]{:S(2)}, u32[]{:S(2)}) collective-permute-start(bf16[2,1024,256]{2,1,0:T(8,128)(2,1)S(1)} %pair.4), channel_id=1, source_target_pairs={{0,8},{8,0},{16,24},{24,16},{1,9},{9,1},{17,25},{25,17},{2,10},{10... | collective-permute-start | bytes 3145736 | tf_op jit(solution)/shard_map/ppermute | solution.py:15
  16.4 25.0 %collective-permute-start.6 = (bf16[2,1024,256]{2,1,0:T(8,128)(2,1)S(1)}, bf16[2,1024,256]{2,1,0:T(8,128)(2,1)S(1)}, u32[]{:S(2)}, u32[]{:S(2)}) collective-permute-start(bf16[2,1024,256]{2,1,0:T(8,128)(2,1)S(1)} %pair.5), channel_id=1, source_target_pairs={{0,16},{8,24},{16,0},{24,8},{1,17},{9,25},{17,1},{25,9},{2,18},{10... | collective-permute-start | bytes 3145736 | tf_op jit(solution)/shard_map/ppermute | solution.py:15
  39.3 13.8 %collective-permute-start.4 = (bf16[1,1024,256]{2,1,0:T(8,128)(2,1)}, bf16[1,1024,256]{2,1,0:T(8,128)(2,1)}, u32[]{:S(2)}, u32[]{:S(2)}) collective-permute-start(bf16[1,1024,256]{2,1,0:T(8,128)(2,1)} %add_convert_fusion.1), channel_id=1, source_target_pairs={{0,16},{8,24},{16,0},{24,8},{1,17},{9,25},{17,1},{25,9},{2,18},{10... | collective-permute-start | bytes 1572872 | tf_op jit(solution)/shard_map/ppermute | solution.py:15
  42.6 13.1 %collective-permute-start.7 = (bf16[1,1024,256]{2,1,0:T(8,128)(2,1)}, bf16[1,1024,256]{2,1,0:T(8,128)(2,1)}, u32[]{:S(2)}, u32[]{:S(2)}) collective-permute-start(bf16[1,1024,256]{2,1,0:T(8,128)(2,1)} %add_convert_fusion), channel_id=1, source_target_pairs={{0,8},{8,0},{16,24},{24,16},{1,9},{9,1},{17,25},{25,17},{2,10},{10... | collective-permute-start | bytes 1572872 | tf_op jit(solution)/shard_map/ppermute | solution.py:15
  58.5 8.9 %collective-permute-start.22 = (bf16[256,256]{1,0:T(8,128)(2,1)S(1)}, bf16[256,256]{1,0:T(8,128)(2,1)S(1)}, u32[]{:S(2)}, u32[]{:S(2)}) collective-permute-start(bf16[256,256]{1,0:T(8,128)(2,1)S(1)} %get-tuple-element.43), channel_id=1, source_target_pairs={{0,6},{1,7},{2,4},{3,5},{4,2},{5,3},{6,0},{7,1},{8,14},{9,15},{10,... | collective-permute-start | bytes 393224 | tf_op jit(solution)/shard_map/ppermute | solution.py:15
  62.2 15.9 %collective-permute-start.21 = (bf16[256,256]{1,0:T(8,128)(2,1)S(1)}, bf16[256,256]{1,0:T(8,128)(2,1)S(1)}, u32[]{:S(2)}, u32[]{:S(2)}) collective-permute-start(bf16[256,256]{1,0:T(8,128)(2,1)S(1)} %get-tuple-element.44), channel_id=1, source_target_pairs={{0,4},{1,5},{2,6},{3,7},{4,0},{5,1},{6,2},{7,3},{8,12},{9,13},{10,... | collective-permute-start | bytes 393224 | tf_op jit(solution)/shard_map/ppermute | solution.py:15
  62.2 15.9 %collective-permute-start.20 = (bf16[256,256]{1,0:T(8,128)(2,1)S(1)}, bf16[256,256]{1,0:T(8,128)(2,1)S(1)}, u32[]{:S(2)}, u32[]{:S(2)}) collective-permute-start(bf16[256,256]{1,0:T(8,128)(2,1)S(1)} %get-tuple-element.45), channel_id=1, source_target_pairs={{0,2},{1,3},{2,0},{3,1},{4,6},{5,7},{6,4},{7,5},{8,10},{9,11},{10,... | collective-permute-start | bytes 393224 | tf_op jit(solution)/shard_map/ppermute | solution.py:15
  63.0 19.0 %collective-permute-start.16 = (bf16[256,256]{1,0:T(8,128)(2,1)S(1)}, bf16[256,256]{1,0:T(8,128)(2,1)S(1)}, u32[]{:S(2)}, u32[]{:S(2)}) collective-permute-start(bf16[256,256]{1,0:T(8,128)(2,1)S(1)} %get-tuple-element.46), channel_id=1, source_target_pairs={{0,6},{1,7},{2,4},{3,5},{4,2},{5,3},{6,0},{7,1},{8,14},{9,15},{10,... | collective-permute-start | bytes 393224 | tf_op jit(solution)/shard_map/ppermute | solution.py:15
  67.4 15.5 %collective-permute-start.15 = (bf16[256,256]{1,0:T(8,128)(2,1)S(1)}, bf16[256,256]{1,0:T(8,128)(2,1)S(1)}, u32[]{:S(2)}, u32[]{:S(2)}) collective-permute-start(bf16[256,256]{1,0:T(8,128)(2,1)S(1)} %get-tuple-element.47), channel_id=1, source_target_pairs={{0,4},{1,5},{2,6},{3,7},{4,0},{5,1},{6,2},{7,3},{8,12},{9,13},{10,... | collective-permute-start | bytes 393224 | tf_op jit(solution)/shard_map/ppermute | solution.py:15
  67.4 19.0 %collective-permute-start.14 = (bf16[256,256]{1,0:T(8,128)(2,1)S(1)}, bf16[256,256]{1,0:T(8,128)(2,1)S(1)}, u32[]{:S(2)}, u32[]{:S(2)}) collective-permute-start(bf16[256,256]{1,0:T(8,128)(2,1)S(1)} %get-tuple-element.48), channel_id=1, source_target_pairs={{0,2},{1,3},{2,0},{3,1},{4,6},{5,7},{6,4},{7,5},{8,10},{9,11},{10,... | collective-permute-start | bytes 393224 | tf_op jit(solution)/shard_map/ppermute | solution.py:15
  80.8 31.8 %collective-permute-start.8 = (bf16[512,512]{1,0:T(8,128)(2,1)S(1)}, bf16[512,512]{1,0:T(8,128)(2,1)S(1)}, u32[]{:S(2)}, u32[]{:S(2)}) collective-permute-start(bf16[512,512]{1,0:T(8,128)(2,1)S(1)} %get-tuple-element.33.refs_0_), channel_id=1, source_target_pairs={{0,8},{8,0},{16,24},{24,16},{1,9},{9,1},{17,25},{25,17},{2,10},{10... | collective-permute-start | bytes 1572872 | tf_op jit(solution)/shard_map/ppermute | solution.py:15
  82.0 31.8 %collective-permute-start.11 = (bf16[512,512]{1,0:T(8,128)(2,1)S(1)}, bf16[512,512]{1,0:T(8,128)(2,1)S(1)}, u32[]{:S(2)}, u32[]{:S(2)}) collective-permute-start(bf16[512,512]{1,0:T(8,128)(2,1)S(1)} %get-tuple-element.34.refs_1_), channel_id=1, source_target_pairs={{0,16},{8,24},{16,0},{24,8},{1,17},{9,25},{17,1},{25,9},{2,18},{10... | collective-permute-start | bytes 1572872 | tf_op jit(solution)/shard_map/ppermute | solution.py:15
  82.9 8.4 %collective-permute-start.25 = (bf16[256,256]{1,0:T(8,128)(2,1)}, bf16[256,256]{1,0:T(8,128)(2,1)S(1)}, u32[]{:S(2)}, u32[]{:S(2)}) collective-permute-start(bf16[256,256]{1,0:T(8,128)(2,1)} %amplitude.3.refs_12_), channel_id=1, source_target_pairs={{0,6},{1,7},{2,4},{3,5},{4,2},{5,3},{6,0},{7,1},{8,14},{9,15},{10,... | collective-permute-start | bytes 393224 | tf_op jit(solution)/shard_map/ppermute | solution.py:15
  86.4 10.6 %collective-permute-start.24 = (bf16[256,256]{1,0:T(8,128)(2,1)}, bf16[256,256]{1,0:T(8,128)(2,1)S(1)}, u32[]{:S(2)}, u32[]{:S(2)}) collective-permute-start(bf16[256,256]{1,0:T(8,128)(2,1)} %amplitude.3.refs_12_), channel_id=1, source_target_pairs={{0,4},{1,5},{2,6},{3,7},{4,0},{5,1},{6,2},{7,3},{8,12},{9,13},{10,... | collective-permute-start | bytes 393224 | tf_op jit(solution)/shard_map/ppermute | solution.py:15
  86.4 12.5 %collective-permute-start.23 = (bf16[256,256]{1,0:T(8,128)(2,1)}, bf16[256,256]{1,0:T(8,128)(2,1)S(1)}, u32[]{:S(2)}, u32[]{:S(2)}) collective-permute-start(bf16[256,256]{1,0:T(8,128)(2,1)} %amplitude.3.refs_12_), channel_id=1, source_target_pairs={{0,2},{1,3},{2,0},{3,1},{4,6},{5,7},{6,4},{7,5},{8,10},{9,11},{10,... | collective-permute-start | bytes 393224 | tf_op jit(solution)/shard_map/ppermute | solution.py:15
  91.3 7.6 %collective-permute-start.26 = (bf16[256,256]{1,0:T(8,128)(2,1)}, bf16[256,256]{1,0:T(8,128)(2,1)S(1)}, u32[]{:S(2)}, u32[]{:S(2)}) collective-permute-start(bf16[256,256]{1,0:T(8,128)(2,1)} %amplitude.2.refs_8_), channel_id=1, source_target_pairs={{0,1},{1,0},{2,3},{3,2},{4,5},{5,4},{6,7},{7,6},{8,9},{9,8},{10,11... | collective-permute-start | bytes 393224 | tf_op jit(solution)/shard_map/ppermute | solution.py:15
  97.0 8.4 %collective-permute-start.19 = (bf16[256,256]{1,0:T(8,128)(2,1)}, bf16[256,256]{1,0:T(8,128)(2,1)S(1)}, u32[]{:S(2)}, u32[]{:S(2)}) collective-permute-start(bf16[256,256]{1,0:T(8,128)(2,1)} %amplitude.2.refs_8_), channel_id=1, source_target_pairs={{0,6},{1,7},{2,4},{3,5},{4,2},{5,3},{6,0},{7,1},{8,14},{9,15},{10,... | collective-permute-start | bytes 393224 | tf_op jit(solution)/shard_map/ppermute | solution.py:15
  98.9 10.8 %collective-permute-start.18 = (bf16[256,256]{1,0:T(8,128)(2,1)}, bf16[256,256]{1,0:T(8,128)(2,1)S(1)}, u32[]{:S(2)}, u32[]{:S(2)}) collective-permute-start(bf16[256,256]{1,0:T(8,128)(2,1)} %amplitude.2.refs_8_), channel_id=1, source_target_pairs={{0,4},{1,5},{2,6},{3,7},{4,0},{5,1},{6,2},{7,3},{8,12},{9,13},{10,... | collective-permute-start | bytes 393224 | tf_op jit(solution)/shard_map/ppermute | solution.py:15
  98.9 10.8 %collective-permute-start.17 = (bf16[256,256]{1,0:T(8,128)(2,1)}, bf16[256,256]{1,0:T(8,128)(2,1)S(1)}, u32[]{:S(2)}, u32[]{:S(2)}) collective-permute-start(bf16[256,256]{1,0:T(8,128)(2,1)} %amplitude.2.refs_8_), channel_id=1, source_target_pairs={{0,2},{1,3},{2,0},{3,1},{4,6},{5,7},{6,4},{7,5},{8,10},{9,11},{10,... | collective-permute-start | bytes 393224 | tf_op jit(solution)/shard_map/ppermute | solution.py:15
  110.3 14.8 %collective-permute-start.10 = (bf16[512,512]{1,0:T(8,128)(2,1)S(1)}, bf16[512,512]{1,0:T(8,128)(2,1)S(1)}, u32[]{:S(2)}, u32[]{:S(2)}) collective-permute-start(bf16[512,512]{1,0:T(8,128)(2,1)S(1)} %get-tuple-element.33.refs_0_), channel_id=1, source_target_pairs={{0,16},{8,24},{16,0},{24,8},{1,17},{9,25},{17,1},{25,9},{2,18},{10... | collective-permute-start | bytes 1572872 | tf_op jit(solution)/shard_map/ppermute | solution.py:15
  111.5 14.8 %collective-permute-start.9 = (bf16[512,512]{1,0:T(8,128)(2,1)S(1)}, bf16[512,512]{1,0:T(8,128)(2,1)S(1)}, u32[]{:S(2)}, u32[]{:S(2)}) collective-permute-start(bf16[512,512]{1,0:T(8,128)(2,1)S(1)} %get-tuple-element.34.refs_1_), channel_id=1, source_target_pairs={{0,8},{8,0},{16,24},{24,16},{1,9},{9,1},{17,25},{25,17},{2,10},{10... | collective-permute-start | bytes 1572872 | tf_op jit(solution)/shard_map/ppermute | solution.py:15
  112.6 22.8 %collective-permute-start.12 = (bf16[512,512]{1,0:T(8,128)(2,1)S(1)}, bf16[512,512]{1,0:T(8,128)(2,1)S(1)}, u32[]{:S(2)}, u32[]{:S(2)}) collective-permute-start(bf16[512,512]{1,0:T(8,128)(2,1)S(1)} %collective-permute-done.8.refs_2_), channel_id=1, source_target_pairs={{0,16},{8,24},{16,0},{24,8},{1,17},{9,25},{17,1},{25,9},{2,18},{10... | collective-permute-start | bytes 1572872 | tf_op jit(solution)/shard_map/ppermute | solution.py:15
  113.8 22.5 %collective-permute-start.13 = (bf16[512,512]{1,0:T(8,128)(2,1)S(1)}, bf16[512,512]{1,0:T(8,128)(2,1)S(1)}, u32[]{:S(2)}, u32[]{:S(2)}) collective-permute-start(bf16[512,512]{1,0:T(8,128)(2,1)S(1)} %collective-permute-done.11.refs_5_), channel_id=1, source_target_pairs={{0,8},{8,0},{16,24},{24,16},{1,9},{9,1},{17,25},{25,17},{2,10},{10... | collective-permute-start | bytes 1572872 | tf_op jit(solution)/shard_map/ppermute | solution.py:15
  (23 other events, 76.5 us)

commit v2 on v0

v2 whole, which is shorter than its diff:
```python
import functools

import jax
import jax.numpy as jnp
from jax import lax
from jax.experimental import pallas as pl
from jax.experimental.pallas import tpu as pltpu
from jax.sharding import PartitionSpec as P

F32, BF16 = jnp.float32, jnp.bfloat16
MIB = 1 << 20


def swap(value, axis, size, mask):
    return lax.ppermute(value, axis, [(d, d ^ mask) for d in range(size)])


def whole(shape):
    return pl.BlockSpec(shape, lambda *_: (0,) * len(shape))


def chip_mask(src_count):
    chip = lax.axis_index("aux") // 2
    return (chip % 2) * (src_count // 2) + chip // 2 % 2


def prepare_kernel(n_occ, chunks, src_count, src_ref, x_ref, *refs):
    halves, src_t, theirs, mine, turned = refs[:2], refs[2], refs[3 : 3 + chunks], refs[3 + chunks : -1], refs[-1]
    turned[...] = jnp.swapaxes(x_ref[...], 0, 1)
    width = x_ref.shape[2]
    per_half = src_count // 2
    mask = chip_mask(src_count)
    for s in range(src_count):
        block = turned[src_ref[s ^ mask]]
        place = pl.ds((s % per_half) * width, width)
        halves[s // per_half][:, place] = block
        src_t[pl.ds(s * width, width), :] = block.T
    my_occ, core = lax.axis_index("occ"), lax.axis_index("aux") % 2
    for outs, side in ((theirs, 1 - core), (mine, core)):
        for chunk, out in enumerate(outs):
            for k in range(n_occ):
                out[k] = turned[((k ^ my_occ) * 2 + side) * chunks + chunk]


def prepare(integrals, src, n_occ, chunks):
    rows, occ_count, width = integrals.shape
    src_count = src.shape[0]
    step = min(rows, 128)
    half = src_count * width // 2
    blocks = [(n_occ, rows, width)] * (2 * chunks)
    shapes = [(rows, half)] * 2 + [(src_count * width, rows)] + blocks
    specs = (
        [pl.BlockSpec((step, half), lambda r, *_: (r, 0))] * 2
        + [pl.BlockSpec((src_count * width, step), lambda r, *_: (0, r))]
        + [pl.BlockSpec((n_occ, step, width), lambda r, *_: (0, r, 0)) for _ in blocks]
    )
    return pl.pallas_call(
        functools.partial(prepare_kernel, n_occ, chunks, src_count),
        grid_spec=pltpu.PrefetchScalarGridSpec(
            num_scalar_prefetch=1,
            grid=(rows // step,),
            in_specs=[pl.BlockSpec((step, occ_count, width), lambda r, *_: (r, 0, 0))],
            out_specs=specs,
            scratch_shapes=[pltpu.VMEM((occ_count, step, width), BF16)],
        ),
        out_shape=[jax.ShapeDtypeStruct(s, BF16) for s in shapes],
        compiler_params=pltpu.CompilerParams(vmem_limit_bytes=16 * MIB),
        name="prepare",
    )(src, integrals)


def pair_kernel(src_own, src_other, ints_own, ints_other, *refs):
    out = refs[-1]
    total = jnp.dot(src_own[...], ints_own[0], preferred_element_type=F32)
    total += jnp.dot(src_other[...], ints_other[0], preferred_element_type=F32)
    out[0] = total.astype(BF16)


def pair(src_own, src_other, ints_own, ints_other, pieces, parts, after=()):
    _, rows, width = ints_own.shape
    tall = src_own.shape[0] // parts
    count = len(pieces)
    split = count // 2

    def sequence(column):
        values = [piece[column] for piece in pieces]
        steps = [values[1] - values[0], values[-1] - values[-2]] if split > 1 else [0, 0]
        assert values == [values[i // split * split] + steps[i // split] * (i % split) for i in range(count)]

        def at(i):
            return jnp.where(i < split, values[0] + steps[0] * i, values[split] + steps[1] * (i - split))

        return at

    part, block = sequence(0), sequence(1)
    return pl.pallas_call(
        pair_kernel,
        grid=(count,),
        in_specs=[pl.BlockSpec((tall, rows), lambda i: (part(i), 0))] * 2
        + [pl.BlockSpec((1, rows, width), lambda i: (block(i), 0, 0))] * 2
        + [pl.BlockSpec(memory_space=pl.ANY)] * len(after),
        out_specs=pl.BlockSpec((1, tall, width), lambda i: (i, 0, 0)),
        out_shape=jax.ShapeDtypeStruct((count, tall, width), BF16),
        compiler_params=pltpu.CompilerParams(vmem_limit_bytes=12 * MIB),
        name="pair",
    )(src_own, src_other, ints_own, ints_other, *after)


def add_terms(refs, terms):
    total = None
    for spot, block, first, count in terms:
        value = refs[spot][block, first : first + count, :].astype(F32)
        total = value if total is None else total + value
    return total


def amplitude(total, chunk, chunks, vir, occ, offset, src):
    owner, core = lax.axis_index("occ"), lax.axis_index("aux") % 2
    first = offset[0]
    row = jnp.broadcast_to(vir[...], total.shape)
    denom = row.T + row - occ[first + (owner * 2 + core) * chunks + chunk] - occ[first + src[chip_mask(src.shape[0])]]
    scaled = (total / denom).astype(BF16).astype(F32)
    return 2.0 * scaled - scaled.T


def merge(outputs, energies=None, after=(), through=()):
    arrays, places = [], {}

    def spot(array):
        if id(array) not in places:
            places[id(array)] = len(arrays)
            arrays.append(array)
        return places[id(array)]

    plans = [[[(spot(t[0]), *t[1:]) for t in terms] for terms in blocks] for blocks in outputs]
    shapes = [(len(blocks), blocks[0][0][3], blocks[0][0][0].shape[2]) for blocks in outputs]
    extra = [] if energies is None else list(energies)
    n_in = len(arrays) + len(extra)

    def kernel(*refs):
        outs = refs[n_in + len(after) + len(through) :][: len(outputs)]
        for plan, out in zip(plans, outs, strict=True):
            for j, terms in enumerate(plan):
                total = add_terms(refs, terms)
                if energies is not None:
                    total = amplitude(total, j, len(plan), *refs[len(arrays) : n_in])
                out[j] = total.astype(BF16)

    anywhere = pl.BlockSpec(memory_space=pl.ANY)
    vmem, smem = pl.BlockSpec(memory_space=pltpu.VMEM), pl.BlockSpec(memory_space=pltpu.SMEM)
    results = pl.pallas_call(
        kernel,
        in_specs=[vmem] * len(arrays) + [vmem, smem, smem, smem][: len(extra)] + [anywhere] * (len(after) + len(through)),
        out_specs=[vmem] * len(outputs) + [anywhere] * len(through),
        out_shape=[jax.ShapeDtypeStruct(s, BF16) for s in shapes]
        + [jax.ShapeDtypeStruct(v.shape, v.dtype) for v in through],
        input_output_aliases={n_in + len(after) + i: len(outputs) + i for i in range(len(through))},
        compiler_params=pltpu.CompilerParams(vmem_limit_bytes=12 * MIB),
        name="merge" if energies is None else "amplitude",
    )(*arrays, *extra, *after, *through)
    return results


class Halving:
    def __init__(self, terms, bits, n_occ):
        self.terms, self.bits, self.n_occ = dict(terms), list(bits), n_occ

    def leaving(self):
        return [k for k in sorted(self.terms) if k & self.bits[0]]

    def plan(self):
        return [self.terms[k] for k in self.leaving()]

    def send(self, value):
        leaving, bit = self.leaving(), self.bits.pop(0)
        arrived = swap(value, "occ", self.n_occ, bit)
        for j, k in enumerate(leaving):
            del self.terms[k]
            self.terms[k ^ bit] = self.terms[k ^ bit] + [(arrived, j, 0, value.shape[1])]
        return arrived


def density_kernel(n_occ, chunks, src_count, *refs):
    sources, amps = refs[: 2 * n_occ], refs[2 * n_occ : -2]
    out, gathered = refs[-2:]
    step = pl.program_id(0)
    width = out.shape[2]
    depth = sources[0].shape[1]

    my_core = lax.axis_index("aux") % 2

    @pl.when(step == 0)
    def _():
        spot = 0
        for core in range(2):
            for s in range(src_count):
                for chunk in range(chunks):
                    row = (my_core if core == 0 else 1 - my_core) * chunks + chunk
                    gathered[row, pl.ds(s * width, width), :] = amps[spot][chunk]
                spot += 1

    for k in range(n_occ):

        @pl.when(step == k)
        def _(k=k):
            parts = []
            for i in range(2 * chunks):
                total = jnp.dot(sources[2 * k][...], gathered[i, :depth], preferred_element_type=F32)
                total += jnp.dot(sources[2 * k + 1][...], gathered[i, depth:], preferred_element_type=F32)
                parts.append(total.astype(BF16))
            out[...] = jnp.swapaxes(jnp.stack(parts, axis=0), 0, 1)


def density_of(sources, amps, n_occ, chunks):
    rows, depth = sources[0].shape
    width = amps[0].shape[2]
    src_count = 2 * depth // width
    vmem = pl.BlockSpec(memory_space=pltpu.VMEM)
    return pl.pallas_call(
        functools.partial(density_kernel, n_occ, chunks, src_count),
        grid=(n_occ,),
        in_specs=[vmem] * (len(sources) + len(amps)),
        out_specs=pl.BlockSpec((rows, 2 * chunks, width), lambda k: (k ^ lax.axis_index("occ"), 0, 0)),
        scratch_shapes=[pltpu.VMEM((2 * chunks, 2 * depth, width), BF16)],
        out_shape=jax.ShapeDtypeStruct((n_occ * rows, 2 * chunks, width), BF16),
        compiler_params=pltpu.CompilerParams(vmem_limit_bytes=20 * MIB),
        name="density",
    )(*sources, *amps)


def solution(mesh):
    n_occ, n_aux = mesh.shape["occ"], mesh.shape["aux"]
    occ_bits = [1 << b for b in range(n_occ.bit_length() - 1)]
    n_chip = n_aux // 2

    def local(integrals, eps_occ, eps_vir, src_occ, occ_offset, vir_offset):
        rows, occ_count, width = integrals.shape
        src_count = src_occ.shape[0]
        owned = occ_count // n_occ
        chunks = owned // 2
        near, far = 2, 4
        low, high, src_t, *ints = prepare(integrals, src_occ, n_occ, chunks)
        theirs, mine = ints[:chunks], ints[chunks:]
        low_x = swap(low, "occ", n_occ, occ_bits[0])
        high_y = swap(high, "occ", n_occ, occ_bits[-1])
        src_other = swap(src_t, "aux", n_aux, 1)
        other = [None] * chunks
        for c in reversed(range(chunks)):
            other[c] = swap(theirs[c], "aux", n_aux, 1)

        vir_energy = lax.dynamic_slice_in_dim(eps_vir, vir_offset[0], width).reshape(1, width)

        def product(c, parts, pieces, after=()):
            return pair(src_t, src_other, mine[c], other[c], pieces, parts, after)

        tall = src_count // 2 * width
        small = tall // 2
        half_n = n_occ // 2
        even, odd = list(range(0, n_occ, 2)), list(range(1, n_occ, 2))
        front, back = list(range(half_n)), list(range(half_n, n_occ))
        near_pieces = [
            [(2, k) for k in odd] + [(3, k) for k in back],
            [(2, k) for k in even] + [(3, k) for k in front],
        ]
        near_got = []
        for pieces in near_pieces:
            near_got.append(swap(product(1, 4, pieces), "aux", n_aux, near))
        sent_x = product(0, 2, [(0, k) for k in odd])
        sent_y = product(0, 2, [(1, k) for k in back])
        held = [vir_energy, low_x, high_y]
        kept_x = product(0, 2, [(0, k) for k in even], held)
        kept_y = product(0, 2, [(1, k) for k in front], held)
        first_x = {2 * i: [(kept_x, i, 0, tall)] for i in range(half_n)}
        first_x |= {2 * i + 1: [(sent_x, i, 0, tall)] for i in range(half_n)}
        first_y = {i: [(kept_y, i, 0, tall)] for i in range(half_n)}
        first_y |= {half_n + i: [(sent_y, i, 0, tall)] for i in range(half_n)}
        unit_x, unit_y = Halving(first_x, occ_bits, n_occ), Halving(first_y, occ_bits[::-1], n_occ)
        got_x, got_y = unit_x.send(sent_x), unit_y.send(sent_y)
        while unit_x.bits:
            sent_x, sent_y = merge([unit_x.plan(), unit_y.plan()])
            got_x, got_y = unit_x.send(sent_x), unit_y.send(sent_y)
        near_kept = product(1, 2, [(0, k) for k in range(n_occ)], [sent_x])
        (sent,) = merge([[unit_y.terms[0]]], after=[got_x])
        got = swap(sent, "aux", n_aux, near)
        terms_0 = unit_x.terms[0] + [(got, 0, 0, tall)]

        def rows_of(terms, first, count):
            return [(array, block, start + first, count) for array, block, start, _ in terms]

        both = [{k: [(near_kept, k, small * part, small)] for k in range(n_occ)} for part in range(2)]
        for got, pieces in zip(near_got, near_pieces, strict=True):
            for j, (part, k) in enumerate(pieces):
                both[part - 2][k].append((got, j, 0, small))
        unit_x, unit_y = Halving(both[0], occ_bits, n_occ), Halving(both[1], occ_bits[::-1], n_occ)
        sent_x, sent_y = merge([unit_x.plan(), unit_y.plan()], after=[])
        got_x, got_y = unit_x.send(sent_x), unit_y.send(sent_y)

        (sent_0,) = merge([[rows_of(terms_0, small, small)]])
        got = swap(sent_0, "aux", n_aux, far)
        terms_0 = rows_of(terms_0, 0, small) + [(got, 0, 0, small)]

        while unit_x.bits:
            sent_x, sent_y = merge([unit_x.plan(), unit_y.plan()])
            got_x, got_y = unit_x.send(sent_x), unit_y.send(sent_y)
        sent, low, high, low_x, high_y = merge(
            [[unit_y.terms[0]]], after=[got_x, sent_0], through=[low, high, low_x, high_y]
        )
        low_y = swap(low, "occ", n_occ, occ_bits[-1])
        high_x = swap(high, "occ", n_occ, occ_bits[0])
        got = swap(sent, "aux", n_aux, far)
        terms_1 = unit_x.terms[0] + [(got, 0, 0, small)]

        sums = [terms_0, terms_1]
        for bit in range(2, n_chip.bit_length() - 1):
            (sent,) = merge([sums])
            got = swap(sent, "aux", n_aux, 2 << bit)
            sums = [[(sent, c, 0, small), (got, c, 0, small)] for c in range(chunks)]
        (amp,) = merge([sums], energies=[vir_energy, eps_occ, occ_offset, src_occ])
        halves = {(0, 0): low, (0, 1): high}
        halves[occ_bits[0], 0], halves[occ_bits[-1], 0] = low_x, low_y
        halves[occ_bits[0], 1], halves[occ_bits[-1], 1] = high_x, high_y
        for h, order in enumerate([occ_bits, occ_bits[::-1]]):
            have = [0]
            for bit in order:
                for k in have:
                    if (k | bit, h) not in halves:
                        halves[k | bit, h] = swap(halves[k, h], "occ", n_occ, bit)
                have = have + [k | bit for k in have]

        far_amp = swap(amp, "aux", n_aux, far)
        near_amp = swap(amp, "aux", n_aux, near)
        (far_amp,) = merge([], after=[low_y, high_x], through=[far_amp])
        both_amp = swap(far_amp, "aux", n_aux, near)
        amps = [amp, far_amp, near_amp, both_amp]
        amps += [swap(v, "aux", n_aux, 1) for v in amps]
        sources = [halves[k, h] for k in range(n_occ) for h in range(2)]
        return density_of(sources, amps, n_occ, chunks)

    in_specs = (P(("aux", "occ"), None, None), P(), P(), P(), P(), P())
    out_specs = P("aux", "occ", None)
    return jax.shard_map(local, mesh=mesh, in_specs=in_specs, out_specs=out_specs, check_vma=False)
```

time: 353 us -> 107 us (0.30)
  waiting for transfers between devices: 226 us -> 38.4 us
  local copies, waits for them, and re-layouts: 42.6 us -> 6.74 us
  matrix products: 33.7 us -> 0 us
  Pallas kernels: 0 us -> 31.7 us
  between operations: 27.5 us -> 1.5 us
  starting transfers between devices: 5.52 us -> 28.2 us
  other arithmetic: 16 us -> 0 us
    psum x2 -> x0, waiting for transfers between devices: 188 us -> none  [the longest x1 96.9 us: spread(): return lax.psum(kept, axis)]
    ppermute x0 -> x29, waiting for transfers between devices: none -> 38.4 us  [swap(): return lax.ppermute(value, axis, [(d, d ^ mask) for d in range(size)])]
    all_to_all x1 -> x0, waiting for transfers between devices: 37.9 us -> none  [local(): lax.all_to_all(integrals, 'occ', split_axis=1, concat_axis=0, tiled=True)]
    dot_general x8 -> x0, matrix products: 33.7 us -> none  [the longest x4 21.4 us: local(): lax.dot_general(source, amplitude.reshape(occ_count * virt_count, virt_co...]
    pallas_call x0 -> x17, Pallas kernels: none -> 31.7 us  [the longest x7 11.4 us: pair(): pl.pallas_call(pair_kernel, grid=(count,), in_specs=[pl.BlockSpec((tall,...]
    ppermute x0 -> x29, starting transfers between devices: none -> 28.2 us  [swap(): return lax.ppermute(value, axis, [(d, d ^ mask) for d in range(size)])]
    reshape x5 -> x0, local copies, waits for them, and re-layouts: 12.7 us -> none  [the longest x1 7.43 us: local(): density_sum.astype(jnp.bfloat16).reshape(aux_rows, occ_count, virt_count)]
    convert_element_type x5 -> x0, other arithmetic: 11.7 us -> none  [the longest x1 6.15 us: local(): scaled_wide = scaled.astype(jnp.float32)]
  transfers between devices with their start and end apart: 3 -> 29, of which waited for: 3 -> 14; matrix products, arithmetic and copies ran while one was open for 3% -> 1% of each run, Pallas kernels for 0% -> 18%
where the time goes in v2:
time: 107 us
  waiting for transfers between devices  38.4 us (36%)
  Pallas kernels  31.7 us (30%)
  starting transfers between devices  28.2 us (26%)
  local copies, waits for them, and re-layouts  6.74 us (6%)
  between operations  1.5 us (1%)
    ppermute x29, waiting for transfers between devices, swap(): return lax.ppermute(value, axis, [(d, d ^ mask) for d in range(size)])  38.4 us
    ppermute x29, starting transfers between devices, swap(): return lax.ppermute(value, axis, [(d, d ^ mask) for d in range(size)])  28.2 us
    pallas_call x7, Pallas kernels, pair(): pl.pallas_call(pair_kernel, grid=(count,), in_specs=[pl.BlockSpec((tall,...  11.4 us
    pallas_call x8, Pallas kernels, merge(): pl.pallas_call(kernel, in_specs=[vmem] * len(arrays) + [vmem, smem, smem,...  8.67 us
    pallas_call x1, Pallas kernels, density_of(): pl.pallas_call(functools.partial(density_kernel, n_occ, chunks, src_count...  8.35 us
    unnamed x30, local copies, waits for them, and re-layouts  5.96 us
    pallas_call x1, Pallas kernels, prepare(): pl.pallas_call(functools.partial(prepare_kernel, n_occ, chunks, src_count...  3.24 us
  transfers between devices with their start and end apart: 29, of which 14 were waited for; matrix products, arithmetic and copies ran while one was open for 1% of the time, Pallas kernels for 18%

profile of v2, /device:TPU:0, one launch (start us, length us, event | category | flops | bytes accessed | tf_op | source)
XLA Modules:
  0.0 106.6 jit_solution(7706833547029223621)
XLA Ops:
  0.0 2.2 %copy-done.9 = bf16[512,16,256]{2,1,0:T(8,128)(2,1)S(1)} copy-done((bf16[512,16,256]{2,1,0:T(8,128)(2,1)S(1)}, bf16[512,16,256]{2,1,0:T(8,128)(2,1)}, u32[]{:S(2)}) %copy-start.9) | copy-done | bytes 4194328
  2.8 3.2 %prepare.1 = (bf16[512,512]{1,0:T(8,128)(2,1)S(1)}, bf16[512,512]{1,0:T(8,128)(2,1)}, bf16[1024,512]{1,0:T(8,128)(2,1)S(1)}, bf16[4,512,256]{2,1,0:T(8,128)(2,1)...) custom-call(s32[4]{0:T(128)S(1)} %copy-done.13, ...), custom_call_target="tpu_custom_call" | custom-call | tf_op jit(solution)/shard_map/prepare/pallas_call | solution.py:57
  7.0 2.5 %collective-permute-start.3 = (bf16[512,512]{1,0:T(8,128)(2,1)S(1)}, bf16[512,512]{1,0:T(8,128)(2,1)S(1)}, u32[]{:S(2)}, u32[]{:S(2)}) collective-permute-start(bf16[512,512]{1,0:T(8,128)(2,1)S(1)} %get-tuple-element.28.refs_6_), channel_id=1, source_target_pairs={{0,8},{8,0},{16,24},{24,16},{1,9},{9,1},{17,25},{25,17},{2,10},{10... | collective-permute-start | bytes 1572872 | tf_op jit(solution)/shard_map/ppermute | solution.py:15
  11.1 1.6 %pair.8 = bf16[2,512,256]{2,1,0:T(8,128)(2,1)} custom-call(bf16[1024,512]{1,0:T(8,128)(2,1)S(1)} %get-tuple-element.23.src_own, bf16[1024,512]{1,0:T(8,128)(2,1)S(1)} %collective-permute-done.src_other, bf16[4,512,256]{2,1,0:T(8,128)(2,1)S(1)} %get-tuple-element.26.ints_own, bf16[4,512,256]{2,1,0:T(8,128)(2,1)S(1)} %collective-permute-done.2.ints_other), custom_call_target="tpu_custom_call" | custom-call | tf_op jit(solution)/shard_map/pair/pallas_call | solution.py:96
  12.8 2.0 %collective-permute-start.5 = (bf16[2,512,256]{2,1,0:T(8,128)(2,1)}, bf16[2,512,256]{2,1,0:T(8,128)(2,1)}, u32[]{:S(2)}, u32[]{:S(2)}) collective-permute-start(bf16[2,512,256]{2,1,0:T(8,128)(2,1)} %pair.8), channel_id=1, source_target_pairs={{0,8},{8,0},{16,24},{24,16},{1,9},{9,1},{17,25},{25,17},{2,10},{10... | collective-permute-start | bytes 1572872 | tf_op jit(solution)/shard_map/ppermute | solution.py:15
  14.8 1.6 %pair.10 = bf16[2,512,256]{2,1,0:T(8,128)(2,1)} custom-call(bf16[1024,512]{1,0:T(8,128)(2,1)S(1)} %get-tuple-element.23.src_own, bf16[1024,512]{1,0:T(8,128)(2,1)S(1)} %collective-permute-done.src_other, bf16[4,512,256]{2,1,0:T(8,128)(2,1)S(1)} %get-tuple-element.26.ints_own, bf16[4,512,256]{2,1,0:T(8,128)(2,1)S(1)} %collective-permute-done.2.ints_other), custom_call_target="tpu_custom_call" | custom-call | tf_op jit(solution)/shard_map/pair/pallas_call | solution.py:96
  17.9 2.3 %pair.13 = bf16[4,256,256]{2,1,0:T(8,128)(2,1)} custom-call(bf16[1024,512]{1,0:T(8,128)(2,1)S(1)} %get-tuple-element.23.src_own, bf16[1024,512]{1,0:T(8,128)(2,1)S(1)} %collective-permute-done.src_other, bf16[4,512,256]{2,1,0:T(8,128)(2,1)S(1)} %get-tuple-element.24.ints_own, bf16[4,512,256]{2,1,0:T(8,128)(2,1)S(1)} %collective-permute-done.1.ints_other), custom_call_target="tpu_custom_call" | custom-call | tf_op jit(solution)/shard_map/pair/pallas_call | solution.py:96
  20.3 1.6 %collective-permute-start.8 = (bf16[4,256,256]{2,1,0:T(8,128)(2,1)}, bf16[4,256,256]{2,1,0:T(8,128)(2,1)}, u32[]{:S(2)}, u32[]{:S(2)}) collective-permute-start(bf16[4,256,256]{2,1,0:T(8,128)(2,1)} %pair.13), channel_id=1, source_target_pairs={{0,2},{1,3},{2,0},{3,1},{4,6},{5,7},{6,4},{7,5},{8,10},{9,11},{10,... | collective-permute-start | bytes 1572872 | tf_op jit(solution)/shard_map/ppermute | solution.py:15
  21.8 2.2 %pair.12 = bf16[4,256,256]{2,1,0:T(8,128)(2,1)} custom-call(bf16[1024,512]{1,0:T(8,128)(2,1)S(1)} %get-tuple-element.23.src_own, bf16[1024,512]{1,0:T(8,128)(2,1)S(1)} %collective-permute-done.src_other, bf16[4,512,256]{2,1,0:T(8,128)(2,1)S(1)} %get-tuple-element.24.ints_own, bf16[4,512,256]{2,1,0:T(8,128)(2,1)S(1)} %collective-permute-done.1.ints_other), custom_call_target="tpu_custom_call" | custom-call | tf_op jit(solution)/shard_map/pair/pallas_call | solution.py:96
  30.9 2.6 %collective-permute-done.5.refs_1_ = bf16[2,512,256]{2,1,0:T(8,128)(2,1)} collective-permute-done((bf16[2,512,256]{2,1,0:T(8,128)(2,1)}, bf16[2,512,256]{2,1,0:T(8,128)(2,1)}, u32[]{:S(2)}, u32[]{:S(2)}) %collective-permute-start.5) | collective-permute-done | bytes 524320 | tf_op jit(solution)/shard_map/ppermute | solution.py:15
  33.5 1.7 %collective-permute-done.6.refs_3_.refs_1_ = bf16[2,512,256]{2,1,0:T(8,128)(2,1)} collective-permute-done((bf16[2,512,256]{2,1,0:T(8,128)(2,1)}, bf16[2,512,256]{2,1,0:T(8,128)(2,1)}, u32[]{:S(2)}, u32[]{:S(2)}) %collective-permute-start.6) | collective-permute-done | bytes 524320 | tf_op jit(solution)/shard_map/ppermute | solution.py:15
  38.6 1.8 %pair.11.refs_0_.refs_5_ = bf16[4,512,256]{2,1,0:T(8,128)(2,1)S(1)} custom-call(bf16[1024,512]{1,0:T(8,128)(2,1)S(1)} %get-tuple-element.23.src_own, bf16[1024,512]{1,0:T(8,128)(2,1)S(1)} %collective-permute-done.src_other, bf16[4,512,256]{2,1,0:T(8,128)(2,1)S(1)} %copy-done.3, bf16[4,512,256]{2,1,0:T(8,128)(2,1)S(1)} %copy-done.5, ...), custom_call_target="tpu_custom_call" | custom-call | tf_op jit(solution)/shard_map/pair/pallas_call | solution.py:96
  44.1 3.2 %collective-permute-done.14.refs_2_ = bf16[1,512,256]{2,1,0:T(8,128)(2,1)S(1)} collective-permute-done((bf16[1,512,256]{2,1,0:T(8,128)(2,1)S(1)}, bf16[1,512,256]{2,1,0:T(8,128)(2,1)S(1)}, u32[]{:S(2)}, u32[]{:S(2)}) %collective-permute-start.14) | collective-permute-done | bytes 262176 | tf_op jit(solution)/shard_map/ppermute | solution.py:15
  48.5 1.7 %collective-permute-start.15 = (bf16[1,512,256]{2,1,0:T(8,128)(2,1)S(1)}, bf16[1,512,256]{2,1,0:T(8,128)(2,1)S(1)}, u32[]{:S(2)}, u32[]{:S(2)}) collective-permute-start(bf16[1,512,256]{2,1,0:T(8,128)(2,1)S(1)} %merge.10), channel_id=1, source_target_pairs={{0,2},{1,3},{2,0},{3,1},{4,6},{5,7},{6,4},{7,5},{8,10},{9,11},{10,... | collective-permute-start | bytes 786440 | tf_op jit(solution)/shard_map/ppermute | solution.py:15
  53.3 1.6 %collective-permute-done.15.refs_3_ = bf16[1,512,256]{2,1,0:T(8,128)(2,1)S(1)} collective-permute-done((bf16[1,512,256]{2,1,0:T(8,128)(2,1)S(1)}, bf16[1,512,256]{2,1,0:T(8,128)(2,1)S(1)}, u32[]{:S(2)}, u32[]{:S(2)}) %collective-permute-start.15) | collective-permute-done | bytes 262176 | tf_op jit(solution)/shard_map/ppermute | solution.py:15
  60.8 2.6 %collective-permute-start.21 = (bf16[1,256,256]{2,1,0:T(8,128)(2,1)S(1)}, bf16[1,256,256]{2,1,0:T(8,128)(2,1)S(1)}, u32[]{:S(2)}, u32[]{:S(2)}) collective-permute-start(bf16[1,256,256]{2,1,0:T(8,128)(2,1)S(1)} %get-tuple-element.40), channel_id=1, source_target_pairs={{0,4},{1,5},{2,6},{3,7},{4,0},{5,1},{6,2},{7,3},{8,12},{9,13},{10,... | collective-permute-start | bytes 393224 | tf_op jit(solution)/shard_map/ppermute | solution.py:15
  64.4 4.5 %collective-permute-done.21.refs_9_ = bf16[1,256,256]{2,1,0:T(8,128)(2,1)S(1)} collective-permute-done((bf16[1,256,256]{2,1,0:T(8,128)(2,1)S(1)}, bf16[1,256,256]{2,1,0:T(8,128)(2,1)S(1)}, u32[]{:S(2)}, u32[]{:S(2)}) %collective-permute-start.21) | collective-permute-done | bytes 131104 | tf_op jit(solution)/shard_map/ppermute | solution.py:15
  68.9 2.8 %collective-permute-done.20.refs_4_ = bf16[1,256,256]{2,1,0:T(8,128)(2,1)S(1)} collective-permute-done((bf16[1,256,256]{2,1,0:T(8,128)(2,1)S(1)}, bf16[1,256,256]{2,1,0:T(8,128)(2,1)S(1)}, u32[]{:S(2)}, u32[]{:S(2)}) %collective-permute-start.20) | collective-permute-done | bytes 131104 | tf_op jit(solution)/shard_map/ppermute | solution.py:15
  71.7 1.6 %amplitude.1.refs_8_ = bf16[2,256,256]{2,1,0:T(8,128)(2,1)S(1)} custom-call(bf16[2,512,256]{2,1,0:T(8,128)(2,1)S(1)} %pair.7.refs_0_, bf16[2,512,256]{2,1,0:T(8,128)(2,1)} %collective-permute-done.5.refs_1_, bf16[1,512,256]{2,1,0:T(8,128)(2,1)S(1)} %collective-permute-done.13.refs_3_.refs_2_, bf16[1,512,256]{2,1,0:T(8,128)(2,1)S(1)} %collective-permute-done.15.refs_3_, ...), custom_call_target="tpu_custom_call" | custom-call | tf_op jit(solution)/shard_map/amplitude/pallas_call | solution.py:151
  76.3 8.5 %collective-permute-done.22.refs_2_ = bf16[2,256,256]{2,1,0:T(8,128)(2,1)S(1)} collective-permute-done((bf16[2,256,256]{2,1,0:T(8,128)(2,1)S(1)}, bf16[2,256,256]{2,1,0:T(8,128)(2,1)S(1)}, u32[]{:S(2)}, u32[]{:S(2)}) %collective-permute-start.22) | collective-permute-done | bytes 262176 | tf_op jit(solution)/shard_map/ppermute | solution.py:15
  84.9 2.1 %collective-permute-start.24 = (bf16[2,256,256]{2,1,0:T(8,128)(2,1)S(1)}, bf16[2,256,256]{2,1,0:T(8,128)(2,1)S(1)}, u32[]{:S(2)}, u32[]{:S(2)}) collective-permute-start(bf16[2,256,256]{2,1,0:T(8,128)(2,1)S(1)} %merge.13.refs_9_), channel_id=1, source_target_pairs={{0,2},{1,3},{2,0},{3,1},{4,6},{5,7},{6,4},{7,5},{8,10},{9,11},{10,... | collective-permute-start | bytes 786440 | tf_op jit(solution)/shard_map/ppermute | solution.py:15
  87.0 6.9 %collective-permute-done.23.refs_10_ = bf16[2,256,256]{2,1,0:T(8,128)(2,1)S(1)} collective-permute-done((bf16[2,256,256]{2,1,0:T(8,128)(2,1)S(1)}, bf16[2,256,256]{2,1,0:T(8,128)(2,1)S(1)}, u32[]{:S(2)}, u32[]{:S(2)}) %collective-permute-start.23) | collective-permute-done | bytes 262176 | tf_op jit(solution)/shard_map/ppermute | solution.py:15
  94.4 2.3 %collective-permute-done.24.refs_11_ = bf16[2,256,256]{2,1,0:T(8,128)(2,1)S(1)} collective-permute-done((bf16[2,256,256]{2,1,0:T(8,128)(2,1)S(1)}, bf16[2,256,256]{2,1,0:T(8,128)(2,1)S(1)}, u32[]{:S(2)}, u32[]{:S(2)}) %collective-permute-start.24) | collective-permute-done | bytes 262176 | tf_op jit(solution)/shard_map/ppermute | solution.py:15
  98.2 8.3 %density.1 = bf16[2048,4,256]{2,1,0:T(4,128)(2,1)} custom-call(bf16[512,512]{1,0:T(8,128)(2,1)S(1)} %get-tuple-element.36.refs_0_, bf16[512,512]{1,0:T(8,128)(2,1)} %get-tuple-element.37.refs_1_, bf16[512,512]{1,0:T(8,128)(2,1)S(1)} %get-tuple-element.38.refs_2_, bf16[512,512]{1,0:T(8,128)(2,1)S(1)} %collective-permute-done.16.refs_1_.refs_3_, ...), custom_call_target="tpu_custom_call" | custom-call | tf_op jit(solution)/shard_map/density/pallas_call | solution.py:219
  (82 shorter events, 33.5 us)
Async XLA Ops:
  6.1 5.0 %collective-permute-start = (bf16[1024,512]{1,0:T(8,128)(2,1)S(1)}, bf16[1024,512]{1,0:T(8,128)(2,1)S(1)}, u32[]{:S(2)}, u32[]{:S(2)}) collective-permute-start(bf16[1024,512]{1,0:T(8,128)(2,1)S(1)} %get-tuple-element.23.src_own), channel_id=1, source_target_pairs={{0,1},{1,0},{2,3},{3,2},{4,5},{5,4},{6,7},{7,6},{8,9},{9,8},{10,11... | collective-permute-start | bytes 3145736 | tf_op jit(solution)/shard_map/ppermute | solution.py:15
  6.6 11.3 %collective-permute-start.1 = (bf16[4,512,256]{2,1,0:T(8,128)(2,1)S(1)}, bf16[4,512,256]{2,1,0:T(8,128)(2,1)S(1)}, u32[]{:S(2)}, u32[]{:S(2)}) collective-permute-start(bf16[4,512,256]{2,1,0:T(8,128)(2,1)S(1)} %get-tuple-element.25), channel_id=1, source_target_pairs={{0,1},{1,0},{2,3},{3,2},{4,5},{5,4},{6,7},{7,6},{8,9},{9,8},{10,11... | collective-permute-start | bytes 3145736 | tf_op jit(solution)/shard_map/ppermute | solution.py:15
  7.0 17.1 %collective-permute-start.3 = (bf16[512,512]{1,0:T(8,128)(2,1)S(1)}, bf16[512,512]{1,0:T(8,128)(2,1)S(1)}, u32[]{:S(2)}, u32[]{:S(2)}) collective-permute-start(bf16[512,512]{1,0:T(8,128)(2,1)S(1)} %get-tuple-element.28.refs_6_), channel_id=1, source_target_pairs={{0,8},{8,0},{16,24},{24,16},{1,9},{9,1},{17,25},{25,17},{2,10},{10... | collective-permute-start | bytes 1572872 | tf_op jit(solution)/shard_map/ppermute | solution.py:15
  9.6 17.2 %collective-permute-start.4 = (bf16[512,512]{1,0:T(8,128)(2,1)}, bf16[512,512]{1,0:T(8,128)(2,1)}, u32[]{:S(2)}, u32[]{:S(2)}) collective-permute-start(bf16[512,512]{1,0:T(8,128)(2,1)} %get-tuple-element.29.refs_7_), channel_id=1, source_target_pairs={{0,16},{8,24},{16,0},{24,8},{1,17},{9,25},{17,1},{25,9},{2,18},{10... | collective-permute-start | bytes 1572872 | tf_op jit(solution)/shard_map/ppermute | solution.py:15
  12.8 20.7 %collective-permute-start.5 = (bf16[2,512,256]{2,1,0:T(8,128)(2,1)}, bf16[2,512,256]{2,1,0:T(8,128)(2,1)}, u32[]{:S(2)}, u32[]{:S(2)}) collective-permute-start(bf16[2,512,256]{2,1,0:T(8,128)(2,1)} %pair.8), channel_id=1, source_target_pairs={{0,8},{8,0},{16,24},{24,16},{1,9},{9,1},{17,25},{25,17},{2,10},{10... | collective-permute-start | bytes 1572872 | tf_op jit(solution)/shard_map/ppermute | solution.py:15
  16.4 18.7 %collective-permute-start.6 = (bf16[2,512,256]{2,1,0:T(8,128)(2,1)}, bf16[2,512,256]{2,1,0:T(8,128)(2,1)}, u32[]{:S(2)}, u32[]{:S(2)}) collective-permute-start(bf16[2,512,256]{2,1,0:T(8,128)(2,1)} %pair.10), channel_id=1, source_target_pairs={{0,16},{8,24},{16,0},{24,8},{1,17},{9,25},{17,1},{25,9},{2,18},{10... | collective-permute-start | bytes 1572872 | tf_op jit(solution)/shard_map/ppermute | solution.py:15
  20.3 20.2 %collective-permute-start.8 = (bf16[4,256,256]{2,1,0:T(8,128)(2,1)}, bf16[4,256,256]{2,1,0:T(8,128)(2,1)}, u32[]{:S(2)}, u32[]{:S(2)}) collective-permute-start(bf16[4,256,256]{2,1,0:T(8,128)(2,1)} %pair.13), channel_id=1, source_target_pairs={{0,2},{1,3},{2,0},{3,1},{4,6},{5,7},{6,4},{7,5},{8,10},{9,11},{10,... | collective-permute-start | bytes 1572872 | tf_op jit(solution)/shard_map/ppermute | solution.py:15
  24.9 25.2 %collective-permute-start.7 = (bf16[4,256,256]{2,1,0:T(8,128)(2,1)}, bf16[4,256,256]{2,1,0:T(8,128)(2,1)}, u32[]{:S(2)}, u32[]{:S(2)}) collective-permute-start(bf16[4,256,256]{2,1,0:T(8,128)(2,1)} %pair.12), channel_id=1, source_target_pairs={{0,2},{1,3},{2,0},{3,1},{4,6},{5,7},{6,4},{7,5},{8,10},{9,11},{10,... | collective-permute-start | bytes 1572872 | tf_op jit(solution)/shard_map/ppermute | solution.py:15
  36.5 7.6 %collective-permute-start.13 = (bf16[1,512,256]{2,1,0:T(8,128)(2,1)S(1)}, bf16[1,512,256]{2,1,0:T(8,128)(2,1)S(1)}, u32[]{:S(2)}, u32[]{:S(2)}) collective-permute-start(bf16[1,512,256]{2,1,0:T(8,128)(2,1)S(1)} %get-tuple-element.30.refs_0_), channel_id=1, source_target_pairs={{0,16},{8,24},{16,0},{24,8},{1,17},{9,25},{17,1},{25,9},{2,18},{10... | collective-permute-start | bytes 786440 | tf_op jit(solution)/shard_map/ppermute | solution.py:15
  38.1 9.2 %collective-permute-start.14 = (bf16[1,512,256]{2,1,0:T(8,128)(2,1)S(1)}, bf16[1,512,256]{2,1,0:T(8,128)(2,1)S(1)}, u32[]{:S(2)}, u32[]{:S(2)}) collective-permute-start(bf16[1,512,256]{2,1,0:T(8,128)(2,1)S(1)} %get-tuple-element.35), channel_id=1, source_target_pairs={{0,8},{8,0},{16,24},{24,16},{1,9},{9,1},{17,25},{25,17},{2,10},{10... | collective-permute-start | bytes 786440 | tf_op jit(solution)/shard_map/ppermute | solution.py:15
  41.7 9.3 %collective-permute-start.10 = (bf16[2,256,256]{2,1,0:T(8,128)(2,1)S(1)}, bf16[2,256,256]{2,1,0:T(8,128)(2,1)S(1)}, u32[]{:S(2)}, u32[]{:S(2)}) collective-permute-start(bf16[2,256,256]{2,1,0:T(8,128)(2,1)S(1)} %get-tuple-element.32), channel_id=1, source_target_pairs={{0,8},{8,0},{16,24},{24,16},{1,9},{9,1},{17,25},{25,17},{2,10},{10... | collective-permute-start | bytes 786440 | tf_op jit(solution)/shard_map/ppermute | solution.py:15
  43.2 7.7 %collective-permute-start.9 = (bf16[2,256,256]{2,1,0:T(8,128)(2,1)S(1)}, bf16[2,256,256]{2,1,0:T(8,128)(2,1)S(1)}, u32[]{:S(2)}, u32[]{:S(2)}) collective-permute-start(bf16[2,256,256]{2,1,0:T(8,128)(2,1)S(1)} %get-tuple-element.31), channel_id=1, source_target_pairs={{0,16},{8,24},{16,0},{24,8},{1,17},{9,25},{17,1},{25,9},{2,18},{10... | collective-permute-start | bytes 786440 | tf_op jit(solution)/shard_map/ppermute | solution.py:15
  48.5 6.4 %collective-permute-start.15 = (bf16[1,512,256]{2,1,0:T(8,128)(2,1)S(1)}, bf16[1,512,256]{2,1,0:T(8,128)(2,1)S(1)}, u32[]{:S(2)}, u32[]{:S(2)}) collective-permute-start(bf16[1,512,256]{2,1,0:T(8,128)(2,1)S(1)} %merge.10), channel_id=1, source_target_pairs={{0,2},{1,3},{2,0},{3,1},{4,6},{5,7},{6,4},{7,5},{8,10},{9,11},{10,... | collective-permute-start | bytes 786440 | tf_op jit(solution)/shard_map/ppermute | solution.py:15
  52.1 5.0 %collective-permute-start.11 = (bf16[1,256,256]{2,1,0:T(8,128)(2,1)S(1)}, bf16[1,256,256]{2,1,0:T(8,128)(2,1)S(1)}, u32[]{:S(2)}, u32[]{:S(2)}) collective-permute-start(bf16[1,256,256]{2,1,0:T(8,128)(2,1)S(1)} %get-tuple-element.33), channel_id=1, source_target_pairs={{0,8},{8,0},{16,24},{24,16},{1,9},{9,1},{17,25},{25,17},{2,10},{10... | collective-permute-start | bytes 393224 | tf_op jit(solution)/shard_map/ppermute | solution.py:15
  58.8 26.1 %collective-permute-start.16 = (bf16[512,512]{1,0:T(8,128)(2,1)}, bf16[512,512]{1,0:T(8,128)(2,1)S(1)}, u32[]{:S(2)}, u32[]{:S(2)}) collective-permute-start(bf16[512,512]{1,0:T(8,128)(2,1)} %get-tuple-element.37.refs_1_), channel_id=1, source_target_pairs={{0,8},{8,0},{16,24},{24,16},{1,9},{9,1},{17,25},{25,17},{2,10},{10... | collective-permute-start | bytes 1572872 | tf_op jit(solution)/shard_map/ppermute | solution.py:15
  60.3 24.5 %collective-permute-start.17 = (bf16[512,512]{1,0:T(8,128)(2,1)S(1)}, bf16[512,512]{1,0:T(8,128)(2,1)S(1)}, u32[]{:S(2)}, u32[]{:S(2)}) collective-permute-start(bf16[512,512]{1,0:T(8,128)(2,1)S(1)} %get-tuple-element.36.refs_0_), channel_id=1, source_target_pairs={{0,16},{8,24},{16,0},{24,8},{1,17},{9,25},{17,1},{25,9},{2,18},{10... | collective-permute-start | bytes 1572872 | tf_op jit(solution)/shard_map/ppermute | solution.py:15
  60.8 8.1 %collective-permute-start.21 = (bf16[1,256,256]{2,1,0:T(8,128)(2,1)S(1)}, bf16[1,256,256]{2,1,0:T(8,128)(2,1)S(1)}, u32[]{:S(2)}, u32[]{:S(2)}) collective-permute-start(bf16[1,256,256]{2,1,0:T(8,128)(2,1)S(1)} %get-tuple-element.40), channel_id=1, source_target_pairs={{0,4},{1,5},{2,6},{3,7},{4,0},{5,1},{6,2},{7,3},{8,12},{9,13},{10,... | collective-permute-start | bytes 393224 | tf_op jit(solution)/shard_map/ppermute | solution.py:15
  63.4 8.3 %collective-permute-start.20 = (bf16[1,256,256]{2,1,0:T(8,128)(2,1)S(1)}, bf16[1,256,256]{2,1,0:T(8,128)(2,1)S(1)}, u32[]{:S(2)}, u32[]{:S(2)}) collective-permute-start(bf16[1,256,256]{2,1,0:T(8,128)(2,1)S(1)} %merge.11.refs_5_), channel_id=1, source_target_pairs={{0,4},{1,5},{2,6},{3,7},{4,0},{5,1},{6,2},{7,3},{8,12},{9,13},{10,... | collective-permute-start | bytes 393224 | tf_op jit(solution)/shard_map/ppermute | solution.py:15
  73.3 11.5 %collective-permute-start.22 = (bf16[2,256,256]{2,1,0:T(8,128)(2,1)S(1)}, bf16[2,256,256]{2,1,0:T(8,128)(2,1)S(1)}, u32[]{:S(2)}, u32[]{:S(2)}) collective-permute-start(bf16[2,256,256]{2,1,0:T(8,128)(2,1)S(1)} %amplitude.1.refs_8_), channel_id=1, source_target_pairs={{0,4},{1,5},{2,6},{3,7},{4,0},{5,1},{6,2},{7,3},{8,12},{9,13},{10,... | collective-permute-start | bytes 786440 | tf_op jit(solution)/shard_map/ppermute | solution.py:15
  73.4 23.3 %collective-permute-start.18 = (bf16[512,512]{1,0:T(8,128)(2,1)S(1)}, bf16[512,512]{1,0:T(8,128)(2,1)S(1)}, u32[]{:S(2)}, u32[]{:S(2)}) collective-permute-start(bf16[512,512]{1,0:T(8,128)(2,1)S(1)} %get-tuple-element.38.refs_2_), channel_id=1, source_target_pairs={{0,16},{8,24},{16,0},{24,8},{1,17},{9,25},{17,1},{25,9},{2,18},{10... | collective-permute-start | bytes 1572872 | tf_op jit(solution)/shard_map/ppermute | solution.py:15
  75.0 21.7 %collective-permute-start.19 = (bf16[512,512]{1,0:T(8,128)(2,1)}, bf16[512,512]{1,0:T(8,128)(2,1)S(1)}, u32[]{:S(2)}, u32[]{:S(2)}) collective-permute-start(bf16[512,512]{1,0:T(8,128)(2,1)} %get-tuple-element.39.refs_5_), channel_id=1, source_target_pairs={{0,8},{8,0},{16,24},{24,16},{1,9},{9,1},{17,25},{25,17},{2,10},{10... | collective-permute-start | bytes 1572872 | tf_op jit(solution)/shard_map/ppermute | solution.py:15
  84.8 9.0 %collective-permute-start.23 = (bf16[2,256,256]{2,1,0:T(8,128)(2,1)S(1)}, bf16[2,256,256]{2,1,0:T(8,128)(2,1)S(1)}, u32[]{:S(2)}, u32[]{:S(2)}) collective-permute-start(bf16[2,256,256]{2,1,0:T(8,128)(2,1)S(1)} %amplitude.1.refs_8_), channel_id=1, source_target_pairs={{0,2},{1,3},{2,0},{3,1},{4,6},{5,7},{6,4},{7,5},{8,10},{9,11},{10,... | collective-permute-start | bytes 786440 | tf_op jit(solution)/shard_map/ppermute | solution.py:15
  84.9 9.0 %collective-permute-start.25 = (bf16[2,256,256]{2,1,0:T(8,128)(2,1)S(1)}, bf16[2,256,256]{2,1,0:T(8,128)(2,1)S(1)}, u32[]{:S(2)}, u32[]{:S(2)}) collective-permute-start(bf16[2,256,256]{2,1,0:T(8,128)(2,1)S(1)} %amplitude.1.refs_8_), channel_id=1, source_target_pairs={{0,1},{1,0},{2,3},{3,2},{4,5},{5,4},{6,7},{7,6},{8,9},{9,8},{10,11... | collective-permute-start | bytes 786440 | tf_op jit(solution)/shard_map/ppermute | solution.py:15
  84.9 11.8 %collective-permute-start.24 = (bf16[2,256,256]{2,1,0:T(8,128)(2,1)S(1)}, bf16[2,256,256]{2,1,0:T(8,128)(2,1)S(1)}, u32[]{:S(2)}, u32[]{:S(2)}) collective-permute-start(bf16[2,256,256]{2,1,0:T(8,128)(2,1)S(1)} %merge.13.refs_9_), channel_id=1, source_target_pairs={{0,2},{1,3},{2,0},{3,1},{4,6},{5,7},{6,4},{7,5},{8,10},{9,11},{10,... | collective-permute-start | bytes 786440 | tf_op jit(solution)/shard_map/ppermute | solution.py:15
  (20 other events, 158.5 us)

commit v3 on v2

v3 whole, which is shorter than its diff:
```python
import functools

import jax
import jax.numpy as jnp
from jax import lax
from jax.experimental import pallas as pl
from jax.experimental.pallas import tpu as pltpu
from jax.sharding import PartitionSpec as P

F32, BF16 = jnp.float32, jnp.bfloat16
MIB = 1 << 20


def swap(value, axis, size, mask):
    return lax.ppermute(value, axis, [(d, d ^ mask) for d in range(size)])


def whole(shape):
    return pl.BlockSpec(shape, lambda *_: (0,) * len(shape))


def chip_mask(src_count):
    chip = lax.axis_index("aux") // 2
    return (chip % 2) * (src_count // 2) + chip // 2 % 2


def prepare_kernel(n_occ, chunks, src_count, src_hbm, x_ref, *refs):
    low_a, high_a, src_b, src_t, theirs, mine = *refs[:4], refs[4 : 4 + chunks], refs[4 + chunks : -4]
    arriving, turned, src_ref, arrived = refs[-4:]
    count, step, _, width = arriving.shape
    per_half = src_count // 2
    piece = min(step, src_b.shape[0])
    copies = [
        pltpu.make_async_copy(x_ref.at[pl.ds(r * step, step)], arriving.at[r], arrived.at[r]) for r in range(count)
    ]
    src_copy = pltpu.make_async_copy(src_hbm, src_ref, arrived.at[count])
    src_copy.start()
    for copy in copies:
        copy.start()
    src_copy.wait()
    mask = chip_mask(src_count)
    my_occ, core = lax.axis_index("occ"), lax.axis_index("aux") % 2
    for r, copy in enumerate(copies):
        rows = pl.ds(r * step, step)
        copy.wait()
        turned[...] = jnp.swapaxes(arriving[r], 0, 1)
        for s in range(src_count):
            block = turned[src_ref[s ^ mask]]
            for first in range(0, step, piece):
                second, place = divmod(r * step + first, src_b.shape[0])
                out, column = (src_b, s) if second else (low_a if s < per_half else high_a, s % per_half)
                out[pl.ds(place, piece), pl.ds(column * width, width)] = block[first : first + piece]
            src_t[pl.ds(s * width, width), rows] = block.T
        for outs, side in ((theirs, 1 - core), (mine, core)):
            for chunk, out in enumerate(outs):
                for k in range(n_occ):
                    out[k, rows, :] = turned[((k ^ my_occ) * 2 + side) * chunks + chunk]


def prepare(integrals, src, n_occ, chunks):
    rows, occ_count, width = integrals.shape
    src_count = src.shape[0]
    step = min(rows, 128)
    half = src_count * width // 2
    blocks = [(n_occ, rows, width)] * (2 * chunks)
    shapes = [(rows // 2, half)] * 2 + [(rows // 2, 2 * half)] + [(src_count * width, rows)] + blocks
    vmem = pl.BlockSpec(memory_space=pltpu.VMEM)
    return pl.pallas_call(
        functools.partial(prepare_kernel, n_occ, chunks, src_count),
        in_specs=[pl.BlockSpec(memory_space=pltpu.HBM)] * 2,
        out_specs=[vmem] * len(shapes),
        out_shape=[jax.ShapeDtypeStruct(s, BF16) for s in shapes],
        scratch_shapes=[
            pltpu.VMEM((rows // step, step, occ_count, width), BF16),
            pltpu.VMEM((occ_count, step, width), BF16),
            pltpu.SMEM((src_count,), jnp.int32),
            pltpu.SemaphoreType.DMA((rows // step + 1,)),
        ],
        cost_estimate=pl.CostEstimate(flops=0, bytes_accessed=0, transcendentals=0),
        compiler_params=pltpu.CompilerParams(vmem_limit_bytes=24 * MIB),
        name="prepare",
    )(*(pltpu.with_memory_space_constraint(v, pltpu.HBM) for v in (src, integrals)))


def pair_kernel(pieces, src_own, src_other, ints_own, ints_other, *refs):
    out = refs[-1]
    tall = out.shape[1]
    for j, (part, block) in enumerate(pieces):
        rows = pl.ds(part * tall, tall)
        total = jnp.dot(src_own[rows, :], ints_own[block], preferred_element_type=F32)
        total += jnp.dot(src_other[rows, :], ints_other[block], preferred_element_type=F32)
        out[j] = total.astype(BF16)


def pair(src_own, src_other, ints_own, ints_other, pieces, parts, after=()):
    vmem = pl.BlockSpec(memory_space=pltpu.VMEM)
    tall, width = src_own.shape[0] // parts, ints_own.shape[2]
    return pl.pallas_call(
        functools.partial(pair_kernel, pieces),
        in_specs=[vmem] * 4 + [pl.BlockSpec(memory_space=pl.ANY)] * len(after),
        out_specs=vmem,
        out_shape=jax.ShapeDtypeStruct((len(pieces), tall, width), BF16),
        compiler_params=pltpu.CompilerParams(vmem_limit_bytes=16 * MIB),
        name="pair",
    )(src_own, src_other, ints_own, ints_other, *after)


def add_terms(refs, terms):
    total = None
    for spot, block, first, count in terms:
        value = refs[spot][block, first : first + count, :].astype(F32)
        total = value if total is None else total + value
    return total


def amplitude(total, chunk, chunks, vir, occ, offset, src):
    owner, core = lax.axis_index("occ"), lax.axis_index("aux") % 2
    first = offset[0]
    row = jnp.broadcast_to(vir[...], total.shape)
    denom = row.T + row - occ[first + (owner * 2 + core) * chunks + chunk] - occ[first + src[chip_mask(src.shape[0])]]
    scaled = (total / denom).astype(BF16).astype(F32)
    return 2.0 * scaled - scaled.T


def merge(outputs, energies=None, after=(), through=()):
    arrays, places = [], {}

    def spot(array):
        if id(array) not in places:
            places[id(array)] = len(arrays)
            arrays.append(array)
        return places[id(array)]

    plans = [[[(spot(t[0]), *t[1:]) for t in terms] for terms in blocks] for blocks in outputs]
    shapes = [(len(blocks), blocks[0][0][3], blocks[0][0][0].shape[2]) for blocks in outputs]
    extra = [] if energies is None else list(energies)
    n_in = len(arrays) + len(extra)

    def kernel(*refs):
        outs = refs[n_in + len(after) + len(through) :][: len(outputs)]
        for plan, out in zip(plans, outs, strict=True):
            for j, terms in enumerate(plan):
                total = add_terms(refs, terms)
                if energies is not None:
                    total = amplitude(total, j, len(plan), *refs[len(arrays) : n_in])
                out[j] = total.astype(BF16)

    anywhere = pl.BlockSpec(memory_space=pl.ANY)
    vmem, smem = pl.BlockSpec(memory_space=pltpu.VMEM), pl.BlockSpec(memory_space=pltpu.SMEM)
    results = pl.pallas_call(
        kernel,
        in_specs=[vmem] * len(arrays) + [vmem, smem, smem, smem][: len(extra)] + [anywhere] * (len(after) + len(through)),
        out_specs=[vmem] * len(outputs) + [anywhere] * len(through),
        out_shape=[jax.ShapeDtypeStruct(s, BF16) for s in shapes]
        + [jax.ShapeDtypeStruct(v.shape, v.dtype) for v in through],
        input_output_aliases={n_in + len(after) + i: len(outputs) + i for i in range(len(through))},
        compiler_params=pltpu.CompilerParams(vmem_limit_bytes=12 * MIB),
        name="merge" if energies is None else "amplitude",
    )(*arrays, *extra, *after, *through)
    return results


def spotted(values):
    arrays, spots = [], []
    for array, index in values:
        same = [array is v for v in arrays]
        if not any(same):
            arrays.append(array)
            same.append(True)
        spots.append((same.index(True), index))
    return arrays, spots


def take(refs, spot):
    number, index = spot
    return refs[number][index] if index else refs[number][...]


def cut(array, index):
    return jax.eval_shape(lambda v: v[index], array).shape


def pack_kernel(spots, sizes, *refs):
    outs = refs[-len(sizes) :]
    for out, size in zip(outs, sizes, strict=True):
        for j in range(size):
            out[j] = take(refs, spots[j])
        spots = spots[size:]


def pack(groups, after=()):
    arrays, spots = spotted([v for group in groups for v in group])
    sizes = [len(group) for group in groups]
    shape = cut(*groups[0][0])
    vmem = pl.BlockSpec(memory_space=pltpu.VMEM)
    return pl.pallas_call(
        functools.partial(pack_kernel, spots, sizes),
        in_specs=[vmem] * len(arrays) + [pl.BlockSpec(memory_space=pl.ANY)] * len(after),
        out_specs=[vmem] * len(groups),
        out_shape=[jax.ShapeDtypeStruct((size, *shape), BF16) for size in sizes],
        compiler_params=pltpu.CompilerParams(vmem_limit_bytes=12 * MIB),
        name="pack",
    )(*arrays, *after)


class Halving:
    def __init__(self, terms, bits, n_occ):
        self.terms, self.bits, self.n_occ = dict(terms), list(bits), n_occ

    def leaving(self):
        return [k for k in sorted(self.terms) if k & self.bits[0]]

    def plan(self):
        return [self.terms[k] for k in self.leaving()]

    def send(self, value):
        leaving, bit = self.leaving(), self.bits.pop(0)
        arrived = swap(value, "occ", self.n_occ, bit)
        for j, k in enumerate(leaving):
            del self.terms[k]
            self.terms[k ^ bit] = self.terms[k ^ bit] + [(arrived, j, 0, value.shape[1])]
        return arrived


def source_block(arrays, spots, k):
    low_a, low_b, high_a, high_b = (take(arrays, spot) for spot in spots[4 * k : 4 * k + 4])
    halves = [jnp.concatenate(pair_of, axis=1) for pair_of in ((low_a, high_a), (low_b, high_b))]
    return jnp.concatenate(halves, axis=0)


def gather_amplitudes(amps, chunks, gathered):
    my_core = lax.axis_index("aux") % 2
    steps = len(amps) // 2
    width = gathered.shape[2]
    for spot, amp in enumerate(amps):
        core, s = divmod(spot, steps)
        for chunk in range(chunks):
            row = (my_core if core == 0 else 1 - my_core) * chunks + chunk
            gathered[row, pl.ds(s * width, width), :] = amp[chunk]


def density_first_kernel(n_occ, chunks, spots, count, *refs):
    arrays, amps = refs[:count], refs[count:-2]
    out, gathered = refs[-2:]
    depth, width = gathered.shape[1:]
    gather_amplitudes(amps, chunks, gathered)
    for k in range(n_occ):
        sources = source_block(arrays, spots, k)[:, :depth]
        for i in range(2 * chunks):
            out[k, :, pl.ds(i * width, width)] = jnp.dot(sources, gathered[i], preferred_element_type=F32)


def density_last_kernel(n_occ, chunks, spots, count, *refs):
    arrays, amps, first = refs[:count], refs[count:-3], refs[-3]
    out, gathered = refs[-2:]
    step = pl.program_id(0)
    depth, width = gathered.shape[1:]

    @pl.when(step == 0)
    def _():
        gather_amplitudes(amps, chunks, gathered)

    for k in range(n_occ):

        @pl.when(step == k)
        def _(k=k):
            sources = source_block(arrays, spots, k)[:, -depth:]
            parts = []
            for i in range(2 * chunks):
                total = jnp.dot(sources, gathered[i], preferred_element_type=F32)
                parts.append((total + first[k, :, i * width : (i + 1) * width]).astype(BF16))
            out[...] = jnp.swapaxes(jnp.stack(parts, axis=0), 0, 1)


def density_first(sources, amps, n_occ, chunks):
    arrays, spots = spotted([v for block in sources for v in block])
    rows, width = 2 * cut(*sources[0][0])[0], amps[0][0].shape[2]
    vmem = pl.BlockSpec(memory_space=pltpu.VMEM)
    early = [amp for by_core in amps for amp in by_core]
    return pl.pallas_call(
        functools.partial(density_first_kernel, n_occ, chunks, spots, len(arrays)),
        in_specs=[vmem] * (len(arrays) + len(early)),
        out_specs=vmem,
        scratch_shapes=[pltpu.VMEM((2 * chunks, len(amps[0]) * width, width), BF16)],
        out_shape=jax.ShapeDtypeStruct((n_occ, rows, 2 * chunks * width), F32),
        compiler_params=pltpu.CompilerParams(vmem_limit_bytes=20 * MIB),
        name="density_first",
    )(*arrays, *early)


def density_last(sources, late, first, n_occ, chunks):
    arrays, spots = spotted([v for block in sources for v in block])
    rows, width = 2 * cut(*sources[0][0])[0], late[0].shape[2]
    vmem = pl.BlockSpec(memory_space=pltpu.VMEM)
    return pl.pallas_call(
        functools.partial(density_last_kernel, n_occ, chunks, spots, len(arrays)),
        grid=(n_occ,),
        in_specs=[vmem] * (len(arrays) + len(late) + 1),
        out_specs=pl.BlockSpec((rows, 2 * chunks, width), lambda k: (k ^ lax.axis_index("occ"), 0, 0)),
        scratch_shapes=[pltpu.VMEM((2 * chunks, width, width), BF16)],
        out_shape=jax.ShapeDtypeStruct((n_occ * rows, 2 * chunks, width), BF16),
        compiler_params=pltpu.CompilerParams(vmem_limit_bytes=20 * MIB),
        name="density_last",
    )(*arrays, *late, first)


def solution(mesh):
    n_occ, n_aux = mesh.shape["occ"], mesh.shape["aux"]
    occ_bits = [1 << b for b in range(n_occ.bit_length() - 1)]
    n_chip = n_aux // 2

    def local(integrals, eps_occ, eps_vir, src_occ, occ_offset, vir_offset):
        rows, occ_count, width = integrals.shape
        src_count = src_occ.shape[0]
        owned = occ_count // n_occ
        chunks = owned // 2
        near, far = 2, 4
        low_a, high_a, src_b, src_t, *ints = prepare(integrals, src_occ, n_occ, chunks)
        theirs, mine = ints[:chunks], ints[chunks:]
        columns = low_a.shape[1]
        part_low, part_high = (slice(None), slice(0, columns)), (slice(None), slice(columns, 2 * columns))
        streams = [
            (occ_bits, {0: (low_a, ()), occ_bits[0]: (swap(low_a, "occ", n_occ, occ_bits[0]), ())}),
            (occ_bits[::-1], {0: (high_a, ()), occ_bits[-1]: (swap(high_a, "occ", n_occ, occ_bits[-1]), ())}),
            (occ_bits, {0: (src_b, part_low)}),
            (occ_bits[::-1], {0: (src_b, part_high)}),
        ]
        ahead = [streams[h][1][bit][0] for h, bit in ((0, occ_bits[0]), (1, occ_bits[-1]))]

        def leaving_sources(step):
            groups = {}
            for number, (order, have) in enumerate(streams):
                blocks = [0]
                for bit in order[:step]:
                    blocks = blocks + [k | bit for k in blocks]
                wanted = [(number, k) for k in blocks if k | order[step] not in have]
                groups.setdefault(order[step], []).extend(wanted)
            return groups

        def pack_sources(groups, after=()):
            return pack([[streams[number][1][k] for number, k in group] for group in groups.values()], after)

        def send_sources(groups, packs):
            arrived = [swap(packed, "occ", n_occ, bit) for bit, packed in zip(groups, packs, strict=True)]
            for (bit, group), array in zip(groups.items(), arrived, strict=True):
                for j, (number, k) in enumerate(group):
                    streams[number][1][k | bit] = (array, (j,))
            return arrived

        src_other = swap(src_t, "aux", n_aux, 1)
        other = [None] * chunks
        for c in reversed(range(chunks)):
            other[c] = swap(theirs[c], "aux", n_aux, 1)

        vir_energy = lax.dynamic_slice_in_dim(eps_vir, vir_offset[0], width).reshape(1, width)

        def product(c, parts, pieces, after=()):
            return pair(src_t, src_other, mine[c], other[c], pieces, parts, after)

        tall = src_count // 2 * width
        small = tall // 2
        half_n = n_occ // 2
        even, odd = list(range(0, n_occ, 2)), list(range(1, n_occ, 2))
        front, back = list(range(half_n)), list(range(half_n, n_occ))
        near_pieces = [
            [(2, k) for k in odd] + [(3, k) for k in back],
            [(2, k) for k in even] + [(3, k) for k in front],
        ]
        near_sent = product(1, 4, near_pieces[0])
        near_got = [swap(near_sent, "aux", n_aux, near)]
        sent_x = product(0, 2, [(0, k) for k in odd], [near_sent])
        sent_y = product(0, 2, [(1, k) for k in back], [near_sent, *ahead])
        near_got.append(swap(product(1, 4, near_pieces[1], [sent_x, sent_y]), "aux", n_aux, near))
        held = [vir_energy, near_got[0]]
        kept_x = product(0, 2, [(0, k) for k in even], held)
        kept_y = product(0, 2, [(1, k) for k in front], held)
        first_x = {2 * i: [(kept_x, i, 0, tall)] for i in range(half_n)}
        first_x |= {2 * i + 1: [(sent_x, i, 0, tall)] for i in range(half_n)}
        first_y = {i: [(kept_y, i, 0, tall)] for i in range(half_n)}
        first_y |= {half_n + i: [(sent_y, i, 0, tall)] for i in range(half_n)}
        unit_x, unit_y = Halving(first_x, occ_bits, n_occ), Halving(first_y, occ_bits[::-1], n_occ)
        got_x, got_y = unit_x.send(sent_x), unit_y.send(sent_y)
        while unit_x.bits:
            sent_x, sent_y = merge([unit_x.plan(), unit_y.plan()])
            got_x, got_y = unit_x.send(sent_x), unit_y.send(sent_y)
        near_kept = product(1, 2, [(0, k) for k in range(n_occ)], [sent_x])
        (sent,) = merge([[unit_y.terms[0]]], after=[got_x])
        got = swap(sent, "aux", n_aux, near)
        terms_0 = unit_x.terms[0] + [(got, 0, 0, tall)]

        def rows_of(terms, first, count):
            return [(array, block, start + first, count) for array, block, start, _ in terms]

        both = [{k: [(near_kept, k, small * part, small)] for k in range(n_occ)} for part in range(2)]
        for got, pieces in zip(near_got, near_pieces, strict=True):
            for j, (part, k) in enumerate(pieces):
                both[part - 2][k].append((got, j, 0, small))
        unit_x, unit_y = Halving(both[0], occ_bits, n_occ), Halving(both[1], occ_bits[::-1], n_occ)
        sent_x, sent_y = merge([unit_x.plan(), unit_y.plan()], after=[])
        got_x, got_y = unit_x.send(sent_x), unit_y.send(sent_y)

        while unit_x.bits:
            sent_x, sent_y = merge([unit_x.plan(), unit_y.plan()])
            got_x, got_y = unit_x.send(sent_x), unit_y.send(sent_y)
        sent, src_b = merge(
            [[rows_of(terms_0, small, small), unit_y.terms[0]]],
            after=[got_x],
            through=[src_b],
        )
        got = swap(sent, "aux", n_aux, far)
        terms_0 = rows_of(terms_0, 0, small) + [(got, 0, 0, small)]
        terms_1 = unit_x.terms[0] + [(got, 1, 0, small)]
        for number, part in ((2, part_low), (3, part_high)):
            streams[number][1][0] = (src_b, part)
        for bit in {occ_bits[0], occ_bits[-1]}:
            arrived = swap(src_b, "occ", n_occ, bit)
            streams[2][1][bit], streams[3][1][bit] = (arrived, part_low), (arrived, part_high)
        for step in range(len(occ_bits)):
            groups = leaving_sources(step)
            if any(groups.values()):
                last = send_sources(groups, pack_sources(groups, [got]))

        sums = [terms_0, terms_1]
        for bit in range(2, n_chip.bit_length() - 1):
            (sent,) = merge([sums])
            got = swap(sent, "aux", n_aux, 2 << bit)
            sums = [[(sent, c, 0, small), (got, c, 0, small)] for c in range(chunks)]
        (amp,) = merge([sums], energies=[vir_energy, eps_occ, occ_offset, src_occ])
        far_amp, near_amp = swap(amp, "aux", n_aux, far), swap(amp, "aux", n_aux, near)
        far_amp, near_amp, amp = merge([], through=[far_amp, near_amp, amp])
        both_amp = swap(far_amp, "aux", n_aux, near)
        amps = [amp, far_amp, near_amp]
        other = [swap(v, "aux", n_aux, 1) for v in amps]
        sources = [[streams[number][1][k] for number in (0, 2, 1, 3)] for k in range(n_occ)]
        first = density_first(sources, [amps, other], n_occ, chunks)
        (both_amp,) = merge([], after=[first], through=[both_amp])
        late = [both_amp, swap(both_amp, "aux", n_aux, 1)]
        return density_last(sources, late, first, n_occ, chunks)

    in_specs = (P(("aux", "occ"), None, None), P(), P(), P(), P(), P())
    out_specs = P("aux", "occ", None)
    return jax.shard_map(local, mesh=mesh, in_specs=in_specs, out_specs=out_specs, check_vma=False)
```

time: 107 us -> 99.1 us (0.926)
  local copies, waits for them, and re-layouts: 6.74 us -> 2.06 us
  Pallas kernels: 31.7 us -> 27.4 us
  starting transfers between devices: 28.2 us -> 32.2 us
  waiting for transfers between devices: 38.4 us -> 35.5 us
    unnamed x30 -> x32, local copies, waits for them, and re-layouts: 5.96 us -> 1.29 us
    ppermute x29 -> x28, starting transfers between devices: 28.2 us -> 32.2 us  [swap(): return lax.ppermute(value, axis, [(d, d ^ mask) for d in range(size)])]
    pallas_call x8 -> x10, Pallas kernels: 19.8 us -> 16.5 us  [the longest x7 8.71 us: pair(): pl.pallas_call(functools.partial(pair_kernel, pieces), in_specs=[vmem] *...]
    ppermute x29 -> x28, waiting for transfers between devices: 38.4 us -> 35.5 us  [swap(): return lax.ppermute(value, axis, [(d, d ^ mask) for d in range(size)])]
  transfers between devices with their start and end apart: 29 -> 28, of which waited for: 14 -> 16; matrix products, arithmetic and copies ran while one was open for 1% -> 1% of each run, Pallas kernels for 18% -> 19%
where the time goes in v3:
time: 99.1 us; the launch traced here: 98.7 us
  waiting for transfers between devices  35.5 us (36%)
  starting transfers between devices  32.2 us (32%)
  Pallas kernels  27.4 us (28%)
  local copies, waits for them, and re-layouts  2.06 us (2%)
  between operations  1.55 us (2%)
    ppermute x28, waiting for transfers between devices, swap(): return lax.ppermute(value, axis, [(d, d ^ mask) for d in range(size)])  35.5 us
    ppermute x28, starting transfers between devices, swap(): return lax.ppermute(value, axis, [(d, d ^ mask) for d in range(size)])  32.2 us
    pallas_call x7, Pallas kernels, pair(): pl.pallas_call(functools.partial(pair_kernel, pieces), in_specs=[vmem] *...  8.71 us
    pallas_call x8, Pallas kernels, merge(): pl.pallas_call(kernel, in_specs=[vmem] * len(arrays) + [vmem, smem, smem,...  7.7 us
    pallas_call x1, Pallas kernels, density_last(): pl.pallas_call(functools.partial(density_last_kernel, n_occ, chunks, spot...  4.18 us
    pallas_call x1, Pallas kernels, density_first(): pl.pallas_call(functools.partial(density_first_kernel, n_occ, chunks, spo...  3.49 us
    pallas_call x1, Pallas kernels, prepare(): pl.pallas_call(functools.partial(prepare_kernel, n_occ, chunks, src_count...  3.2 us
  transfers between devices with their start and end apart: 28, of which 16 were waited for; matrix products, arithmetic and copies ran while one was open for 1% of the time, Pallas kernels for 19%

profile of v3, /device:TPU:0, one launch (start us, length us, event | category | flops | bytes accessed | tf_op | source)
XLA Modules:
  0.0 98.7 jit_solution(14099316132892838251)
XLA Ops:
  0.0 3.2 %prepare.1 = (bf16[256,512]{1,0:T(8,128)(2,1)S(1)}, bf16[256,512]{1,0:T(8,128)(2,1)S(1)}, bf16[256,1024]{1,0:T(8,128)(2,1)S(1)}, bf16[1024,512]{1,0:T(8,128)(2,1...) custom-call(s32[4]{0:T(128)} %refs_12_.1, ...), custom_call_target="tpu_custom_call" | custom-call | tf_op jit(solution)/shard_map/prepare/pallas_call | solution.py:68
  4.3 2.6 %collective-permute-start.5 = (bf16[256,512]{1,0:T(8,128)(2,1)S(1)}, bf16[256,512]{1,0:T(8,128)(2,1)S(1)}, u32[]{:S(2)}, u32[]{:S(2)}) collective-permute-start(bf16[256,512]{1,0:T(8,128)(2,1)S(1)} %get-tuple-element.26.refs_0_), channel_id=1, source_target_pairs={{0,8},{8,0},{16,24},{24,16},{1,9},{9,1},{17,25},{25,17},{2,10},{10... | collective-permute-start | bytes 786440 | tf_op jit(solution)/shard_map/ppermute | solution.py:15
  6.8 1.5 %collective-permute-start.6 = (bf16[256,512]{1,0:T(8,128)(2,1)S(1)}, bf16[256,512]{1,0:T(8,128)(2,1)S(1)}, u32[]{:S(2)}, u32[]{:S(2)}) collective-permute-start(bf16[256,512]{1,0:T(8,128)(2,1)S(1)} %get-tuple-element.32.refs_3_.refs_2_), channel_id=1, source_target_pairs={{0,16},{8,24},{16,0},{24,8},{1,17},{9,25},{17,1},{25,9},{2,18},{10... | collective-permute-start | bytes 786440 | tf_op jit(solution)/shard_map/ppermute | solution.py:15
  9.9 2.1 %collective-permute-start.3 = (bf16[4,256,256]{2,1,0:T(8,128)(2,1)}, bf16[4,256,256]{2,1,0:T(8,128)(2,1)}, u32[]{:S(2)}, u32[]{:S(2)}) collective-permute-start(bf16[4,256,256]{2,1,0:T(8,128)(2,1)} %pair.7.refs_0_), channel_id=1, source_target_pairs={{0,2},{1,3},{2,0},{3,1},{4,6},{5,7},{6,4},{7,5},{8,10},{9,11},{10,... | collective-permute-start | bytes 1572872 | tf_op jit(solution)/shard_map/ppermute | solution.py:15
  13.5 1.6 %collective-permute-start.4 = (bf16[2,512,256]{2,1,0:T(8,128)(2,1)}, bf16[2,512,256]{2,1,0:T(8,128)(2,1)}, u32[]{:S(2)}, u32[]{:S(2)}) collective-permute-start(bf16[2,512,256]{2,1,0:T(8,128)(2,1)} %pair.9.refs_0_), channel_id=1, source_target_pairs={{0,8},{8,0},{16,24},{24,16},{1,9},{9,1},{17,25},{25,17},{2,10},{10... | collective-permute-start | bytes 1572872 | tf_op jit(solution)/shard_map/ppermute | solution.py:15
  16.7 1.5 %collective-permute-start.7 = (bf16[2,512,256]{2,1,0:T(8,128)(2,1)}, bf16[2,512,256]{2,1,0:T(8,128)(2,1)}, u32[]{:S(2)}, u32[]{:S(2)}) collective-permute-start(bf16[2,512,256]{2,1,0:T(8,128)(2,1)} %pair.11.refs_1_), channel_id=1, source_target_pairs={{0,16},{8,24},{16,0},{24,8},{1,17},{9,25},{17,1},{25,9},{2,18},{10... | collective-permute-start | bytes 1572872 | tf_op jit(solution)/shard_map/ppermute | solution.py:15
  18.3 1.5 %pair.13 = bf16[4,256,256]{2,1,0:T(8,128)(2,1)} custom-call(bf16[1024,512]{1,0:T(8,128)(2,1)S(1)} %get-tuple-element.27.src_own, bf16[1024,512]{1,0:T(8,128)(2,1)S(1)} %collective-permute-done.src_other, bf16[4,512,256]{2,1,0:T(8,128)(2,1)S(1)} %get-tuple-element.30.ints_own, bf16[4,512,256]{2,1,0:T(8,128)(2,1)S(1)} %collective-permute-done.2.ints_other, ...), custom_call_target="tpu_custom_call" | custom-call | tf_op jit(solution)/shard_map/pair/pallas_call | solution.py:98
  19.8 1.6 %collective-permute-start.11 = (bf16[4,256,256]{2,1,0:T(8,128)(2,1)}, bf16[4,256,256]{2,1,0:T(8,128)(2,1)}, u32[]{:S(2)}, u32[]{:S(2)}) collective-permute-start(bf16[4,256,256]{2,1,0:T(8,128)(2,1)} %pair.13), channel_id=1, source_target_pairs={{0,2},{1,3},{2,0},{3,1},{4,6},{5,7},{6,4},{7,5},{8,10},{9,11},{10,... | collective-permute-start | bytes 1572872 | tf_op jit(solution)/shard_map/ppermute | solution.py:15
  22.8 2.3 %collective-permute-done.3.refs_1_ = bf16[4,256,256]{2,1,0:T(8,128)(2,1)} collective-permute-done((bf16[4,256,256]{2,1,0:T(8,128)(2,1)}, bf16[4,256,256]{2,1,0:T(8,128)(2,1)}, u32[]{:S(2)}, u32[]{:S(2)}) %collective-permute-start.3) | collective-permute-done | bytes 524320 | tf_op jit(solution)/shard_map/ppermute | solution.py:15
  27.7 2.6 %collective-permute-done.7.refs_3_.refs_1_ = bf16[2,512,256]{2,1,0:T(8,128)(2,1)} collective-permute-done((bf16[2,512,256]{2,1,0:T(8,128)(2,1)}, bf16[2,512,256]{2,1,0:T(8,128)(2,1)}, u32[]{:S(2)}, u32[]{:S(2)}) %collective-permute-start.7) | collective-permute-done | bytes 524320 | tf_op jit(solution)/shard_map/ppermute | solution.py:15
  32.3 1.5 %collective-permute-start.8 = (bf16[1,512,256]{2,1,0:T(8,128)(2,1)S(1)}, bf16[1,512,256]{2,1,0:T(8,128)(2,1)S(1)}, u32[]{:S(2)}, u32[]{:S(2)}) collective-permute-start(bf16[1,512,256]{2,1,0:T(8,128)(2,1)S(1)} %get-tuple-element.33.refs_0_), channel_id=1, source_target_pairs={{0,16},{8,24},{16,0},{24,8},{1,17},{9,25},{17,1},{25,9},{2,18},{10... | collective-permute-start | bytes 786440 | tf_op jit(solution)/shard_map/ppermute | solution.py:15
  47.1 1.5 %collective-permute-start.15 = (bf16[1,256,256]{2,1,0:T(8,128)(2,1)S(1)}, bf16[1,256,256]{2,1,0:T(8,128)(2,1)S(1)}, u32[]{:S(2)}, u32[]{:S(2)}) collective-permute-start(bf16[1,256,256]{2,1,0:T(8,128)(2,1)S(1)} %get-tuple-element.38), channel_id=1, source_target_pairs={{0,16},{8,24},{16,0},{24,8},{1,17},{9,25},{17,1},{25,9},{2,18},{10... | collective-permute-start | bytes 393224 | tf_op jit(solution)/shard_map/ppermute | solution.py:15
  48.6 2.1 %collective-permute-done.14.refs_7_ = bf16[1,256,256]{2,1,0:T(8,128)(2,1)S(1)} collective-permute-done((bf16[1,256,256]{2,1,0:T(8,128)(2,1)S(1)}, bf16[1,256,256]{2,1,0:T(8,128)(2,1)S(1)}, u32[]{:S(2)}, u32[]{:S(2)}) %collective-permute-start.14) | collective-permute-done | bytes 131104 | tf_op jit(solution)/shard_map/ppermute | solution.py:15
  53.4 1.6 %collective-permute-start.17 = (bf16[256,1024]{1,0:T(8,128)(2,1)S(1)}, bf16[256,1024]{1,0:T(8,128)(2,1)S(1)}, u32[]{:S(2)}, u32[]{:S(2)}) collective-permute-start(bf16[256,1024]{1,0:T(8,128)(2,1)S(1)} %get-tuple-element.40.refs_1_), channel_id=1, source_target_pairs={{0,16},{8,24},{16,0},{24,8},{1,17},{9,25},{17,1},{25,9},{2,18},{10... | collective-permute-start | bytes 1572872 | tf_op jit(solution)/shard_map/ppermute | solution.py:15
  55.5 2.6 %collective-permute-start.18 = (bf16[2,256,256]{2,1,0:T(8,128)(2,1)S(1)}, bf16[2,256,256]{2,1,0:T(8,128)(2,1)S(1)}, u32[]{:S(2)}, u32[]{:S(2)}) collective-permute-start(bf16[2,256,256]{2,1,0:T(8,128)(2,1)S(1)} %get-tuple-element.41), channel_id=1, source_target_pairs={{0,4},{1,5},{2,6},{3,7},{4,0},{5,1},{6,2},{7,3},{8,12},{9,13},{10,... | collective-permute-start | bytes 786440 | tf_op jit(solution)/shard_map/ppermute | solution.py:15
  58.7 7.7 %collective-permute-done.18.refs_6_.refs_4_ = bf16[2,256,256]{2,1,0:T(8,128)(2,1)S(1)} collective-permute-done((bf16[2,256,256]{2,1,0:T(8,128)(2,1)S(1)}, bf16[2,256,256]{2,1,0:T(8,128)(2,1)S(1)}, u32[]{:S(2)}, u32[]{:S(2)}) %collective-permute-start.18) | collective-permute-done | bytes 262176 | tf_op jit(solution)/shard_map/ppermute | solution.py:15
  66.4 1.6 %amplitude.1.refs_2_ = bf16[2,256,256]{2,1,0:T(8,128)(2,1)S(1)} custom-call(bf16[2,512,256]{2,1,0:T(8,128)(2,1)S(1)} %pair.8.refs_0_, bf16[2,512,256]{2,1,0:T(8,128)(2,1)} %collective-permute-done.4.refs_1_, bf16[1,512,256]{2,1,0:T(8,128)(2,1)S(1)} %collective-permute-done.8.refs_3_.refs_2_, bf16[1,512,256]{2,1,0:T(8,128)(2,1)S(1)} %collective-permute-done.10.refs_3_, ...), custom_call_target="tpu_custom_call" | custom-call | tf_op jit(solution)/shard_map/amplitude/pallas_call | solution.py:150
  68.8 3.4 %collective-permute-start.21 = (bf16[2,256,256]{2,1,0:T(8,128)(2,1)S(1)}, bf16[2,256,256]{2,1,0:T(8,128)(2,1)S(1)}, u32[]{:S(2)}, u32[]{:S(2)}) collective-permute-start(bf16[2,256,256]{2,1,0:T(8,128)(2,1)S(1)} %amplitude.1.refs_2_), channel_id=1, source_target_pairs={{0,4},{1,5},{2,6},{3,7},{4,0},{5,1},{6,2},{7,3},{8,12},{9,13},{10,... | collective-permute-start | bytes 786440 | tf_op jit(solution)/shard_map/ppermute | solution.py:15
  74.4 5.3 %collective-permute-done.22.refs_1_ = bf16[2,256,256]{2,1,0:T(8,128)(2,1)S(1)} collective-permute-done((bf16[2,256,256]{2,1,0:T(8,128)(2,1)S(1)}, bf16[2,256,256]{2,1,0:T(8,128)(2,1)S(1)}, u32[]{:S(2)}, u32[]{:S(2)}) %collective-permute-start.22) | collective-permute-done | bytes 262176 | tf_op jit(solution)/shard_map/ppermute | solution.py:15
  79.8 2.3 %collective-permute-done.21.refs_0_ = bf16[2,256,256]{2,1,0:T(8,128)(2,1)S(1)} collective-permute-done((bf16[2,256,256]{2,1,0:T(8,128)(2,1)S(1)}, bf16[2,256,256]{2,1,0:T(8,128)(2,1)S(1)}, u32[]{:S(2)}, u32[]{:S(2)}) %collective-permute-start.21) | collective-permute-done | bytes 262176 | tf_op jit(solution)/shard_map/ppermute | solution.py:15
  84.4 5.0 %collective-permute-done.19.refs_5_ = bf16[3,256,512]{2,1,0:T(8,128)(2,1)S(1)} collective-permute-done((bf16[3,256,512]{2,1,0:T(8,128)(2,1)S(1)}, bf16[3,256,512]{2,1,0:T(8,128)(2,1)S(1)}, u32[]{:S(2)}, u32[]{:S(2)}) %collective-permute-start.19) | collective-permute-done | bytes 786464 | tf_op jit(solution)/shard_map/ppermute | solution.py:15
  89.4 3.5 %density_first.1.refs_0_.refs_11_ = f32[4,512,1024]{2,1,0:T(8,128)S(1)} custom-call(bf16[256,512]{1,0:T(8,128)(2,1)S(1)} %copy-done.11, bf16[256,1024]{1,0:T(8,128)(2,1)S(1)} %get-tuple-element.40.refs_1_, bf16[256,512]{1,0:T(8,128)(2,1)S(1)} %copy-done.13, bf16[256,512]{1,0:T(8,128)(2,1)S(1)} %collective-permute-done.5.refs_1_.refs_3_, ...), custom_call_target="tpu_custom_call" | custom-call | tf_op jit(solution)/shard_map/density_first/pallas_call | solution.py:280
  93.0 1.5 %collective-permute-done.27.refs_10_ = bf16[2,256,256]{2,1,0:T(8,128)(2,1)S(1)} collective-permute-done((bf16[2,256,256]{2,1,0:T(8,128)(2,1)S(1)}, bf16[2,256,256]{2,1,0:T(8,128)(2,1)S(1)}, u32[]{:S(2)}, u32[]{:S(2)}) %collective-permute-start.27) | collective-permute-done | bytes 262176 | tf_op jit(solution)/shard_map/ppermute | solution.py:15
  94.5 4.2 %density_last.1 = bf16[2048,4,256]{2,1,0:T(4,128)(2,1)} custom-call(bf16[256,512]{1,0:T(8,128)(2,1)S(1)} %copy-done.11, bf16[256,1024]{1,0:T(8,128)(2,1)S(1)} %get-tuple-element.40.refs_1_, bf16[256,512]{1,0:T(8,128)(2,1)S(1)} %copy-done.13, bf16[256,512]{1,0:T(8,128)(2,1)S(1)} %collective-permute-done.5.refs_1_.refs_3_, ...), custom_call_target="tpu_custom_call" | custom-call | tf_op jit(solution)/shard_map/density_last/pallas_call | solution.py:295
  (84 shorter events, 33.0 us)
Async XLA Ops:
  3.2 5.1 %collective-permute-start.2 = (bf16[4,512,256]{2,1,0:T(8,128)(2,1)S(1)}, bf16[4,512,256]{2,1,0:T(8,128)(2,1)S(1)}, u32[]{:S(2)}, u32[]{:S(2)}) collective-permute-start(bf16[4,512,256]{2,1,0:T(8,128)(2,1)S(1)} %get-tuple-element.31), channel_id=1, source_target_pairs={{0,1},{1,0},{2,3},{3,2},{4,5},{5,4},{6,7},{7,6},{8,9},{9,8},{10,11... | collective-permute-start | bytes 3145736 | tf_op jit(solution)/shard_map/ppermute | solution.py:15
  3.8 4.6 %collective-permute-start = (bf16[1024,512]{1,0:T(8,128)(2,1)S(1)}, bf16[1024,512]{1,0:T(8,128)(2,1)S(1)}, u32[]{:S(2)}, u32[]{:S(2)}) collective-permute-start(bf16[1024,512]{1,0:T(8,128)(2,1)S(1)} %get-tuple-element.27.src_own), channel_id=1, source_target_pairs={{0,1},{1,0},{2,3},{3,2},{4,5},{5,4},{6,7},{7,6},{8,9},{9,8},{10,11... | collective-permute-start | bytes 3145736 | tf_op jit(solution)/shard_map/ppermute | solution.py:15
  3.8 8.2 %collective-permute-start.1 = (bf16[4,512,256]{2,1,0:T(8,128)(2,1)S(1)}, bf16[4,512,256]{2,1,0:T(8,128)(2,1)S(1)}, u32[]{:S(2)}, u32[]{:S(2)}) collective-permute-start(bf16[4,512,256]{2,1,0:T(8,128)(2,1)S(1)} %get-tuple-element.29), channel_id=1, source_target_pairs={{0,1},{1,0},{2,3},{3,2},{4,5},{5,4},{6,7},{7,6},{8,9},{9,8},{10,11... | collective-permute-start | bytes 3145736 | tf_op jit(solution)/shard_map/ppermute | solution.py:15
  4.3 10.8 %collective-permute-start.5 = (bf16[256,512]{1,0:T(8,128)(2,1)S(1)}, bf16[256,512]{1,0:T(8,128)(2,1)S(1)}, u32[]{:S(2)}, u32[]{:S(2)}) collective-permute-start(bf16[256,512]{1,0:T(8,128)(2,1)S(1)} %get-tuple-element.26.refs_0_), channel_id=1, source_target_pairs={{0,8},{8,0},{16,24},{24,16},{1,9},{9,1},{17,25},{25,17},{2,10},{10... | collective-permute-start | bytes 786440 | tf_op jit(solution)/shard_map/ppermute | solution.py:15
  6.8 8.4 %collective-permute-start.6 = (bf16[256,512]{1,0:T(8,128)(2,1)S(1)}, bf16[256,512]{1,0:T(8,128)(2,1)S(1)}, u32[]{:S(2)}, u32[]{:S(2)}) collective-permute-start(bf16[256,512]{1,0:T(8,128)(2,1)S(1)} %get-tuple-element.32.refs_3_.refs_2_), channel_id=1, source_target_pairs={{0,16},{8,24},{16,0},{24,8},{1,17},{9,25},{17,1},{25,9},{2,18},{10... | collective-permute-start | bytes 786440 | tf_op jit(solution)/shard_map/ppermute | solution.py:15
  9.9 15.1 %collective-permute-start.3 = (bf16[4,256,256]{2,1,0:T(8,128)(2,1)}, bf16[4,256,256]{2,1,0:T(8,128)(2,1)}, u32[]{:S(2)}, u32[]{:S(2)}) collective-permute-start(bf16[4,256,256]{2,1,0:T(8,128)(2,1)} %pair.7.refs_0_), channel_id=1, source_target_pairs={{0,2},{1,3},{2,0},{3,1},{4,6},{5,7},{6,4},{7,5},{8,10},{9,11},{10,... | collective-permute-start | bytes 1572872 | tf_op jit(solution)/shard_map/ppermute | solution.py:15
  13.5 14.2 %collective-permute-start.4 = (bf16[2,512,256]{2,1,0:T(8,128)(2,1)}, bf16[2,512,256]{2,1,0:T(8,128)(2,1)}, u32[]{:S(2)}, u32[]{:S(2)}) collective-permute-start(bf16[2,512,256]{2,1,0:T(8,128)(2,1)} %pair.9.refs_0_), channel_id=1, source_target_pairs={{0,8},{8,0},{16,24},{24,16},{1,9},{9,1},{17,25},{25,17},{2,10},{10... | collective-permute-start | bytes 1572872 | tf_op jit(solution)/shard_map/ppermute | solution.py:15
  16.7 13.6 %collective-permute-start.7 = (bf16[2,512,256]{2,1,0:T(8,128)(2,1)}, bf16[2,512,256]{2,1,0:T(8,128)(2,1)}, u32[]{:S(2)}, u32[]{:S(2)}) collective-permute-start(bf16[2,512,256]{2,1,0:T(8,128)(2,1)} %pair.11.refs_1_), channel_id=1, source_target_pairs={{0,16},{8,24},{16,0},{24,8},{1,17},{9,25},{17,1},{25,9},{2,18},{10... | collective-permute-start | bytes 1572872 | tf_op jit(solution)/shard_map/ppermute | solution.py:15
  19.8 23.5 %collective-permute-start.11 = (bf16[4,256,256]{2,1,0:T(8,128)(2,1)}, bf16[4,256,256]{2,1,0:T(8,128)(2,1)}, u32[]{:S(2)}, u32[]{:S(2)}) collective-permute-start(bf16[4,256,256]{2,1,0:T(8,128)(2,1)} %pair.13), channel_id=1, source_target_pairs={{0,2},{1,3},{2,0},{3,1},{4,6},{5,7},{6,4},{7,5},{8,10},{9,11},{10,... | collective-permute-start | bytes 1572872 | tf_op jit(solution)/shard_map/ppermute | solution.py:15
  31.7 8.0 %collective-permute-start.9 = (bf16[1,512,256]{2,1,0:T(8,128)(2,1)S(1)}, bf16[1,512,256]{2,1,0:T(8,128)(2,1)S(1)}, u32[]{:S(2)}, u32[]{:S(2)}) collective-permute-start(bf16[1,512,256]{2,1,0:T(8,128)(2,1)S(1)} %get-tuple-element.34), channel_id=1, source_target_pairs={{0,8},{8,0},{16,24},{24,16},{1,9},{9,1},{17,25},{25,17},{2,10},{10... | collective-permute-start | bytes 786440 | tf_op jit(solution)/shard_map/ppermute | solution.py:15
  32.3 8.6 %collective-permute-start.8 = (bf16[1,512,256]{2,1,0:T(8,128)(2,1)S(1)}, bf16[1,512,256]{2,1,0:T(8,128)(2,1)S(1)}, u32[]{:S(2)}, u32[]{:S(2)}) collective-permute-start(bf16[1,512,256]{2,1,0:T(8,128)(2,1)S(1)} %get-tuple-element.33.refs_0_), channel_id=1, source_target_pairs={{0,16},{8,24},{16,0},{24,8},{1,17},{9,25},{17,1},{25,9},{2,18},{10... | collective-permute-start | bytes 786440 | tf_op jit(solution)/shard_map/ppermute | solution.py:15
  36.2 8.2 %collective-permute-start.12 = (bf16[2,256,256]{2,1,0:T(8,128)(2,1)S(1)}, bf16[2,256,256]{2,1,0:T(8,128)(2,1)S(1)}, u32[]{:S(2)}, u32[]{:S(2)}) collective-permute-start(bf16[2,256,256]{2,1,0:T(8,128)(2,1)S(1)} %get-tuple-element.35), channel_id=1, source_target_pairs={{0,16},{8,24},{16,0},{24,8},{1,17},{9,25},{17,1},{25,9},{2,18},{10... | collective-permute-start | bytes 786440 | tf_op jit(solution)/shard_map/ppermute | solution.py:15
  36.8 7.7 %collective-permute-start.13 = (bf16[2,256,256]{2,1,0:T(8,128)(2,1)S(1)}, bf16[2,256,256]{2,1,0:T(8,128)(2,1)S(1)}, u32[]{:S(2)}, u32[]{:S(2)}) collective-permute-start(bf16[2,256,256]{2,1,0:T(8,128)(2,1)S(1)} %get-tuple-element.36), channel_id=1, source_target_pairs={{0,8},{8,0},{16,24},{24,16},{1,9},{9,1},{17,25},{25,17},{2,10},{10... | collective-permute-start | bytes 786440 | tf_op jit(solution)/shard_map/ppermute | solution.py:15
  42.0 10.1 %collective-permute-start.10 = (bf16[1,512,256]{2,1,0:T(8,128)(2,1)S(1)}, bf16[1,512,256]{2,1,0:T(8,128)(2,1)S(1)}, u32[]{:S(2)}, u32[]{:S(2)}) collective-permute-start(bf16[1,512,256]{2,1,0:T(8,128)(2,1)S(1)} %merge.8), channel_id=1, source_target_pairs={{0,2},{1,3},{2,0},{3,1},{4,6},{5,7},{6,4},{7,5},{8,10},{9,11},{10,... | collective-permute-start | bytes 786440 | tf_op jit(solution)/shard_map/ppermute | solution.py:15
  45.6 5.0 %collective-permute-start.14 = (bf16[1,256,256]{2,1,0:T(8,128)(2,1)S(1)}, bf16[1,256,256]{2,1,0:T(8,128)(2,1)S(1)}, u32[]{:S(2)}, u32[]{:S(2)}) collective-permute-start(bf16[1,256,256]{2,1,0:T(8,128)(2,1)S(1)} %get-tuple-element.37), channel_id=1, source_target_pairs={{0,8},{8,0},{16,24},{24,16},{1,9},{9,1},{17,25},{25,17},{2,10},{10... | collective-permute-start | bytes 393224 | tf_op jit(solution)/shard_map/ppermute | solution.py:15
  47.1 5.0 %collective-permute-start.15 = (bf16[1,256,256]{2,1,0:T(8,128)(2,1)S(1)}, bf16[1,256,256]{2,1,0:T(8,128)(2,1)S(1)}, u32[]{:S(2)}, u32[]{:S(2)}) collective-permute-start(bf16[1,256,256]{2,1,0:T(8,128)(2,1)S(1)} %get-tuple-element.38), channel_id=1, source_target_pairs={{0,16},{8,24},{16,0},{24,8},{1,17},{9,25},{17,1},{25,9},{2,18},{10... | collective-permute-start | bytes 393224 | tf_op jit(solution)/shard_map/ppermute | solution.py:15
  53.4 18.8 %collective-permute-start.17 = (bf16[256,1024]{1,0:T(8,128)(2,1)S(1)}, bf16[256,1024]{1,0:T(8,128)(2,1)S(1)}, u32[]{:S(2)}, u32[]{:S(2)}) collective-permute-start(bf16[256,1024]{1,0:T(8,128)(2,1)S(1)} %get-tuple-element.40.refs_1_), channel_id=1, source_target_pairs={{0,16},{8,24},{16,0},{24,8},{1,17},{9,25},{17,1},{25,9},{2,18},{10... | collective-permute-start | bytes 1572872 | tf_op jit(solution)/shard_map/ppermute | solution.py:15
  55.0 17.2 %collective-permute-start.16 = (bf16[256,1024]{1,0:T(8,128)(2,1)S(1)}, bf16[256,1024]{1,0:T(8,128)(2,1)S(1)}, u32[]{:S(2)}, u32[]{:S(2)}) collective-permute-start(bf16[256,1024]{1,0:T(8,128)(2,1)S(1)} %get-tuple-element.40.refs_1_), channel_id=1, source_target_pairs={{0,8},{8,0},{16,24},{24,16},{1,9},{9,1},{17,25},{25,17},{2,10},{10... | collective-permute-start | bytes 1572872 | tf_op jit(solution)/shard_map/ppermute | solution.py:15
  55.5 10.9 %collective-permute-start.18 = (bf16[2,256,256]{2,1,0:T(8,128)(2,1)S(1)}, bf16[2,256,256]{2,1,0:T(8,128)(2,1)S(1)}, u32[]{:S(2)}, u32[]{:S(2)}) collective-permute-start(bf16[2,256,256]{2,1,0:T(8,128)(2,1)S(1)} %get-tuple-element.41), channel_id=1, source_target_pairs={{0,4},{1,5},{2,6},{3,7},{4,0},{5,1},{6,2},{7,3},{8,12},{9,13},{10,... | collective-permute-start | bytes 786440 | tf_op jit(solution)/shard_map/ppermute | solution.py:15
  68.0 11.7 %collective-permute-start.22 = (bf16[2,256,256]{2,1,0:T(8,128)(2,1)S(1)}, bf16[2,256,256]{2,1,0:T(8,128)(2,1)S(1)}, u32[]{:S(2)}, u32[]{:S(2)}) collective-permute-start(bf16[2,256,256]{2,1,0:T(8,128)(2,1)S(1)} %amplitude.1.refs_2_), channel_id=1, source_target_pairs={{0,2},{1,3},{2,0},{3,1},{4,6},{5,7},{6,4},{7,5},{8,10},{9,11},{10,... | collective-permute-start | bytes 786440 | tf_op jit(solution)/shard_map/ppermute | solution.py:15
  68.8 13.3 %collective-permute-start.21 = (bf16[2,256,256]{2,1,0:T(8,128)(2,1)S(1)}, bf16[2,256,256]{2,1,0:T(8,128)(2,1)S(1)}, u32[]{:S(2)}, u32[]{:S(2)}) collective-permute-start(bf16[2,256,256]{2,1,0:T(8,128)(2,1)S(1)} %amplitude.1.refs_2_), channel_id=1, source_target_pairs={{0,4},{1,5},{2,6},{3,7},{4,0},{5,1},{6,2},{7,3},{8,12},{9,13},{10,... | collective-permute-start | bytes 786440 | tf_op jit(solution)/shard_map/ppermute | solution.py:15
  72.3 17.0 %collective-permute-start.19 = (bf16[3,256,512]{2,1,0:T(8,128)(2,1)S(1)}, bf16[3,256,512]{2,1,0:T(8,128)(2,1)S(1)}, u32[]{:S(2)}, u32[]{:S(2)}) collective-permute-start(bf16[3,256,512]{2,1,0:T(8,128)(2,1)S(1)} %get-tuple-element.42), channel_id=1, source_target_pairs={{0,8},{8,0},{16,24},{24,16},{1,9},{9,1},{17,25},{25,17},{2,10},{10... | collective-permute-start | bytes 2359304 | tf_op jit(solution)/shard_map/ppermute | solution.py:15
  73.3 16.1 %collective-permute-start.20 = (bf16[3,256,512]{2,1,0:T(8,128)(2,1)S(1)}, bf16[3,256,512]{2,1,0:T(8,128)(2,1)S(1)}, u32[]{:S(2)}, u32[]{:S(2)}) collective-permute-start(bf16[3,256,512]{2,1,0:T(8,128)(2,1)S(1)} %get-tuple-element.43), channel_id=1, source_target_pairs={{0,16},{8,24},{16,0},{24,8},{1,17},{9,25},{17,1},{25,9},{2,18},{10... | collective-permute-start | bytes 2359304 | tf_op jit(solution)/shard_map/ppermute | solution.py:15
  83.6 9.3 %collective-permute-start.26 = (bf16[2,256,256]{2,1,0:T(8,128)(2,1)S(1)}, bf16[2,256,256]{2,1,0:T(8,128)(2,1)S(1)}, u32[]{:S(2)}, u32[]{:S(2)}) collective-permute-start(bf16[2,256,256]{2,1,0:T(8,128)(2,1)S(1)} %get-tuple-element.45.refs_10_), channel_id=1, source_target_pairs={{0,2},{1,3},{2,0},{3,1},{4,6},{5,7},{6,4},{7,5},{8,10},{9,11},{10,... | collective-permute-start | bytes 786440 | tf_op jit(solution)/shard_map/ppermute | solution.py:15
  (20 other events, 246.6 us)

commit v4 on v3

--- a/solution.py
+++ b/solution.py
@@ -25,11 +25,11 @@
 
 
 def prepare_kernel(n_occ, chunks, src_count, src_hbm, x_ref, *refs):
-    low_a, high_a, src_b, src_t, theirs, mine = *refs[:4], refs[4 : 4 + chunks], refs[4 + chunks : -4]
+    quarters, src_t, theirs, mine = refs[:4], refs[4], refs[5 : 5 + chunks], refs[5 + chunks : -4]
     arriving, turned, src_ref, arrived = refs[-4:]
     count, step, _, width = arriving.shape
     per_half = src_count // 2
-    piece = min(step, src_b.shape[0])
+    piece = min(step, quarters[0].shape[0])
     copies = [
         pltpu.make_async_copy(x_ref.at[pl.ds(r * step, step)], arriving.at[r], arrived.at[r]) for r in range(count)
     ]
@@ -47,8 +47,8 @@
         for s in range(src_count):
             block = turned[src_ref[s ^ mask]]
             for first in range(0, step, piece):
-                second, place = divmod(r * step + first, src_b.shape[0])
-                out, column = (src_b, s) if second else (low_a if s < per_half else high_a, s % per_half)
+                number, place = divmod(r * step + first, quarters[0].shape[0])
+                out, column = quarters[2 * number + s // per_half], s % per_half
                 out[pl.ds(place, piece), pl.ds(column * width, width)] = block[first : first + piece]
             src_t[pl.ds(s * width, width), rows] = block.T
         for outs, side in ((theirs, 1 - core), (mine, core)):
@@ -63,7 +63,7 @@
     step = min(rows, 128)
     half = src_count * width // 2
     blocks = [(n_occ, rows, width)] * (2 * chunks)
-    shapes = [(rows // 2, half)] * 2 + [(rows // 2, 2 * half)] + [(src_count * width, rows)] + blocks
+    shapes = [(rows // 2, half)] * 4 + [(src_count * width, rows)] + blocks
     vmem = pl.BlockSpec(memory_space=pltpu.VMEM)
     return pl.pallas_call(
         functools.partial(prepare_kernel, n_occ, chunks, src_count),
@@ -113,16 +113,19 @@
     return total
 
 
-def amplitude(total, chunk, chunks, vir, occ, offset, src):
-    owner, core = lax.axis_index("occ"), lax.axis_index("aux") % 2
+def occupied(chunk, chunks):
+    return (lax.axis_index("occ") * 2 + lax.axis_index("aux") % 2) * chunks + chunk
+
+
+def amplitude(total, place, vir, occ, offset, src):
     first = offset[0]
     row = jnp.broadcast_to(vir[...], total.shape)
-    denom = row.T + row - occ[first + (owner * 2 + core) * chunks + chunk] - occ[first + src[chip_mask(src.shape[0])]]
+    denom = row.T + row - occ[first + place()] - occ[first + src[chip_mask(src.shape[0])]]
     scaled = (total / denom).astype(BF16).astype(F32)
     return 2.0 * scaled - scaled.T
 
 
-def merge(outputs, energies=None, after=(), through=()):
+def merge(outputs, energies=None, chunk=0, chunks=1, after=(), through=()):
     arrays, places = [], {}
 
     def spot(array):
@@ -142,7 +145,7 @@
             for j, terms in enumerate(plan):
                 total = add_terms(refs, terms)
                 if energies is not None:
-                    total = amplitude(total, j, len(plan), *refs[len(arrays) : n_in])
+                    total = amplitude(total, functools.partial(occupied, chunk + j, chunks), *refs[len(arrays) : n_in])
                 out[j] = total.astype(BF16)
 
     anywhere = pl.BlockSpec(memory_space=pl.ANY)
@@ -222,86 +225,95 @@
         return arrived
 
 
-def source_block(arrays, spots, k):
-    low_a, low_b, high_a, high_b = (take(arrays, spot) for spot in spots[4 * k : 4 * k + 4])
-    halves = [jnp.concatenate(pair_of, axis=1) for pair_of in ((low_a, high_a), (low_b, high_b))]
-    return jnp.concatenate(halves, axis=0)
-
-
-def gather_amplitudes(amps, chunks, gathered):
-    my_core = lax.axis_index("aux") % 2
-    steps = len(amps) // 2
+def gather_amplitudes(refs, keys, spots, chunks, gathered):
     width = gathered.shape[2]
-    for spot, amp in enumerate(amps):
-        core, s = divmod(spot, steps)
-        for chunk in range(chunks):
-            row = (my_core if core == 0 else 1 - my_core) * chunks + chunk
-            gathered[row, pl.ds(s * width, width), :] = amp[chunk]
-
-
-def density_first_kernel(n_occ, chunks, spots, count, *refs):
-    arrays, amps = refs[:count], refs[count:-2]
-    out, gathered = refs[-2:]
-    depth, width = gathered.shape[1:]
-    gather_amplitudes(amps, chunks, gathered)
-    for k in range(n_occ):
-        sources = source_block(arrays, spots, k)[:, :depth]
-        for i in range(2 * chunks):
-            out[k, :, pl.ds(i * width, width)] = jnp.dot(sources, gathered[i], preferred_element_type=F32)
-
-
-def density_last_kernel(n_occ, chunks, spots, count, *refs):
-    arrays, amps, first = refs[:count], refs[count:-3], refs[-3]
-    out, gathered = refs[-2:]
+    for (core, step, chunk), spot in zip(keys, spots, strict=True):
+        gathered[core * chunks + chunk, pl.ds(step * width, width), :] = take(refs, spot)
+
+
+def density_first_kernel(plan, *refs):
+    keys, spots, amp_keys = plan
+    arrays, (out, gathered) = refs[:-2], refs[-2:]
+    chunks, depth, width = gathered.shape
+    gather_amplitudes(arrays, amp_keys, spots[2 * len(keys) :], chunks, gathered)
+    rows = out.shape[1] // 2
+    for place, (k, part) in enumerate(keys):
+        halves = [take(arrays, spot) for spot in spots[2 * place : 2 * place + 2]]
+        sources = jnp.concatenate(halves, axis=1)[:, :depth]
+        for i in range(chunks):
+            total = jnp.dot(sources, gathered[i], preferred_element_type=F32)
+            out[k, pl.ds(part * rows, rows), pl.ds(i * width, width)] = total
+
+
+def density_last_kernel(chunks, plan, early, *refs):
+    keys, spots, amp_keys = plan
+    arrays, first, (out, gathered, turned) = refs[:-4], refs[-4], refs[-3:]
     step = pl.program_id(0)
     depth, width = gathered.shape[1:]
+    rows = out.shape[0] // 2
+    my_core = lax.axis_index("aux") % 2
 
     @pl.when(step == 0)
     def _():
-        gather_amplitudes(amps, chunks, gathered)
-
-    for k in range(n_occ):
+        gather_amplitudes(arrays, amp_keys, spots[2 * len(keys) :], chunks, gathered)
+
+    for place, (k, part) in enumerate(keys):
 
         @pl.when(step == k)
-        def _(k=k):
-            sources = source_block(arrays, spots, k)[:, -depth:]
-            parts = []
-            for i in range(2 * chunks):
-                total = jnp.dot(sources, gathered[i], preferred_element_type=F32)
-                parts.append((total + first[k, :, i * width : (i + 1) * width]).astype(BF16))
-            out[...] = jnp.swapaxes(jnp.stack(parts, axis=0), 0, 1)
+        def _(place=place, k=k, part=part):
+            halves = [take(arrays, spot) for spot in spots[2 * place : 2 * place + 2]]
+            sources = jnp.concatenate(halves, axis=1)
+            mine = slice(part * rows, (part + 1) * rows)
+            for core in range(2):
+                for chunk in range(chunks):
+                    done = depth - width if core == 0 and (k, part) in early else 0
+                    amps = gathered[core * chunks + chunk, done:]
+                    total = jnp.dot(sources[:, done:], amps, preferred_element_type=F32)
+                    if done:
+                        total += first[k, mine, chunk * width : (chunk + 1) * width]
+                    turned[(my_core if core == 0 else 1 - my_core) * chunks + chunk] = total.astype(BF16)
+            out[mine] = jnp.swapaxes(turned[...], 0, 1)
+
+
+def density_plan(sources, amps):
+    values = [v for halves in sources.values() for v in halves]
+    arrays, spots = spotted(values + list(amps.values()))
+    rows, columns = cut(*values[0])
+    return arrays, (list(sources), spots, list(amps)), 2 * rows, 2 * columns
 
 
 def density_first(sources, amps, n_occ, chunks):
-    arrays, spots = spotted([v for block in sources for v in block])
-    rows, width = 2 * cut(*sources[0][0])[0], amps[0][0].shape[2]
+    arrays, plan, rows, columns = density_plan(sources, amps)
+    width = cut(*amps[0, 0, 0])[1]
     vmem = pl.BlockSpec(memory_space=pltpu.VMEM)
-    early = [amp for by_core in amps for amp in by_core]
     return pl.pallas_call(
-        functools.partial(density_first_kernel, n_occ, chunks, spots, len(arrays)),
-        in_specs=[vmem] * (len(arrays) + len(early)),
+        functools.partial(density_first_kernel, plan),
+        in_specs=[vmem] * len(arrays),
         out_specs=vmem,
-        scratch_shapes=[pltpu.VMEM((2 * chunks, len(amps[0]) * width, width), BF16)],
-        out_shape=jax.ShapeDtypeStruct((n_occ, rows, 2 * chunks * width), F32),
+        scratch_shapes=[pltpu.VMEM((chunks, columns - width, width), BF16)],
+        out_shape=jax.ShapeDtypeStruct((n_occ, rows, chunks * width), F32),
         compiler_params=pltpu.CompilerParams(vmem_limit_bytes=20 * MIB),
         name="density_first",
-    )(*arrays, *early)
-
-
-def density_last(sources, late, first, n_occ, chunks):
-    arrays, spots = spotted([v for block in sources for v in block])
-    rows, width = 2 * cut(*sources[0][0])[0], late[0].shape[2]
+    )(*arrays)
+
+
+def density_last(sources, early, amps, first, n_occ, chunks):
+    arrays, plan, rows, columns = density_plan(sources, amps)
+    width = cut(*amps[0, 0, 0])[1]
     vmem = pl.BlockSpec(memory_space=pltpu.VMEM)
     return pl.pallas_call(
-        functools.partial(density_last_kernel, n_occ, chunks, spots, len(arrays)),
+        functools.partial(density_last_kernel, chunks, plan, early),
         grid=(n_occ,),
-        in_specs=[vmem] * (len(arrays) + len(late) + 1),
+        in_specs=[vmem] * (len(arrays) + 1),
         out_specs=pl.BlockSpec((rows, 2 * chunks, width), lambda k: (k ^ lax.axis_index("occ"), 0, 0)),
-        scratch_shapes=[pltpu.VMEM((2 * chunks, width, width), BF16)],
+        scratch_shapes=[
+            pltpu.VMEM((2 * chunks, columns, width), BF16),
+            pltpu.VMEM((2 * chunks, rows // 2, width), BF16),
+        ],
         out_shape=jax.ShapeDtypeStruct((n_occ * rows, 2 * chunks, width), BF16),
         compiler_params=pltpu.CompilerParams(vmem_limit_bytes=20 * MIB),
         name="density_last",
-    )(*arrays, *late, first)
+    )(*arrays, first)
 
 
 def solution(mesh):
@@ -315,37 +327,33 @@
         owned = occ_count // n_occ
         chunks = owned // 2
         near, far = 2, 4
-        low_a, high_a, src_b, src_t, *ints = prepare(integrals, src_occ, n_occ, chunks)
+        low_a, high_a, low_b, high_b, src_t, *ints = prepare(integrals, src_occ, n_occ, chunks)
         theirs, mine = ints[:chunks], ints[chunks:]
-        columns = low_a.shape[1]
-        part_low, part_high = (slice(None), slice(0, columns)), (slice(None), slice(columns, 2 * columns))
-        streams = [
-            (occ_bits, {0: (low_a, ()), occ_bits[0]: (swap(low_a, "occ", n_occ, occ_bits[0]), ())}),
-            (occ_bits[::-1], {0: (high_a, ()), occ_bits[-1]: (swap(high_a, "occ", n_occ, occ_bits[-1]), ())}),
-            (occ_bits, {0: (src_b, part_low)}),
-            (occ_bits[::-1], {0: (src_b, part_high)}),
-        ]
-        ahead = [streams[h][1][bit][0] for h, bit in ((0, occ_bits[0]), (1, occ_bits[-1]))]
-
-        def leaving_sources(step):
+        orders = [occ_bits, occ_bits[::-1]] * 2
+        streams = [{0: (value, ())} for value in (low_a, high_a, low_b, high_b)]
+        for order, have in zip(orders[:2], streams[:2], strict=True):
+            have[order[0]] = (swap(have[0][0], "occ", n_occ, order[0]), ())
+        ahead = [have[order[0]][0] for order, have in zip(orders[:2], streams[:2], strict=True)]
+
+        def leaving_sources():
             groups = {}
-            for number, (order, have) in enumerate(streams):
+            for number, (order, have) in enumerate(zip(orders, streams, strict=True)):
                 blocks = [0]
-                for bit in order[:step]:
+                for bit in order:
+                    wanted = [(number, k) for k in blocks if k in have and k | bit not in have]
+                    if wanted:
+                        groups.setdefault(bit, []).extend(wanted)
                     blocks = blocks + [k | bit for k in blocks]
-                wanted = [(number, k) for k in blocks if k | order[step] not in have]
-                groups.setdefault(order[step], []).extend(wanted)
             return groups
 
         def pack_sources(groups, after=()):
-            return pack([[streams[number][1][k] for number, k in group] for group in groups.values()], after)
+            return pack([[streams[number][k] for number, k in group] for group in groups.values()], after)
 
         def send_sources(groups, packs):
             arrived = [swap(packed, "occ", n_occ, bit) for bit, packed in zip(groups, packs, strict=True)]
             for (bit, group), array in zip(groups.items(), arrived, strict=True):
                 for j, (number, k) in enumerate(group):
-                    streams[number][1][k | bit] = (array, (j,))
-            return arrived
+                    streams[number][k | bit] = (array, (j,))
 
         src_other = swap(src_t, "aux", n_aux, 1)
         other = [None] * chunks
@@ -371,6 +379,8 @@
         sent_x = product(0, 2, [(0, k) for k in odd], [near_sent])
         sent_y = product(0, 2, [(1, k) for k in back], [near_sent, *ahead])
         near_got.append(swap(product(1, 4, near_pieces[1], [sent_x, sent_y]), "aux", n_aux, near))
+        groups = leaving_sources()
+        packs = pack_sources(groups)
         held = [vir_energy, near_got[0]]
         kept_x = product(0, 2, [(0, k) for k in even], held)
         kept_y = product(0, 2, [(1, k) for k in front], held)
@@ -399,43 +409,50 @@
         sent_x, sent_y = merge([unit_x.plan(), unit_y.plan()], after=[])
         got_x, got_y = unit_x.send(sent_x), unit_y.send(sent_y)
 
+        (sent_0,) = merge([[rows_of(terms_0, small, small)]])
+        got_0 = swap(sent_0, "aux", n_aux, far)
+        terms_0 = rows_of(terms_0, 0, small) + [(got_0, 0, 0, small)]
+
         while unit_x.bits:
             sent_x, sent_y = merge([unit_x.plan(), unit_y.plan()])
             got_x, got_y = unit_x.send(sent_x), unit_y.send(sent_y)
-        sent, src_b = merge(
-            [[rows_of(terms_0, small, small), unit_y.terms[0]]],
-            after=[got_x],
-            through=[src_b],
-        )
-        got = swap(sent, "aux", n_aux, far)
-        terms_0 = rows_of(terms_0, 0, small) + [(got, 0, 0, small)]
-        terms_1 = unit_x.terms[0] + [(got, 1, 0, small)]
-        for number, part in ((2, part_low), (3, part_high)):
-            streams[number][1][0] = (src_b, part)
-        for bit in {occ_bits[0], occ_bits[-1]}:
-            arrived = swap(src_b, "occ", n_occ, bit)
-            streams[2][1][bit], streams[3][1][bit] = (arrived, part_low), (arrived, part_high)
-        for step in range(len(occ_bits)):
-            groups = leaving_sources(step)
-            if any(groups.values()):
-                last = send_sources(groups, pack_sources(groups, [got]))
-
+        sent_1, *packs = merge([[unit_y.terms[0]]], after=[got_x, sent_0], through=packs)
+        got_1 = swap(sent_1, "aux", n_aux, far)
+        terms_1 = unit_x.terms[0] + [(got_1, 0, 0, small)]
+
+        send_sources(groups, packs)
+        while groups := leaving_sources():
+            soon = [dict(have) for have in streams]
+            send_sources(groups, pack_sources(groups))
+        early, late_rows = [], []
+        for k in range(n_occ):
+            for part in range(2):
+                (early if all(k in soon[2 * part + h] for h in range(2)) else late_rows).append((k, part))
+
+        energies = [vir_energy, eps_occ, occ_offset, src_occ]
         sums = [terms_0, terms_1]
         for bit in range(2, n_chip.bit_length() - 1):
             (sent,) = merge([sums])
             got = swap(sent, "aux", n_aux, 2 << bit)
             sums = [[(sent, c, 0, small), (got, c, 0, small)] for c in range(chunks)]
-        (amp,) = merge([sums], energies=[vir_energy, eps_occ, occ_offset, src_occ])
+        (amp,) = merge([sums], energies=energies, chunks=chunks)
         far_amp, near_amp = swap(amp, "aux", n_aux, far), swap(amp, "aux", n_aux, near)
-        far_amp, near_amp, amp = merge([], through=[far_amp, near_amp, amp])
         both_amp = swap(far_amp, "aux", n_aux, near)
-        amps = [amp, far_amp, near_amp]
-        other = [swap(v, "aux", n_aux, 1) for v in amps]
-        sources = [[streams[number][1][k] for number in (0, 2, 1, 3)] for k in range(n_occ)]
-        first = density_first(sources, [amps, other], n_occ, chunks)
-        (both_amp,) = merge([], after=[first], through=[both_amp])
-        late = [both_amp, swap(both_amp, "aux", n_aux, 1)]
-        return density_last(sources, late, first, n_occ, chunks)
+        amps = {
+            (0, step, c): (value, (c,))
+            for step, value in enumerate([amp, far_amp, near_amp, both_amp])
+            for c in range(chunks)
+        }
+        sources = {(k, part): [streams[2 * part + h][k] for h in range(2)] for k in range(n_occ) for part in range(2)}
+        known = {key: value for key, value in amps.items() if key[1] < src_count - 1}
+        first = density_first({key: sources[key] for key in early}, known, n_occ, chunks)
+        last_sources = [streams[2 * part + h][k] for k, part in late_rows for h in range(2)]
+        own = list(amps)
+        (packed,) = pack([[amps[key] for key in own]], [first, *spotted(last_sources)[0]])
+        arrived = swap(packed, "aux", n_aux, 1)
+        for j, (_, step, c) in enumerate(own):
+            amps[1, step, c] = (arrived, (j,))
+        return density_last(sources, set(early), amps, first, n_occ, chunks)
 
     in_specs = (P(("aux", "occ"), None, None), P(), P(), P(), P(), P())
     out_specs = P("aux", "occ", None)

time: 99.1 us -> 96.4 us (0.973)
  waiting for transfers between devices: 35.5 us -> 29.2 us
  starting transfers between devices: 32.2 us -> 34.9 us
    ppermute x28 -> x26, waiting for transfers between devices: 35.5 us -> 29.2 us  [swap(): return lax.ppermute(value, axis, [(d, d ^ mask) for d in range(size)])]
    ppermute x28 -> x26, starting transfers between devices: 32.2 us -> 34.9 us  [swap(): return lax.ppermute(value, axis, [(d, d ^ mask) for d in range(size)])]
    pallas_call x8 -> x7, Pallas kernels: 7.7 us -> 8.57 us  [merge(): pl.pallas_call(kernel, in_specs=[vmem] * len(arrays) + [vmem, smem, smem,...]
  transfers between devices with their start and end apart: 28 -> 26, of which waited for: 16 -> 16; matrix products, arithmetic and copies ran while one was open for 1% -> 1% of each run, Pallas kernels for 19% -> 19%
where the time goes in v4:
time: 96.4 us; the launch traced here: 95.9 us
  starting transfers between devices  34.9 us (36%)
  waiting for transfers between devices  29.2 us (30%)
  Pallas kernels  28.3 us (29%)
  local copies, waits for them, and re-layouts  2.08 us (2%)
  between operations  1.56 us (2%)
    ppermute x26, starting transfers between devices, swap(): return lax.ppermute(value, axis, [(d, d ^ mask) for d in range(size)])  34.9 us
    ppermute x26, waiting for transfers between devices, swap(): return lax.ppermute(value, axis, [(d, d ^ mask) for d in range(size)])  29.2 us
    pallas_call x7, Pallas kernels, pair(): pl.pallas_call(functools.partial(pair_kernel, pieces), in_specs=[vmem] *...  8.72 us
    pallas_call x7, Pallas kernels, merge(): pl.pallas_call(kernel, in_specs=[vmem] * len(arrays) + [vmem, smem, smem,...  8.57 us
    pallas_call x1, Pallas kernels, density_last(): pl.pallas_call(functools.partial(density_last_kernel, chunks, plan, early...  5.95 us
    pallas_call x1, Pallas kernels, prepare(): pl.pallas_call(functools.partial(prepare_kernel, n_occ, chunks, src_count...  3.18 us
  transfers between devices with their start and end apart: 26, of which 16 were waited for; matrix products, arithmetic and copies ran while one was open for 1% of the time, Pallas kernels for 19%

profile of v4, /device:TPU:0, one launch (start us, length us, event | category | flops | bytes accessed | tf_op | source)
XLA Modules:
  0.0 95.9 jit_solution(18251785536556332649)
XLA Ops:
  0.0 3.2 %prepare.1 = (bf16[256,512]{1,0:T(8,128)(2,1)S(1)}, bf16[256,512]{1,0:T(8,128)(2,1)S(1)}, bf16[256,512]{1,0:T(8,128)(2,1)S(1)}, bf16[256,512]{1,0:T(8,128)(2,1)S...) custom-call(s32[4]{0:T(128)} %refs_13_.1, ...), custom_call_target="tpu_custom_call" | custom-call | tf_op jit(solution)/shard_map/prepare/pallas_call | solution.py:68
  4.3 2.6 %collective-permute-start = (bf16[256,512]{1,0:T(8,128)(2,1)S(1)}, bf16[256,512]{1,0:T(8,128)(2,1)S(1)}, u32[]{:S(2)}, u32[]{:S(2)}) collective-permute-start(bf16[256,512]{1,0:T(8,128)(2,1)S(1)} %get-tuple-element.27.refs_0_), channel_id=1, source_target_pairs={{0,8},{8,0},{16,24},{24,16},{1,9},{9,1},{17,25},{25,17},{2,10},{10... | collective-permute-start | bytes 786440 | tf_op jit(solution)/shard_map/ppermute | solution.py:15
  6.8 1.5 %collective-permute-start.6 = (bf16[256,512]{1,0:T(8,128)(2,1)S(1)}, bf16[256,512]{1,0:T(8,128)(2,1)S(1)}, u32[]{:S(2)}, u32[]{:S(2)}) collective-permute-start(bf16[256,512]{1,0:T(8,128)(2,1)S(1)} %get-tuple-element.28.refs_4_.refs_1_), channel_id=1, source_target_pairs={{0,16},{8,24},{16,0},{24,8},{1,17},{9,25},{17,1},{25,9},{2,18},{10... | collective-permute-start | bytes 786440 | tf_op jit(solution)/shard_map/ppermute | solution.py:15
  8.4 1.5 %pair.7.refs_0_ = bf16[4,256,256]{2,1,0:T(8,128)(2,1)} custom-call(bf16[1024,512]{1,0:T(8,128)(2,1)S(1)} %get-tuple-element.31.src_own, bf16[1024,512]{1,0:T(8,128)(2,1)S(1)} %collective-permute-done.1.src_other, bf16[4,512,256]{2,1,0:T(8,128)(2,1)S(1)} %get-tuple-element.32.ints_own, bf16[4,512,256]{2,1,0:T(8,128)(2,1)S(1)} %collective-permute-done.2.ints_other), custom_call_target="tpu_custom_call" | custom-call | tf_op jit(solution)/shard_map/pair/pallas_call | solution.py:98
  9.9 2.1 %collective-permute-start.4 = (bf16[4,256,256]{2,1,0:T(8,128)(2,1)}, bf16[4,256,256]{2,1,0:T(8,128)(2,1)}, u32[]{:S(2)}, u32[]{:S(2)}) collective-permute-start(bf16[4,256,256]{2,1,0:T(8,128)(2,1)} %pair.7.refs_0_), channel_id=1, source_target_pairs={{0,2},{1,3},{2,0},{3,1},{4,6},{5,7},{6,4},{7,5},{8,10},{9,11},{10,... | collective-permute-start | bytes 1572872 | tf_op jit(solution)/shard_map/ppermute | solution.py:15
  12.0 1.5 %pair.9.refs_0_ = bf16[2,512,256]{2,1,0:T(8,128)(2,1)} custom-call(bf16[1024,512]{1,0:T(8,128)(2,1)S(1)} %get-tuple-element.31.src_own, bf16[1024,512]{1,0:T(8,128)(2,1)S(1)} %collective-permute-done.1.src_other, bf16[4,512,256]{2,1,0:T(8,128)(2,1)S(1)} %get-tuple-element.34.ints_own, bf16[4,512,256]{2,1,0:T(8,128)(2,1)S(1)} %collective-permute-done.3.ints_other, ...), custom_call_target="tpu_custom_call" | custom-call | tf_op jit(solution)/shard_map/pair/pallas_call | solution.py:98
  13.5 1.6 %collective-permute-start.5 = (bf16[2,512,256]{2,1,0:T(8,128)(2,1)}, bf16[2,512,256]{2,1,0:T(8,128)(2,1)}, u32[]{:S(2)}, u32[]{:S(2)}) collective-permute-start(bf16[2,512,256]{2,1,0:T(8,128)(2,1)} %pair.9.refs_0_), channel_id=1, source_target_pairs={{0,8},{8,0},{16,24},{24,16},{1,9},{9,1},{17,25},{25,17},{2,10},{10... | collective-permute-start | bytes 1572872 | tf_op jit(solution)/shard_map/ppermute | solution.py:15
  16.7 1.5 %collective-permute-start.7 = (bf16[2,512,256]{2,1,0:T(8,128)(2,1)}, bf16[2,512,256]{2,1,0:T(8,128)(2,1)}, u32[]{:S(2)}, u32[]{:S(2)}) collective-permute-start(bf16[2,512,256]{2,1,0:T(8,128)(2,1)} %pair.11.refs_1_), channel_id=1, source_target_pairs={{0,16},{8,24},{16,0},{24,8},{1,17},{9,25},{17,1},{25,9},{2,18},{10... | collective-permute-start | bytes 1572872 | tf_op jit(solution)/shard_map/ppermute | solution.py:15
  18.3 1.5 %pair.13 = bf16[4,256,256]{2,1,0:T(8,128)(2,1)} custom-call(bf16[1024,512]{1,0:T(8,128)(2,1)S(1)} %get-tuple-element.31.src_own, bf16[1024,512]{1,0:T(8,128)(2,1)S(1)} %collective-permute-done.1.src_other, bf16[4,512,256]{2,1,0:T(8,128)(2,1)S(1)} %get-tuple-element.32.ints_own, bf16[4,512,256]{2,1,0:T(8,128)(2,1)S(1)} %collective-permute-done.2.ints_other, ...), custom_call_target="tpu_custom_call" | custom-call | tf_op jit(solution)/shard_map/pair/pallas_call | solution.py:98
  19.8 1.6 %collective-permute-start.8 = (bf16[4,256,256]{2,1,0:T(8,128)(2,1)}, bf16[4,256,256]{2,1,0:T(8,128)(2,1)}, u32[]{:S(2)}, u32[]{:S(2)}) collective-permute-start(bf16[4,256,256]{2,1,0:T(8,128)(2,1)} %pair.13), channel_id=1, source_target_pairs={{0,2},{1,3},{2,0},{3,1},{4,6},{5,7},{6,4},{7,5},{8,10},{9,11},{10,... | collective-permute-start | bytes 1572872 | tf_op jit(solution)/shard_map/ppermute | solution.py:15
  22.8 2.2 %collective-permute-done.4.refs_1_ = bf16[4,256,256]{2,1,0:T(8,128)(2,1)} collective-permute-done((bf16[4,256,256]{2,1,0:T(8,128)(2,1)}, bf16[4,256,256]{2,1,0:T(8,128)(2,1)}, u32[]{:S(2)}, u32[]{:S(2)}) %collective-permute-start.4) | collective-permute-done | bytes 524320 | tf_op jit(solution)/shard_map/ppermute | solution.py:15
  27.7 2.6 %collective-permute-done.7.refs_3_.refs_1_ = bf16[2,512,256]{2,1,0:T(8,128)(2,1)} collective-permute-done((bf16[2,512,256]{2,1,0:T(8,128)(2,1)}, bf16[2,512,256]{2,1,0:T(8,128)(2,1)}, u32[]{:S(2)}, u32[]{:S(2)}) %collective-permute-start.7) | collective-permute-done | bytes 524320 | tf_op jit(solution)/shard_map/ppermute | solution.py:15
  32.3 1.6 %collective-permute-start.13 = (bf16[1,512,256]{2,1,0:T(8,128)(2,1)S(1)}, bf16[1,512,256]{2,1,0:T(8,128)(2,1)S(1)}, u32[]{:S(2)}, u32[]{:S(2)}) collective-permute-start(bf16[1,512,256]{2,1,0:T(8,128)(2,1)S(1)} %get-tuple-element.36.refs_0_), channel_id=1, source_target_pairs={{0,16},{8,24},{16,0},{24,8},{1,17},{9,25},{17,1},{25,9},{2,18},{10... | collective-permute-start | bytes 786440 | tf_op jit(solution)/shard_map/ppermute | solution.py:15
  47.2 1.5 %collective-permute-start.12 = (bf16[1,256,256]{2,1,0:T(8,128)(2,1)S(1)}, bf16[1,256,256]{2,1,0:T(8,128)(2,1)S(1)}, u32[]{:S(2)}, u32[]{:S(2)}) collective-permute-start(bf16[1,256,256]{2,1,0:T(8,128)(2,1)S(1)} %get-tuple-element.40), channel_id=1, source_target_pairs={{0,16},{8,24},{16,0},{24,8},{1,17},{9,25},{17,1},{25,9},{2,18},{10... | collective-permute-start | bytes 393224 | tf_op jit(solution)/shard_map/ppermute | solution.py:15
  55.4 2.6 %collective-permute-start.20 = (bf16[1,256,256]{2,1,0:T(8,128)(2,1)S(1)}, bf16[1,256,256]{2,1,0:T(8,128)(2,1)S(1)}, u32[]{:S(2)}, u32[]{:S(2)}) collective-permute-start(bf16[1,256,256]{2,1,0:T(8,128)(2,1)S(1)} %merge.10.refs_5_), channel_id=1, source_target_pairs={{0,4},{1,5},{2,6},{3,7},{4,0},{5,1},{6,2},{7,3},{8,12},{9,13},{10,... | collective-permute-start | bytes 393224 | tf_op jit(solution)/shard_map/ppermute | solution.py:15
  58.9 4.4 %collective-permute-done.20.refs_4_ = bf16[1,256,256]{2,1,0:T(8,128)(2,1)S(1)} collective-permute-done((bf16[1,256,256]{2,1,0:T(8,128)(2,1)S(1)}, bf16[1,256,256]{2,1,0:T(8,128)(2,1)S(1)}, u32[]{:S(2)}, u32[]{:S(2)}) %collective-permute-start.20) | collective-permute-done | bytes 131104 | tf_op jit(solution)/shard_map/ppermute | solution.py:15
  63.4 2.8 %collective-permute-done.21.refs_9_ = bf16[1,256,256]{2,1,0:T(8,128)(2,1)S(1)} collective-permute-done((bf16[1,256,256]{2,1,0:T(8,128)(2,1)S(1)}, bf16[1,256,256]{2,1,0:T(8,128)(2,1)S(1)}, u32[]{:S(2)}, u32[]{:S(2)}) %collective-permute-start.21) | collective-permute-done | bytes 131104 | tf_op jit(solution)/shard_map/ppermute | solution.py:15
  66.2 1.6 %amplitude.1.refs_8_.refs_0_.refs_10_ = bf16[2,256,256]{2,1,0:T(8,128)(2,1)S(1)} custom-call(bf16[2,512,256]{2,1,0:T(8,128)(2,1)S(1)} %pair.8.refs_0_, bf16[2,512,256]{2,1,0:T(8,128)(2,1)} %collective-permute-done.5.refs_1_, bf16[1,512,256]{2,1,0:T(8,128)(2,1)S(1)} %collective-permute-done.13.refs_3_.refs_2_, ...), custom_call_target="tpu_custom_call" | custom-call | tf_op jit(solution)/shard_map/amplitude/pallas_call | solution.py:153
  67.8 7.0 %collective-permute-start.23 = (bf16[2,256,256]{2,1,0:T(8,128)(2,1)S(1)}, bf16[2,256,256]{2,1,0:T(8,128)(2,1)S(1)}, u32[]{:S(2)}, u32[]{:S(2)}) collective-permute-start(bf16[2,256,256]{2,1,0:T(8,128)(2,1)S(1)} %amplitude.1.refs_8_.refs_0_.refs_10_), channel_id=1, source_target_pairs={{0,2},{1,3},{2,0},{3,1},{4,6},{5,7},{6,4},{7,5},{8,10},{9,11},{10,... | collective-permute-start | bytes 786440 | tf_op jit(solution)/shard_map/ppermute | solution.py:15
  74.8 4.5 %collective-permute-done.22.refs_9_.refs_1_.refs_11_ = bf16[2,256,256]{2,1,0:T(8,128)(2,1)S(1)} collective-permute-done((bf16[2,256,256]{2,1,0:T(8,128)(2,1)S(1)}, bf16[2,256,256]{2,1,0:T(8,128)(2,1)S(1)}, u32[]{:S(2)}, u32[]{:S(2)}) %collective-permute-start.22) | collective-permute-done | bytes 262176 | tf_op jit(solution)/shard_map/ppermute | solution.py:15
  82.2 1.6 %density_first.1.refs_4_.refs_15_ = f32[4,512,512]{2,1,0:T(8,128)S(1)} custom-call(bf16[256,512]{1,0:T(8,128)(2,1)S(1)} %copy-done.9, bf16[256,512]{1,0:T(8,128)(2,1)S(1)} %copy-done.11, bf16[256,512]{1,0:T(8,128)(2,1)S(1)} %copy-done.13, bf16[256,512]{1,0:T(8,128)(2,1)S(1)} %copy-done.15, bf16[256,512]{1,0:T(8,128)(2,1)S(1)} %collective-permute-done.refs_1_.refs_4_, ...), custom_call_target="tpu_custom_call" | custom-call | tf_op jit(solution)/shard_map/density_first/pallas_call | solution.py:289
  83.7 1.9 %collective-permute-done.24.refs_3_.refs_13_ = bf16[2,256,256]{2,1,0:T(8,128)(2,1)S(1)} collective-permute-done((bf16[2,256,256]{2,1,0:T(8,128)(2,1)S(1)}, bf16[2,256,256]{2,1,0:T(8,128)(2,1)S(1)}, u32[]{:S(2)}, u32[]{:S(2)}) %collective-permute-start.24) | collective-permute-done | bytes 262176 | tf_op jit(solution)/shard_map/ppermute | solution.py:15
  87.3 2.6 %collective-permute-done.25.refs_14_ = bf16[8,256,256]{2,1,0:T(8,128)(2,1)S(1)} collective-permute-done((bf16[8,256,256]{2,1,0:T(8,128)(2,1)S(1)}, bf16[8,256,256]{2,1,0:T(8,128)(2,1)S(1)}, u32[]{:S(2)}, u32[]{:S(2)}) %collective-permute-start.25) | collective-permute-done | bytes 1048608 | tf_op jit(solution)/shard_map/ppermute | solution.py:15
  90.0 5.9 %density_last.1 = bf16[2048,4,256]{2,1,0:T(4,128)(2,1)} custom-call(bf16[256,512]{1,0:T(8,128)(2,1)S(1)} %copy-done.9, bf16[256,512]{1,0:T(8,128)(2,1)S(1)} %copy-done.11, bf16[256,512]{1,0:T(8,128)(2,1)S(1)} %copy-done.13, bf16[256,512]{1,0:T(8,128)(2,1)S(1)} %copy-done.15, bf16[256,512]{1,0:T(8,128)(2,1)S(1)} %collective-permute-done.refs_1_.refs_4_, ...), custom_call_target="tpu_custom_call" | custom-call | tf_op jit(solution)/shard_map/density_last/pallas_call | solution.py:304
  (85 shorter events, 32.9 us)
Async XLA Ops:
  3.2 5.1 %collective-permute-start.2 = (bf16[4,512,256]{2,1,0:T(8,128)(2,1)S(1)}, bf16[4,512,256]{2,1,0:T(8,128)(2,1)S(1)}, u32[]{:S(2)}, u32[]{:S(2)}) collective-permute-start(bf16[4,512,256]{2,1,0:T(8,128)(2,1)S(1)} %get-tuple-element.33), channel_id=1, source_target_pairs={{0,1},{1,0},{2,3},{3,2},{4,5},{5,4},{6,7},{7,6},{8,9},{9,8},{10,11... | collective-permute-start | bytes 3145736 | tf_op jit(solution)/shard_map/ppermute | solution.py:15
  3.8 8.2 %collective-permute-start.3 = (bf16[4,512,256]{2,1,0:T(8,128)(2,1)S(1)}, bf16[4,512,256]{2,1,0:T(8,128)(2,1)S(1)}, u32[]{:S(2)}, u32[]{:S(2)}) collective-permute-start(bf16[4,512,256]{2,1,0:T(8,128)(2,1)S(1)} %get-tuple-element.35), channel_id=1, source_target_pairs={{0,1},{1,0},{2,3},{3,2},{4,5},{5,4},{6,7},{7,6},{8,9},{9,8},{10,11... | collective-permute-start | bytes 3145736 | tf_op jit(solution)/shard_map/ppermute | solution.py:15
  4.3 10.8 %collective-permute-start = (bf16[256,512]{1,0:T(8,128)(2,1)S(1)}, bf16[256,512]{1,0:T(8,128)(2,1)S(1)}, u32[]{:S(2)}, u32[]{:S(2)}) collective-permute-start(bf16[256,512]{1,0:T(8,128)(2,1)S(1)} %get-tuple-element.27.refs_0_), channel_id=1, source_target_pairs={{0,8},{8,0},{16,24},{24,16},{1,9},{9,1},{17,25},{25,17},{2,10},{10... | collective-permute-start | bytes 786440 | tf_op jit(solution)/shard_map/ppermute | solution.py:15
  6.8 8.4 %collective-permute-start.6 = (bf16[256,512]{1,0:T(8,128)(2,1)S(1)}, bf16[256,512]{1,0:T(8,128)(2,1)S(1)}, u32[]{:S(2)}, u32[]{:S(2)}) collective-permute-start(bf16[256,512]{1,0:T(8,128)(2,1)S(1)} %get-tuple-element.28.refs_4_.refs_1_), channel_id=1, source_target_pairs={{0,16},{8,24},{16,0},{24,8},{1,17},{9,25},{17,1},{25,9},{2,18},{10... | collective-permute-start | bytes 786440 | tf_op jit(solution)/shard_map/ppermute | solution.py:15
  9.9 15.1 %collective-permute-start.4 = (bf16[4,256,256]{2,1,0:T(8,128)(2,1)}, bf16[4,256,256]{2,1,0:T(8,128)(2,1)}, u32[]{:S(2)}, u32[]{:S(2)}) collective-permute-start(bf16[4,256,256]{2,1,0:T(8,128)(2,1)} %pair.7.refs_0_), channel_id=1, source_target_pairs={{0,2},{1,3},{2,0},{3,1},{4,6},{5,7},{6,4},{7,5},{8,10},{9,11},{10,... | collective-permute-start | bytes 1572872 | tf_op jit(solution)/shard_map/ppermute | solution.py:15
  13.5 14.2 %collective-permute-start.5 = (bf16[2,512,256]{2,1,0:T(8,128)(2,1)}, bf16[2,512,256]{2,1,0:T(8,128)(2,1)}, u32[]{:S(2)}, u32[]{:S(2)}) collective-permute-start(bf16[2,512,256]{2,1,0:T(8,128)(2,1)} %pair.9.refs_0_), channel_id=1, source_target_pairs={{0,8},{8,0},{16,24},{24,16},{1,9},{9,1},{17,25},{25,17},{2,10},{10... | collective-permute-start | bytes 1572872 | tf_op jit(solution)/shard_map/ppermute | solution.py:15
  16.7 13.6 %collective-permute-start.7 = (bf16[2,512,256]{2,1,0:T(8,128)(2,1)}, bf16[2,512,256]{2,1,0:T(8,128)(2,1)}, u32[]{:S(2)}, u32[]{:S(2)}) collective-permute-start(bf16[2,512,256]{2,1,0:T(8,128)(2,1)} %pair.11.refs_1_), channel_id=1, source_target_pairs={{0,16},{8,24},{16,0},{24,8},{1,17},{9,25},{17,1},{25,9},{2,18},{10... | collective-permute-start | bytes 1572872 | tf_op jit(solution)/shard_map/ppermute | solution.py:15
  19.8 23.6 %collective-permute-start.8 = (bf16[4,256,256]{2,1,0:T(8,128)(2,1)}, bf16[4,256,256]{2,1,0:T(8,128)(2,1)}, u32[]{:S(2)}, u32[]{:S(2)}) collective-permute-start(bf16[4,256,256]{2,1,0:T(8,128)(2,1)} %pair.13), channel_id=1, source_target_pairs={{0,2},{1,3},{2,0},{3,1},{4,6},{5,7},{6,4},{7,5},{8,10},{9,11},{10,... | collective-permute-start | bytes 1572872 | tf_op jit(solution)/shard_map/ppermute | solution.py:15
  31.7 8.0 %collective-permute-start.14 = (bf16[1,512,256]{2,1,0:T(8,128)(2,1)S(1)}, bf16[1,512,256]{2,1,0:T(8,128)(2,1)S(1)}, u32[]{:S(2)}, u32[]{:S(2)}) collective-permute-start(bf16[1,512,256]{2,1,0:T(8,128)(2,1)S(1)} %get-tuple-element.41), channel_id=1, source_target_pairs={{0,8},{8,0},{16,24},{24,16},{1,9},{9,1},{17,25},{25,17},{2,10},{10... | collective-permute-start | bytes 786440 | tf_op jit(solution)/shard_map/ppermute | solution.py:15
  32.3 8.7 %collective-permute-start.13 = (bf16[1,512,256]{2,1,0:T(8,128)(2,1)S(1)}, bf16[1,512,256]{2,1,0:T(8,128)(2,1)S(1)}, u32[]{:S(2)}, u32[]{:S(2)}) collective-permute-start(bf16[1,512,256]{2,1,0:T(8,128)(2,1)S(1)} %get-tuple-element.36.refs_0_), channel_id=1, source_target_pairs={{0,16},{8,24},{16,0},{24,8},{1,17},{9,25},{17,1},{25,9},{2,18},{10... | collective-permute-start | bytes 786440 | tf_op jit(solution)/shard_map/ppermute | solution.py:15
  36.3 8.3 %collective-permute-start.9 = (bf16[2,256,256]{2,1,0:T(8,128)(2,1)S(1)}, bf16[2,256,256]{2,1,0:T(8,128)(2,1)S(1)}, u32[]{:S(2)}, u32[]{:S(2)}) collective-permute-start(bf16[2,256,256]{2,1,0:T(8,128)(2,1)S(1)} %get-tuple-element.37), channel_id=1, source_target_pairs={{0,16},{8,24},{16,0},{24,8},{1,17},{9,25},{17,1},{25,9},{2,18},{10... | collective-permute-start | bytes 786440 | tf_op jit(solution)/shard_map/ppermute | solution.py:15
  36.9 7.7 %collective-permute-start.10 = (bf16[2,256,256]{2,1,0:T(8,128)(2,1)S(1)}, bf16[2,256,256]{2,1,0:T(8,128)(2,1)S(1)}, u32[]{:S(2)}, u32[]{:S(2)}) collective-permute-start(bf16[2,256,256]{2,1,0:T(8,128)(2,1)S(1)} %get-tuple-element.38), channel_id=1, source_target_pairs={{0,8},{8,0},{16,24},{24,16},{1,9},{9,1},{17,25},{25,17},{2,10},{10... | collective-permute-start | bytes 786440 | tf_op jit(solution)/shard_map/ppermute | solution.py:15
  42.1 6.8 %collective-permute-start.15 = (bf16[1,512,256]{2,1,0:T(8,128)(2,1)S(1)}, bf16[1,512,256]{2,1,0:T(8,128)(2,1)S(1)}, u32[]{:S(2)}, u32[]{:S(2)}) collective-permute-start(bf16[1,512,256]{2,1,0:T(8,128)(2,1)S(1)} %merge.9), channel_id=1, source_target_pairs={{0,2},{1,3},{2,0},{3,1},{4,6},{5,7},{6,4},{7,5},{8,10},{9,11},{10,... | collective-permute-start | bytes 786440 | tf_op jit(solution)/shard_map/ppermute | solution.py:15
  45.7 5.0 %collective-permute-start.11 = (bf16[1,256,256]{2,1,0:T(8,128)(2,1)S(1)}, bf16[1,256,256]{2,1,0:T(8,128)(2,1)S(1)}, u32[]{:S(2)}, u32[]{:S(2)}) collective-permute-start(bf16[1,256,256]{2,1,0:T(8,128)(2,1)S(1)} %get-tuple-element.39), channel_id=1, source_target_pairs={{0,8},{8,0},{16,24},{24,16},{1,9},{9,1},{17,25},{25,17},{2,10},{10... | collective-permute-start | bytes 393224 | tf_op jit(solution)/shard_map/ppermute | solution.py:15
  47.2 5.0 %collective-permute-start.12 = (bf16[1,256,256]{2,1,0:T(8,128)(2,1)S(1)}, bf16[1,256,256]{2,1,0:T(8,128)(2,1)S(1)}, u32[]{:S(2)}, u32[]{:S(2)}) collective-permute-start(bf16[1,256,256]{2,1,0:T(8,128)(2,1)S(1)} %get-tuple-element.40), channel_id=1, source_target_pairs={{0,16},{8,24},{16,0},{24,8},{1,17},{9,25},{17,1},{25,9},{2,18},{10... | collective-permute-start | bytes 393224 | tf_op jit(solution)/shard_map/ppermute | solution.py:15
  53.3 26.0 %collective-permute-start.16 = (bf16[4,256,512]{2,1,0:T(8,128)(2,1)S(1)}, bf16[4,256,512]{2,1,0:T(8,128)(2,1)S(1)}, u32[]{:S(2)}, u32[]{:S(2)}) collective-permute-start(bf16[4,256,512]{2,1,0:T(8,128)(2,1)S(1)} %get-tuple-element.44), channel_id=1, source_target_pairs={{0,8},{8,0},{16,24},{24,16},{1,9},{9,1},{17,25},{25,17},{2,10},{10... | collective-permute-start | bytes 3145736 | tf_op jit(solution)/shard_map/ppermute | solution.py:15
  54.0 25.3 %collective-permute-start.17 = (bf16[4,256,512]{2,1,0:T(8,128)(2,1)S(1)}, bf16[4,256,512]{2,1,0:T(8,128)(2,1)S(1)}, u32[]{:S(2)}, u32[]{:S(2)}) collective-permute-start(bf16[4,256,512]{2,1,0:T(8,128)(2,1)S(1)} %get-tuple-element.45), channel_id=1, source_target_pairs={{0,16},{8,24},{16,0},{24,8},{1,17},{9,25},{17,1},{25,9},{2,18},{10... | collective-permute-start | bytes 3145736 | tf_op jit(solution)/shard_map/ppermute | solution.py:15
  55.4 8.0 %collective-permute-start.20 = (bf16[1,256,256]{2,1,0:T(8,128)(2,1)S(1)}, bf16[1,256,256]{2,1,0:T(8,128)(2,1)S(1)}, u32[]{:S(2)}, u32[]{:S(2)}) collective-permute-start(bf16[1,256,256]{2,1,0:T(8,128)(2,1)S(1)} %merge.10.refs_5_), channel_id=1, source_target_pairs={{0,4},{1,5},{2,6},{3,7},{4,0},{5,1},{6,2},{7,3},{8,12},{9,13},{10,... | collective-permute-start | bytes 393224 | tf_op jit(solution)/shard_map/ppermute | solution.py:15
  58.0 8.2 %collective-permute-start.21 = (bf16[1,256,256]{2,1,0:T(8,128)(2,1)S(1)}, bf16[1,256,256]{2,1,0:T(8,128)(2,1)S(1)}, u32[]{:S(2)}, u32[]{:S(2)}) collective-permute-start(bf16[1,256,256]{2,1,0:T(8,128)(2,1)S(1)} %get-tuple-element.48), channel_id=1, source_target_pairs={{0,4},{1,5},{2,6},{3,7},{4,0},{5,1},{6,2},{7,3},{8,12},{9,13},{10,... | collective-permute-start | bytes 393224 | tf_op jit(solution)/shard_map/ppermute | solution.py:15
  67.8 11.5 %collective-permute-start.22 = (bf16[2,256,256]{2,1,0:T(8,128)(2,1)S(1)}, bf16[2,256,256]{2,1,0:T(8,128)(2,1)S(1)}, u32[]{:S(2)}, u32[]{:S(2)}) collective-permute-start(bf16[2,256,256]{2,1,0:T(8,128)(2,1)S(1)} %amplitude.1.refs_8_.refs_0_.refs_10_), channel_id=1, source_target_pairs={{0,4},{1,5},{2,6},{3,7},{4,0},{5,1},{6,2},{7,3},{8,12},{9,13},{10,... | collective-permute-start | bytes 786440 | tf_op jit(solution)/shard_map/ppermute | solution.py:15
  67.8 14.3 %collective-permute-start.23 = (bf16[2,256,256]{2,1,0:T(8,128)(2,1)S(1)}, bf16[2,256,256]{2,1,0:T(8,128)(2,1)S(1)}, u32[]{:S(2)}, u32[]{:S(2)}) collective-permute-start(bf16[2,256,256]{2,1,0:T(8,128)(2,1)S(1)} %amplitude.1.refs_8_.refs_0_.refs_10_), channel_id=1, source_target_pairs={{0,2},{1,3},{2,0},{3,1},{4,6},{5,7},{6,4},{7,5},{8,10},{9,11},{10,... | collective-permute-start | bytes 786440 | tf_op jit(solution)/shard_map/ppermute | solution.py:15
  79.3 6.4 %collective-permute-start.24 = (bf16[2,256,256]{2,1,0:T(8,128)(2,1)S(1)}, bf16[2,256,256]{2,1,0:T(8,128)(2,1)S(1)}, u32[]{:S(2)}, u32[]{:S(2)}) collective-permute-start(bf16[2,256,256]{2,1,0:T(8,128)(2,1)S(1)} %collective-permute-done.22.refs_9_.refs_1_.refs_11_), channel_id=1, source_target_pairs={{0,2},{1,3},{2,0},{3,1},{4,6},{5,7},{6,4},{7,5},{8,10},{9,11},{10,... | collective-permute-start | bytes 786440 | tf_op jit(solution)/shard_map/ppermute | solution.py:15
  79.3 6.4 %collective-permute-start.18 = (bf16[1,256,512]{2,1,0:T(8,128)(2,1)S(1)}, bf16[1,256,512]{2,1,0:T(8,128)(2,1)S(1)}, u32[]{:S(2)}, u32[]{:S(2)}) collective-permute-start(bf16[1,256,512]{2,1,0:T(8,128)(2,1)S(1)} %get-tuple-element.46), channel_id=1, source_target_pairs={{0,16},{8,24},{16,0},{24,8},{1,17},{9,25},{17,1},{25,9},{2,18},{10... | collective-permute-start | bytes 786440 | tf_op jit(solution)/shard_map/ppermute | solution.py:15
  80.8 6.4 %collective-permute-start.19 = (bf16[1,256,512]{2,1,0:T(8,128)(2,1)S(1)}, bf16[1,256,512]{2,1,0:T(8,128)(2,1)S(1)}, u32[]{:S(2)}, u32[]{:S(2)}) collective-permute-start(bf16[1,256,512]{2,1,0:T(8,128)(2,1)S(1)} %get-tuple-element.47), channel_id=1, source_target_pairs={{0,8},{8,0},{16,24},{24,16},{1,9},{9,1},{17,25},{25,17},{2,10},{10... | collective-permute-start | bytes 786440 | tf_op jit(solution)/shard_map/ppermute | solution.py:15
  (20 other events, 221.0 us)

commit v5 on v4

--- a/solution.py
+++ b/solution.py
@@ -381,7 +381,7 @@
         near_got.append(swap(product(1, 4, near_pieces[1], [sent_x, sent_y]), "aux", n_aux, near))
         groups = leaving_sources()
         packs = pack_sources(groups)
-        held = [vir_energy, near_got[0]]
+        held = [near_got[0]]
         kept_x = product(0, 2, [(0, k) for k in even], held)
         kept_y = product(0, 2, [(1, k) for k in front], held)
         first_x = {2 * i: [(kept_x, i, 0, tall)] for i in range(half_n)}
@@ -424,10 +424,8 @@
         while groups := leaving_sources():
             soon = [dict(have) for have in streams]
             send_sources(groups, pack_sources(groups))
-        early, late_rows = [], []
-        for k in range(n_occ):
-            for part in range(2):
-                (early if all(k in soon[2 * part + h] for h in range(2)) else late_rows).append((k, part))
+        early = [(k, part) for k in range(n_occ) for part in range(2)]
+        late_rows = []
 
         energies = [vir_energy, eps_occ, occ_offset, src_occ]
         sums = [terms_0, terms_1]

time: 96.4 us -> 94.9 us (0.984)
  Pallas kernels: 28.3 us -> 21.2 us
  local copies, waits for them, and re-layouts: 2.08 us -> 6.83 us
  waiting for transfers between devices: 29.2 us -> 32.2 us
  starting transfers between devices: 34.9 us -> 32.7 us
    pallas_call x7, Pallas kernels: 8.57 us -> 3.39 us  [merge(): pl.pallas_call(kernel, in_specs=[vmem] * len(arrays) + [vmem, smem, smem,...]
    unnamed x36 -> x48, local copies, waits for them, and re-layouts: 1.3 us -> 6.05 us
    pallas_call x7, Pallas kernels: 8.72 us -> 5.49 us  [pair(): pl.pallas_call(functools.partial(pair_kernel, pieces), in_specs=[vmem] *...]
    ppermute x26, waiting for transfers between devices: 29.2 us -> 32.2 us  [swap(): return lax.ppermute(value, axis, [(d, d ^ mask) for d in range(size)])]
    ppermute x26, starting transfers between devices: 34.9 us -> 32.7 us  [swap(): return lax.ppermute(value, axis, [(d, d ^ mask) for d in range(size)])]
    pallas_call x3, Pallas kernels: 0.24 us -> 1.57 us  [pack(): pl.pallas_call(functools.partial(pack_kernel, spots, sizes), in_specs=[vm...]
  transfers between devices with their start and end apart: 26 -> 26, of which waited for: 16 -> 16; matrix products, arithmetic and copies ran while one was open for 1% -> 1% of each run, Pallas kernels for 19% -> 12%
where the time goes in v5:
time: 94.9 us; the launch traced here: 94.5 us
  starting transfers between devices  32.7 us (34%)
  waiting for transfers between devices  32.2 us (34%)
  Pallas kernels  21.2 us (22%)
  local copies, waits for them, and re-layouts  6.83 us (7%)
  between operations  1.59 us (2%)
    ppermute x26, starting transfers between devices, swap(): return lax.ppermute(value, axis, [(d, d ^ mask) for d in range(size)])  32.7 us
    ppermute x26, waiting for transfers between devices, swap(): return lax.ppermute(value, axis, [(d, d ^ mask) for d in range(size)])  32.2 us
    unnamed x48, local copies, waits for them, and re-layouts  6.05 us
    pallas_call x1, Pallas kernels, density_last(): pl.pallas_call(functools.partial(density_last_kernel, chunks, plan, early...  5.78 us
    pallas_call x7, Pallas kernels, pair(): pl.pallas_call(functools.partial(pair_kernel, pieces), in_specs=[vmem] *...  5.49 us
    pallas_call x7, Pallas kernels, merge(): pl.pallas_call(kernel, in_specs=[vmem] * len(arrays) + [vmem, smem, smem,...  3.39 us
    pallas_call x1, Pallas kernels, prepare(): pl.pallas_call(functools.partial(prepare_kernel, n_occ, chunks, src_count...  3.18 us
  transfers between devices with their start and end apart: 26, of which 16 were waited for; matrix products, arithmetic and copies ran while one was open for 1% of the time, Pallas kernels for 12%

profile of v5, /device:TPU:0, one launch (start us, length us, event | category | flops | bytes accessed | tf_op | source)
XLA Modules:
  0.0 94.5 jit_solution(9060291847261030062)
XLA Ops:
  0.0 3.2 %prepare.1 = (bf16[256,512]{1,0:T(8,128)(2,1)S(1)}, bf16[256,512]{1,0:T(8,128)(2,1)S(1)}, bf16[256,512]{1,0:T(8,128)(2,1)S(1)}, bf16[256,512]{1,0:T(8,128)(2,1)S...) custom-call(s32[4]{0:T(128)} %refs_13_.1, ...), custom_call_target="tpu_custom_call" | custom-call | tf_op jit(solution)/shard_map/prepare/pallas_call | solution.py:68
  4.3 2.6 %collective-permute-start = (bf16[256,512]{1,0:T(8,128)(2,1)S(1)}, bf16[256,512]{1,0:T(8,128)(2,1)S(1)}, u32[]{:S(2)}, u32[]{:S(2)}) collective-permute-start(bf16[256,512]{1,0:T(8,128)(2,1)S(1)} %get-tuple-element.27.refs_0_), channel_id=1, source_target_pairs={{0,8},{8,0},{16,24},{24,16},{1,9},{9,1},{17,25},{25,17},{2,10},{10... | collective-permute-start | bytes 786440 | tf_op jit(solution)/shard_map/ppermute | solution.py:15
  6.8 1.5 %collective-permute-start.6 = (bf16[256,512]{1,0:T(8,128)(2,1)S(1)}, bf16[256,512]{1,0:T(8,128)(2,1)S(1)}, u32[]{:S(2)}, u32[]{:S(2)}) collective-permute-start(bf16[256,512]{1,0:T(8,128)(2,1)S(1)} %get-tuple-element.28.refs_4_.refs_1_), channel_id=1, source_target_pairs={{0,16},{8,24},{16,0},{24,8},{1,17},{9,25},{17,1},{25,9},{2,18},{10... | collective-permute-start | bytes 786440 | tf_op jit(solution)/shard_map/ppermute | solution.py:15
  9.1 2.2 %collective-permute-start.4 = (bf16[4,256,256]{2,1,0:T(8,128)(2,1)S(1)}, bf16[4,256,256]{2,1,0:T(8,128)(2,1)S(1)}, u32[]{:S(2)}, u32[]{:S(2)}) collective-permute-start(bf16[4,256,256]{2,1,0:T(8,128)(2,1)S(1)} %pair.7.refs_0_), channel_id=1, source_target_pairs={{0,2},{1,3},{2,0},{3,1},{4,6},{5,7},{6,4},{7,5},{8,10},{9,11},{10,... | collective-permute-start | bytes 1572872 | tf_op jit(solution)/shard_map/ppermute | solution.py:15
  12.0 1.6 %collective-permute-start.5 = (bf16[2,512,256]{2,1,0:T(8,128)(2,1)S(1)}, bf16[2,512,256]{2,1,0:T(8,128)(2,1)S(1)}, u32[]{:S(2)}, u32[]{:S(2)}) collective-permute-start(bf16[2,512,256]{2,1,0:T(8,128)(2,1)S(1)} %pair.9.refs_0_), channel_id=1, source_target_pairs={{0,8},{8,0},{16,24},{24,16},{1,9},{9,1},{17,25},{25,17},{2,10},{10... | collective-permute-start | bytes 1572872 | tf_op jit(solution)/shard_map/ppermute | solution.py:15
  13.7 1.5 %collective-permute-done.6.refs_2_.refs_5_.refs_7_ = bf16[256,512]{1,0:T(8,128)(2,1)S(1)} collective-permute-done((bf16[256,512]{1,0:T(8,128)(2,1)S(1)}, bf16[256,512]{1,0:T(8,128)(2,1)S(1)}, u32[]{:S(2)}, u32[]{:S(2)}) %collective-permute-start.6) | collective-permute-done | bytes 262176 | tf_op jit(solution)/shard_map/ppermute | solution.py:15
  15.9 1.6 %collective-permute-start.7 = (bf16[2,512,256]{2,1,0:T(8,128)(2,1)S(1)}, bf16[2,512,256]{2,1,0:T(8,128)(2,1)S(1)}, u32[]{:S(2)}, u32[]{:S(2)}) collective-permute-start(bf16[2,512,256]{2,1,0:T(8,128)(2,1)S(1)} %pair.11.refs_1_), channel_id=1, source_target_pairs={{0,16},{8,24},{16,0},{24,8},{1,17},{9,25},{17,1},{25,9},{2,18},{10... | collective-permute-start | bytes 1572872 | tf_op jit(solution)/shard_map/ppermute | solution.py:15
  18.2 1.6 %collective-permute-start.8 = (bf16[4,256,256]{2,1,0:T(8,128)(2,1)S(1)}, bf16[4,256,256]{2,1,0:T(8,128)(2,1)S(1)}, u32[]{:S(2)}, u32[]{:S(2)}) collective-permute-start(bf16[4,256,256]{2,1,0:T(8,128)(2,1)S(1)} %pair.13), channel_id=1, source_target_pairs={{0,2},{1,3},{2,0},{3,1},{4,6},{5,7},{6,4},{7,5},{8,10},{9,11},{10,... | collective-permute-start | bytes 1572872 | tf_op jit(solution)/shard_map/ppermute | solution.py:15
  19.9 4.1 %collective-permute-done.4.refs_0_.refs_1_ = bf16[4,256,256]{2,1,0:T(8,128)(2,1)S(1)} collective-permute-done((bf16[4,256,256]{2,1,0:T(8,128)(2,1)S(1)}, bf16[4,256,256]{2,1,0:T(8,128)(2,1)S(1)}, u32[]{:S(2)}, u32[]{:S(2)}) %collective-permute-start.4) | collective-permute-done | bytes 524320 | tf_op jit(solution)/shard_map/ppermute | solution.py:15
  25.7 3.4 %collective-permute-done.7.refs_3_.refs_1_ = bf16[2,512,256]{2,1,0:T(8,128)(2,1)S(1)} collective-permute-done((bf16[2,512,256]{2,1,0:T(8,128)(2,1)S(1)}, bf16[2,512,256]{2,1,0:T(8,128)(2,1)S(1)}, u32[]{:S(2)}, u32[]{:S(2)}) %collective-permute-start.7) | collective-permute-done | bytes 524320 | tf_op jit(solution)/shard_map/ppermute | solution.py:15
  30.0 1.5 %collective-permute-start.13 = (bf16[1,512,256]{2,1,0:T(8,128)(2,1)S(1)}, bf16[1,512,256]{2,1,0:T(8,128)(2,1)S(1)}, u32[]{:S(2)}, u32[]{:S(2)}) collective-permute-start(bf16[1,512,256]{2,1,0:T(8,128)(2,1)S(1)} %get-tuple-element.36.refs_0_), channel_id=1, source_target_pairs={{0,16},{8,24},{16,0},{24,8},{1,17},{9,25},{17,1},{25,9},{2,18},{10... | collective-permute-start | bytes 786440 | tf_op jit(solution)/shard_map/ppermute | solution.py:15
  34.8 3.1 %collective-permute-done.14.refs_2_ = bf16[1,512,256]{2,1,0:T(8,128)(2,1)S(1)} collective-permute-done((bf16[1,512,256]{2,1,0:T(8,128)(2,1)S(1)}, bf16[1,512,256]{2,1,0:T(8,128)(2,1)S(1)}, u32[]{:S(2)}, u32[]{:S(2)}) %collective-permute-start.14) | collective-permute-done | bytes 262176 | tf_op jit(solution)/shard_map/ppermute | solution.py:15
  39.3 1.6 %collective-permute-start.15 = (bf16[1,512,256]{2,1,0:T(8,128)(2,1)S(1)}, bf16[1,512,256]{2,1,0:T(8,128)(2,1)S(1)}, u32[]{:S(2)}, u32[]{:S(2)}) collective-permute-start(bf16[1,512,256]{2,1,0:T(8,128)(2,1)S(1)} %merge.9), channel_id=1, source_target_pairs={{0,2},{1,3},{2,0},{3,1},{4,6},{5,7},{6,4},{7,5},{8,10},{9,11},{10,... | collective-permute-start | bytes 786440 | tf_op jit(solution)/shard_map/ppermute | solution.py:15
  43.5 1.5 %collective-permute-start.12 = (bf16[1,256,256]{2,1,0:T(8,128)(2,1)S(1)}, bf16[1,256,256]{2,1,0:T(8,128)(2,1)S(1)}, u32[]{:S(2)}, u32[]{:S(2)}) collective-permute-start(bf16[1,256,256]{2,1,0:T(8,128)(2,1)S(1)} %get-tuple-element.40), channel_id=1, source_target_pairs={{0,16},{8,24},{16,0},{24,8},{1,17},{9,25},{17,1},{25,9},{2,18},{10... | collective-permute-start | bytes 393224 | tf_op jit(solution)/shard_map/ppermute | solution.py:15
  45.1 1.5 %pack.3 = (bf16[4,256,512]{2,1,0:T(8,128)(2,1)}, bf16[4,256,512]{2,1,0:T(8,128)(2,1)}) custom-call(bf16[256,512]{1,0:T(8,128)(2,1)S(1)} %get-tuple-element.27.refs_0_, bf16[256,512]{1,0:T(8,128)(2,1)S(1)} %collective-permute-done.refs_1_.refs_4_, bf16[256,512]{1,0:T(8,128)(2,1)S(1)} %get-tuple-element.29.refs_2_, ...), custom_call_target="tpu_custom_call" | custom-call | tf_op jit(solution)/shard_map/pack/pallas_call | solution.py:199
  51.5 2.6 %collective-permute-start.20 = (bf16[1,256,256]{2,1,0:T(8,128)(2,1)}, bf16[1,256,256]{2,1,0:T(8,128)(2,1)}, u32[]{:S(2)}, u32[]{:S(2)}) collective-permute-start(bf16[1,256,256]{2,1,0:T(8,128)(2,1)} %merge.10.refs_5_), channel_id=1, source_target_pairs={{0,4},{1,5},{2,6},{3,7},{4,0},{5,1},{6,2},{7,3},{8,12},{9,13},{10,... | collective-permute-start | bytes 393224 | tf_op jit(solution)/shard_map/ppermute | solution.py:15
  56.5 2.9 %collective-permute-done.20.refs_4_ = bf16[1,256,256]{2,1,0:T(8,128)(2,1)} collective-permute-done((bf16[1,256,256]{2,1,0:T(8,128)(2,1)}, bf16[1,256,256]{2,1,0:T(8,128)(2,1)}, u32[]{:S(2)}, u32[]{:S(2)}) %collective-permute-start.20) | collective-permute-done | bytes 131104 | tf_op jit(solution)/shard_map/ppermute | solution.py:15
  59.4 2.8 %collective-permute-done.21.refs_9_ = bf16[1,256,256]{2,1,0:T(8,128)(2,1)} collective-permute-done((bf16[1,256,256]{2,1,0:T(8,128)(2,1)}, bf16[1,256,256]{2,1,0:T(8,128)(2,1)}, u32[]{:S(2)}, u32[]{:S(2)}) %collective-permute-start.21) | collective-permute-done | bytes 131104 | tf_op jit(solution)/shard_map/ppermute | solution.py:15
  69.8 4.0 %collective-permute-start.23 = (bf16[2,256,256]{2,1,0:T(8,128)(2,1)S(1)}, bf16[2,256,256]{2,1,0:T(8,128)(2,1)S(1)}, u32[]{:S(2)}, u32[]{:S(2)}) collective-permute-start(bf16[2,256,256]{2,1,0:T(8,128)(2,1)S(1)} %amplitude.1.refs_10_.refs_0_), channel_id=1, source_target_pairs={{0,2},{1,3},{2,0},{3,1},{4,6},{5,7},{6,4},{7,5},{8,10},{9,11},{10,... | collective-permute-start | bytes 786440 | tf_op jit(solution)/shard_map/ppermute | solution.py:15
  75.6 3.9 %collective-permute-done.22.refs_11_.refs_1_ = bf16[2,256,256]{2,1,0:T(8,128)(2,1)S(1)} collective-permute-done((bf16[2,256,256]{2,1,0:T(8,128)(2,1)S(1)}, bf16[2,256,256]{2,1,0:T(8,128)(2,1)S(1)}, u32[]{:S(2)}, u32[]{:S(2)}) %collective-permute-start.22) | collective-permute-done | bytes 262176 | tf_op jit(solution)/shard_map/ppermute | solution.py:15
  81.7 1.8 %density_first.1.refs_4_.refs_15_ = f32[4,512,512]{2,1,0:T(8,128)S(1)} custom-call(bf16[256,512]{1,0:T(8,128)(2,1)S(1)} %copy-done.9, bf16[256,512]{1,0:T(8,128)(2,1)S(1)} %copy-done.11, bf16[256,512]{1,0:T(8,128)(2,1)S(1)} %copy-done.13, bf16[256,512]{1,0:T(8,128)(2,1)S(1)} %copy-done.15, bf16[256,512]{1,0:T(8,128)(2,1)S(1)} %collective-permute-done.refs_1_.refs_4_, ...), custom_call_target="tpu_custom_call" | custom-call | tf_op jit(solution)/shard_map/density_first/pallas_call | solution.py:289
  83.5 2.4 %collective-permute-done.24.refs_3_.refs_13_ = bf16[2,256,256]{2,1,0:T(8,128)(2,1)S(1)} collective-permute-done((bf16[2,256,256]{2,1,0:T(8,128)(2,1)S(1)}, bf16[2,256,256]{2,1,0:T(8,128)(2,1)S(1)}, u32[]{:S(2)}, u32[]{:S(2)}) %collective-permute-start.24) | collective-permute-done | bytes 262176 | tf_op jit(solution)/shard_map/ppermute | solution.py:15
  86.0 2.6 %collective-permute-done.25.refs_14_ = bf16[8,256,256]{2,1,0:T(8,128)(2,1)S(1)} collective-permute-done((bf16[8,256,256]{2,1,0:T(8,128)(2,1)S(1)}, bf16[8,256,256]{2,1,0:T(8,128)(2,1)S(1)}, u32[]{:S(2)}, u32[]{:S(2)}) %collective-permute-start.25) | collective-permute-done | bytes 1048608 | tf_op jit(solution)/shard_map/ppermute | solution.py:15
  88.7 5.8 %density_last.1 = bf16[2048,4,256]{2,1,0:T(4,128)(2,1)} custom-call(bf16[256,512]{1,0:T(8,128)(2,1)S(1)} %copy-done.9, bf16[256,512]{1,0:T(8,128)(2,1)S(1)} %copy-done.11, bf16[256,512]{1,0:T(8,128)(2,1)S(1)} %copy-done.13, bf16[256,512]{1,0:T(8,128)(2,1)S(1)} %copy-done.15, bf16[256,512]{1,0:T(8,128)(2,1)S(1)} %collective-permute-done.refs_1_.refs_4_, ...), custom_call_target="tpu_custom_call" | custom-call | tf_op jit(solution)/shard_map/density_last/pallas_call | solution.py:304
  (97 shorter events, 31.6 us)
Async XLA Ops:
  3.2 5.1 %collective-permute-start.2 = (bf16[4,512,256]{2,1,0:T(8,128)(2,1)S(1)}, bf16[4,512,256]{2,1,0:T(8,128)(2,1)S(1)}, u32[]{:S(2)}, u32[]{:S(2)}) collective-permute-start(bf16[4,512,256]{2,1,0:T(8,128)(2,1)S(1)} %get-tuple-element.33), channel_id=1, source_target_pairs={{0,1},{1,0},{2,3},{3,2},{4,5},{5,4},{6,7},{7,6},{8,9},{9,8},{10,11... | collective-permute-start | bytes 3145736 | tf_op jit(solution)/shard_map/ppermute | solution.py:15
  3.8 7.4 %collective-permute-start.3 = (bf16[4,512,256]{2,1,0:T(8,128)(2,1)S(1)}, bf16[4,512,256]{2,1,0:T(8,128)(2,1)S(1)}, u32[]{:S(2)}, u32[]{:S(2)}) collective-permute-start(bf16[4,512,256]{2,1,0:T(8,128)(2,1)S(1)} %get-tuple-element.35), channel_id=1, source_target_pairs={{0,1},{1,0},{2,3},{3,2},{4,5},{5,4},{6,7},{7,6},{8,9},{9,8},{10,11... | collective-permute-start | bytes 3145736 | tf_op jit(solution)/shard_map/ppermute | solution.py:15
  4.3 9.5 %collective-permute-start = (bf16[256,512]{1,0:T(8,128)(2,1)S(1)}, bf16[256,512]{1,0:T(8,128)(2,1)S(1)}, u32[]{:S(2)}, u32[]{:S(2)}) collective-permute-start(bf16[256,512]{1,0:T(8,128)(2,1)S(1)} %get-tuple-element.27.refs_0_), channel_id=1, source_target_pairs={{0,8},{8,0},{16,24},{24,16},{1,9},{9,1},{17,25},{25,17},{2,10},{10... | collective-permute-start | bytes 786440 | tf_op jit(solution)/shard_map/ppermute | solution.py:15
  6.8 8.4 %collective-permute-start.6 = (bf16[256,512]{1,0:T(8,128)(2,1)S(1)}, bf16[256,512]{1,0:T(8,128)(2,1)S(1)}, u32[]{:S(2)}, u32[]{:S(2)}) collective-permute-start(bf16[256,512]{1,0:T(8,128)(2,1)S(1)} %get-tuple-element.28.refs_4_.refs_1_), channel_id=1, source_target_pairs={{0,16},{8,24},{16,0},{24,8},{1,17},{9,25},{17,1},{25,9},{2,18},{10... | collective-permute-start | bytes 786440 | tf_op jit(solution)/shard_map/ppermute | solution.py:15
  9.1 14.9 %collective-permute-start.4 = (bf16[4,256,256]{2,1,0:T(8,128)(2,1)S(1)}, bf16[4,256,256]{2,1,0:T(8,128)(2,1)S(1)}, u32[]{:S(2)}, u32[]{:S(2)}) collective-permute-start(bf16[4,256,256]{2,1,0:T(8,128)(2,1)S(1)} %pair.7.refs_0_), channel_id=1, source_target_pairs={{0,2},{1,3},{2,0},{3,1},{4,6},{5,7},{6,4},{7,5},{8,10},{9,11},{10,... | collective-permute-start | bytes 1572872 | tf_op jit(solution)/shard_map/ppermute | solution.py:15
  12.0 13.8 %collective-permute-start.5 = (bf16[2,512,256]{2,1,0:T(8,128)(2,1)S(1)}, bf16[2,512,256]{2,1,0:T(8,128)(2,1)S(1)}, u32[]{:S(2)}, u32[]{:S(2)}) collective-permute-start(bf16[2,512,256]{2,1,0:T(8,128)(2,1)S(1)} %pair.9.refs_0_), channel_id=1, source_target_pairs={{0,8},{8,0},{16,24},{24,16},{1,9},{9,1},{17,25},{25,17},{2,10},{10... | collective-permute-start | bytes 1572872 | tf_op jit(solution)/shard_map/ppermute | solution.py:15
  15.9 13.2 %collective-permute-start.7 = (bf16[2,512,256]{2,1,0:T(8,128)(2,1)S(1)}, bf16[2,512,256]{2,1,0:T(8,128)(2,1)S(1)}, u32[]{:S(2)}, u32[]{:S(2)}) collective-permute-start(bf16[2,512,256]{2,1,0:T(8,128)(2,1)S(1)} %pair.11.refs_1_), channel_id=1, source_target_pairs={{0,16},{8,24},{16,0},{24,8},{1,17},{9,25},{17,1},{25,9},{2,18},{10... | collective-permute-start | bytes 1572872 | tf_op jit(solution)/shard_map/ppermute | solution.py:15
  18.2 22.7 %collective-permute-start.8 = (bf16[4,256,256]{2,1,0:T(8,128)(2,1)S(1)}, bf16[4,256,256]{2,1,0:T(8,128)(2,1)S(1)}, u32[]{:S(2)}, u32[]{:S(2)}) collective-permute-start(bf16[4,256,256]{2,1,0:T(8,128)(2,1)S(1)} %pair.13), channel_id=1, source_target_pairs={{0,2},{1,3},{2,0},{3,1},{4,6},{5,7},{6,4},{7,5},{8,10},{9,11},{10,... | collective-permute-start | bytes 1572872 | tf_op jit(solution)/shard_map/ppermute | solution.py:15
  29.3 8.7 %collective-permute-start.14 = (bf16[1,512,256]{2,1,0:T(8,128)(2,1)S(1)}, bf16[1,512,256]{2,1,0:T(8,128)(2,1)S(1)}, u32[]{:S(2)}, u32[]{:S(2)}) collective-permute-start(bf16[1,512,256]{2,1,0:T(8,128)(2,1)S(1)} %get-tuple-element.41), channel_id=1, source_target_pairs={{0,8},{8,0},{16,24},{24,16},{1,9},{9,1},{17,25},{25,17},{2,10},{10... | collective-permute-start | bytes 786440 | tf_op jit(solution)/shard_map/ppermute | solution.py:15
  30.0 9.2 %collective-permute-start.13 = (bf16[1,512,256]{2,1,0:T(8,128)(2,1)S(1)}, bf16[1,512,256]{2,1,0:T(8,128)(2,1)S(1)}, u32[]{:S(2)}, u32[]{:S(2)}) collective-permute-start(bf16[1,512,256]{2,1,0:T(8,128)(2,1)S(1)} %get-tuple-element.36.refs_0_), channel_id=1, source_target_pairs={{0,16},{8,24},{16,0},{24,8},{1,17},{9,25},{17,1},{25,9},{2,18},{10... | collective-permute-start | bytes 786440 | tf_op jit(solution)/shard_map/ppermute | solution.py:15
  32.9 9.4 %collective-permute-start.9 = (bf16[2,256,256]{2,1,0:T(8,128)(2,1)S(1)}, bf16[2,256,256]{2,1,0:T(8,128)(2,1)S(1)}, u32[]{:S(2)}, u32[]{:S(2)}) collective-permute-start(bf16[2,256,256]{2,1,0:T(8,128)(2,1)S(1)} %get-tuple-element.37), channel_id=1, source_target_pairs={{0,16},{8,24},{16,0},{24,8},{1,17},{9,25},{17,1},{25,9},{2,18},{10... | collective-permute-start | bytes 786440 | tf_op jit(solution)/shard_map/ppermute | solution.py:15
  33.4 8.8 %collective-permute-start.10 = (bf16[2,256,256]{2,1,0:T(8,128)(2,1)S(1)}, bf16[2,256,256]{2,1,0:T(8,128)(2,1)S(1)}, u32[]{:S(2)}, u32[]{:S(2)}) collective-permute-start(bf16[2,256,256]{2,1,0:T(8,128)(2,1)S(1)} %get-tuple-element.38), channel_id=1, source_target_pairs={{0,8},{8,0},{16,24},{24,16},{1,9},{9,1},{17,25},{25,17},{2,10},{10... | collective-permute-start | bytes 786440 | tf_op jit(solution)/shard_map/ppermute | solution.py:15
  39.3 7.2 %collective-permute-start.15 = (bf16[1,512,256]{2,1,0:T(8,128)(2,1)S(1)}, bf16[1,512,256]{2,1,0:T(8,128)(2,1)S(1)}, u32[]{:S(2)}, u32[]{:S(2)}) collective-permute-start(bf16[1,512,256]{2,1,0:T(8,128)(2,1)S(1)} %merge.9), channel_id=1, source_target_pairs={{0,2},{1,3},{2,0},{3,1},{4,6},{5,7},{6,4},{7,5},{8,10},{9,11},{10,... | collective-permute-start | bytes 786440 | tf_op jit(solution)/shard_map/ppermute | solution.py:15
  42.4 5.0 %collective-permute-start.11 = (bf16[1,256,256]{2,1,0:T(8,128)(2,1)S(1)}, bf16[1,256,256]{2,1,0:T(8,128)(2,1)S(1)}, u32[]{:S(2)}, u32[]{:S(2)}) collective-permute-start(bf16[1,256,256]{2,1,0:T(8,128)(2,1)S(1)} %get-tuple-element.39), channel_id=1, source_target_pairs={{0,8},{8,0},{16,24},{24,16},{1,9},{9,1},{17,25},{25,17},{2,10},{10... | collective-permute-start | bytes 393224 | tf_op jit(solution)/shard_map/ppermute | solution.py:15
  43.5 5.0 %collective-permute-start.12 = (bf16[1,256,256]{2,1,0:T(8,128)(2,1)S(1)}, bf16[1,256,256]{2,1,0:T(8,128)(2,1)S(1)}, u32[]{:S(2)}, u32[]{:S(2)}) collective-permute-start(bf16[1,256,256]{2,1,0:T(8,128)(2,1)S(1)} %get-tuple-element.40), channel_id=1, source_target_pairs={{0,16},{8,24},{16,0},{24,8},{1,17},{9,25},{17,1},{25,9},{2,18},{10... | collective-permute-start | bytes 393224 | tf_op jit(solution)/shard_map/ppermute | solution.py:15
  49.2 24.6 %collective-permute-start.16 = (bf16[4,256,512]{2,1,0:T(8,128)(2,1)}, bf16[4,256,512]{2,1,0:T(8,128)(2,1)S(1)}, u32[]{:S(2)}, u32[]{:S(2)}) collective-permute-start(bf16[4,256,512]{2,1,0:T(8,128)(2,1)} %get-tuple-element.44), channel_id=1, source_target_pairs={{0,8},{8,0},{16,24},{24,16},{1,9},{9,1},{17,25},{25,17},{2,10},{10... | collective-permute-start | bytes 3145736 | tf_op jit(solution)/shard_map/ppermute | solution.py:15
  50.3 23.5 %collective-permute-start.17 = (bf16[4,256,512]{2,1,0:T(8,128)(2,1)}, bf16[4,256,512]{2,1,0:T(8,128)(2,1)S(1)}, u32[]{:S(2)}, u32[]{:S(2)}) collective-permute-start(bf16[4,256,512]{2,1,0:T(8,128)(2,1)} %get-tuple-element.45), channel_id=1, source_target_pairs={{0,16},{8,24},{16,0},{24,8},{1,17},{9,25},{17,1},{25,9},{2,18},{10... | collective-permute-start | bytes 3145736 | tf_op jit(solution)/shard_map/ppermute | solution.py:15
  51.5 7.9 %collective-permute-start.20 = (bf16[1,256,256]{2,1,0:T(8,128)(2,1)}, bf16[1,256,256]{2,1,0:T(8,128)(2,1)}, u32[]{:S(2)}, u32[]{:S(2)}) collective-permute-start(bf16[1,256,256]{2,1,0:T(8,128)(2,1)} %merge.10.refs_5_), channel_id=1, source_target_pairs={{0,4},{1,5},{2,6},{3,7},{4,0},{5,1},{6,2},{7,3},{8,12},{9,13},{10,... | collective-permute-start | bytes 393224 | tf_op jit(solution)/shard_map/ppermute | solution.py:15
  54.1 8.1 %collective-permute-start.21 = (bf16[1,256,256]{2,1,0:T(8,128)(2,1)}, bf16[1,256,256]{2,1,0:T(8,128)(2,1)}, u32[]{:S(2)}, u32[]{:S(2)}) collective-permute-start(bf16[1,256,256]{2,1,0:T(8,128)(2,1)} %get-tuple-element.48), channel_id=1, source_target_pairs={{0,4},{1,5},{2,6},{3,7},{4,0},{5,1},{6,2},{7,3},{8,12},{9,13},{10,... | collective-permute-start | bytes 393224 | tf_op jit(solution)/shard_map/ppermute | solution.py:15
  69.7 9.8 %collective-permute-start.22 = (bf16[2,256,256]{2,1,0:T(8,128)(2,1)S(1)}, bf16[2,256,256]{2,1,0:T(8,128)(2,1)S(1)}, u32[]{:S(2)}, u32[]{:S(2)}) collective-permute-start(bf16[2,256,256]{2,1,0:T(8,128)(2,1)S(1)} %amplitude.1.refs_10_.refs_0_), channel_id=1, source_target_pairs={{0,4},{1,5},{2,6},{3,7},{4,0},{5,1},{6,2},{7,3},{8,12},{9,13},{10,... | collective-permute-start | bytes 786440 | tf_op jit(solution)/shard_map/ppermute | solution.py:15
  69.8 11.9 %collective-permute-start.23 = (bf16[2,256,256]{2,1,0:T(8,128)(2,1)S(1)}, bf16[2,256,256]{2,1,0:T(8,128)(2,1)S(1)}, u32[]{:S(2)}, u32[]{:S(2)}) collective-permute-start(bf16[2,256,256]{2,1,0:T(8,128)(2,1)S(1)} %amplitude.1.refs_10_.refs_0_), channel_id=1, source_target_pairs={{0,2},{1,3},{2,0},{3,1},{4,6},{5,7},{6,4},{7,5},{8,10},{9,11},{10,... | collective-permute-start | bytes 786440 | tf_op jit(solution)/shard_map/ppermute | solution.py:15
  73.9 7.8 %collective-permute-start.18 = (bf16[1,256,512]{2,1,0:T(8,128)(2,1)S(1)}, bf16[1,256,512]{2,1,0:T(8,128)(2,1)S(1)}, u32[]{:S(2)}, u32[]{:S(2)}) collective-permute-start(bf16[1,256,512]{2,1,0:T(8,128)(2,1)S(1)} %get-tuple-element.46), channel_id=1, source_target_pairs={{0,16},{8,24},{16,0},{24,8},{1,17},{9,25},{17,1},{25,9},{2,18},{10... | collective-permute-start | bytes 786440 | tf_op jit(solution)/shard_map/ppermute | solution.py:15
  74.4 7.2 %collective-permute-start.19 = (bf16[1,256,512]{2,1,0:T(8,128)(2,1)S(1)}, bf16[1,256,512]{2,1,0:T(8,128)(2,1)S(1)}, u32[]{:S(2)}, u32[]{:S(2)}) collective-permute-start(bf16[1,256,512]{2,1,0:T(8,128)(2,1)S(1)} %get-tuple-element.47), channel_id=1, source_target_pairs={{0,8},{8,0},{16,24},{24,16},{1,9},{9,1},{17,25},{25,17},{2,10},{10... | collective-permute-start | bytes 786440 | tf_op jit(solution)/shard_map/ppermute | solution.py:15
  79.5 6.4 %collective-permute-start.24 = (bf16[2,256,256]{2,1,0:T(8,128)(2,1)S(1)}, bf16[2,256,256]{2,1,0:T(8,128)(2,1)S(1)}, u32[]{:S(2)}, u32[]{:S(2)}) collective-permute-start(bf16[2,256,256]{2,1,0:T(8,128)(2,1)S(1)} %collective-permute-done.22.refs_11_.refs_1_), channel_id=1, source_target_pairs={{0,2},{1,3},{2,0},{3,1},{4,6},{5,7},{6,4},{7,5},{8,10},{9,11},{10,... | collective-permute-start | bytes 786440 | tf_op jit(solution)/shard_map/ppermute | solution.py:15
  (26 other events, 389.2 us)

commit v6 on v5

--- a/solution.py
+++ b/solution.py
@@ -82,6 +82,29 @@
     )(*(pltpu.with_memory_space_constraint(v, pltpu.HBM) for v in (src, integrals)))
 
 
+def pair_both_kernel(pieces, src_own, src_other, ints_own, ints_other, *refs):
+    for half, (blocks, out) in enumerate(zip(pieces, refs[-2:], strict=True)):
+        tall = out.shape[1]
+        rows = pl.ds(half * tall, tall)
+        for j, block in enumerate(blocks):
+            total = jnp.dot(src_own[rows, :], ints_own[block], preferred_element_type=F32)
+            total += jnp.dot(src_other[rows, :], ints_other[block], preferred_element_type=F32)
+            out[j] = total.astype(BF16)
+
+
+def pair_both(src_own, src_other, ints_own, ints_other, pieces, after=()):
+    vmem = pl.BlockSpec(memory_space=pltpu.VMEM)
+    tall, width = src_own.shape[0] // 2, ints_own.shape[2]
+    return pl.pallas_call(
+        functools.partial(pair_both_kernel, pieces),
+        in_specs=[vmem] * 4 + [pl.BlockSpec(memory_space=pl.ANY)] * len(after),
+        out_specs=[vmem] * 2,
+        out_shape=[jax.ShapeDtypeStruct((len(blocks), tall, width), BF16) for blocks in pieces],
+        compiler_params=pltpu.CompilerParams(vmem_limit_bytes=16 * MIB),
+        name="pair_both",
+    )(src_own, src_other, ints_own, ints_other, *after)
+
+
 def pair_kernel(pieces, src_own, src_other, ints_own, ints_other, *refs):
     out = refs[-1]
     tall = out.shape[1]
@@ -125,7 +148,7 @@
     return 2.0 * scaled - scaled.T
 
 
-def merge(outputs, energies=None, chunk=0, chunks=1, after=(), through=()):
+def merge(outputs, energies=None, chunk=0, chunks=1, wide=(), after=(), through=()):
     arrays, places = [], {}
 
     def spot(array):
@@ -146,7 +169,7 @@
                 total = add_terms(refs, terms)
                 if energies is not None:
                     total = amplitude(total, functools.partial(occupied, chunk + j, chunks), *refs[len(arrays) : n_in])
-                out[j] = total.astype(BF16)
+                out[j] = total.astype(out.dtype)
 
     anywhere = pl.BlockSpec(memory_space=pl.ANY)
     vmem, smem = pl.BlockSpec(memory_space=pltpu.VMEM), pl.BlockSpec(memory_space=pltpu.SMEM)
@@ -154,7 +177,7 @@
         kernel,
         in_specs=[vmem] * len(arrays) + [vmem, smem, smem, smem][: len(extra)] + [anywhere] * (len(after) + len(through)),
         out_specs=[vmem] * len(outputs) + [anywhere] * len(through),
-        out_shape=[jax.ShapeDtypeStruct(s, BF16) for s in shapes]
+        out_shape=[jax.ShapeDtypeStruct(s, F32 if i in wide else BF16) for i, s in enumerate(shapes)]
         + [jax.ShapeDtypeStruct(v.shape, v.dtype) for v in through],
         input_output_aliases={n_in + len(after) + i: len(outputs) + i for i in range(len(through))},
         compiler_params=pltpu.CompilerParams(vmem_limit_bytes=12 * MIB),
@@ -382,8 +405,7 @@
         groups = leaving_sources()
         packs = pack_sources(groups)
         held = [near_got[0]]
-        kept_x = product(0, 2, [(0, k) for k in even], held)
-        kept_y = product(0, 2, [(1, k) for k in front], held)
+        kept_x, kept_y = pair_both(src_t, src_other, mine[0], other[0], (even, front), held)
         first_x = {2 * i: [(kept_x, i, 0, tall)] for i in range(half_n)}
         first_x |= {2 * i + 1: [(sent_x, i, 0, tall)] for i in range(half_n)}
         first_y = {i: [(kept_y, i, 0, tall)] for i in range(half_n)}
@@ -393,7 +415,7 @@
         while unit_x.bits:
             sent_x, sent_y = merge([unit_x.plan(), unit_y.plan()])
             got_x, got_y = unit_x.send(sent_x), unit_y.send(sent_y)
-        near_kept = product(1, 2, [(0, k) for k in range(n_occ)], [sent_x])
+        near_kept = product(1, 2, [(0, k) for k in range(n_occ)], [kept_x, kept_y])
         (sent,) = merge([[unit_y.terms[0]]], after=[got_x])
         got = swap(sent, "aux", n_aux, near)
         terms_0 = unit_x.terms[0] + [(got, 0, 0, tall)]
@@ -409,16 +431,18 @@
         sent_x, sent_y = merge([unit_x.plan(), unit_y.plan()], after=[])
         got_x, got_y = unit_x.send(sent_x), unit_y.send(sent_y)
 
-        (sent_0,) = merge([[rows_of(terms_0, small, small)]])
+        sent_0, kept_0 = merge([[rows_of(terms_0, small, small)], [rows_of(terms_0, 0, small)]], wide=[1])
         got_0 = swap(sent_0, "aux", n_aux, far)
-        terms_0 = rows_of(terms_0, 0, small) + [(got_0, 0, 0, small)]
+        terms_0 = [(kept_0, 0, 0, small), (got_0, 0, 0, small)]
 
         while unit_x.bits:
             sent_x, sent_y = merge([unit_x.plan(), unit_y.plan()])
             got_x, got_y = unit_x.send(sent_x), unit_y.send(sent_y)
-        sent_1, *packs = merge([[unit_y.terms[0]]], after=[got_x, sent_0], through=packs)
+        sent_1, kept_1, *packs = merge(
+            [[unit_y.terms[0]], [unit_x.terms[0]]], wide=[1], after=[sent_0], through=packs
+        )
         got_1 = swap(sent_1, "aux", n_aux, far)
-        terms_1 = unit_x.terms[0] + [(got_1, 0, 0, small)]
+        terms_1 = [(kept_1, 0, 0, small), (got_1, 0, 0, small)]
 
         send_sources(groups, packs)
         while groups := leaving_sources():

time: 94.9 us -> 93.2 us (0.982)
  local copies, waits for them, and re-layouts: 6.83 us -> 4.35 us
  starting transfers between devices: 32.7 us -> 34.1 us
  Pallas kernels: 21.2 us -> 20.2 us
    unnamed x48 -> x16, local copies, waits for them, and re-layouts: 6.05 us -> 3.57 us
    pallas_call x7 -> x5, Pallas kernels: 5.49 us -> 4.07 us  [pair(): pl.pallas_call(functools.partial(pair_kernel, pieces), in_specs=[vmem] *...]
    ppermute x26, starting transfers between devices: 32.7 us -> 34.1 us  [swap(): return lax.ppermute(value, axis, [(d, d ^ mask) for d in range(size)])]
    pallas_call x0 -> x1, Pallas kernels: none -> 1.25 us  [pair_both(): pl.pallas_call(functools.partial(pair_both_kernel, pieces), in_specs=[vme...]
  transfers between devices with their start and end apart: 26 -> 26, of which waited for: 16 -> 18; matrix products, arithmetic and copies ran while one was open for 1% -> 1% of each run, Pallas kernels for 12% -> 11%
where the time goes in v6:
time: 93.2 us; the launch traced here: 92.9 us
  starting transfers between devices  34.1 us (37%)
  waiting for transfers between devices  32.8 us (35%)
  Pallas kernels  20.2 us (22%)
  local copies, waits for them, and re-layouts  4.35 us (5%)
  between operations  1.49 us (2%)
    ppermute x26, starting transfers between devices, swap(): return lax.ppermute(value, axis, [(d, d ^ mask) for d in range(size)])  34.1 us
    ppermute x26, waiting for transfers between devices, swap(): return lax.ppermute(value, axis, [(d, d ^ mask) for d in range(size)])  32.8 us
    pallas_call x1, Pallas kernels, density_last(): pl.pallas_call(functools.partial(density_last_kernel, chunks, plan, early...  5.76 us
    pallas_call x5, Pallas kernels, pair(): pl.pallas_call(functools.partial(pair_kernel, pieces), in_specs=[vmem] *...  4.07 us
    unnamed x16, local copies, waits for them, and re-layouts  3.57 us
    pallas_call x1, Pallas kernels, prepare(): pl.pallas_call(functools.partial(prepare_kernel, n_occ, chunks, src_count...  3.18 us
    pallas_call x7, Pallas kernels, merge(): pl.pallas_call(kernel, in_specs=[vmem] * len(arrays) + [vmem, smem, smem,...  2.57 us
  transfers between devices with their start and end apart: 26, of which 18 were waited for; matrix products, arithmetic and copies ran while one was open for 1% of the time, Pallas kernels for 11%

profile of v6, /device:TPU:0, one launch (start us, length us, event | category | flops | bytes accessed | tf_op | source)
XLA Modules:
  0.0 92.9 jit_solution(12998808526196785790)
XLA Ops:
  0.0 3.2 %prepare.1 = (bf16[256,512]{1,0:T(8,128)(2,1)S(1)}, bf16[256,512]{1,0:T(8,128)(2,1)S(1)}, bf16[256,512]{1,0:T(8,128)(2,1)S(1)}, bf16[256,512]{1,0:T(8,128)(2,1)S...) custom-call(s32[4]{0:T(128)} %refs_7_.1, ...), custom_call_target="tpu_custom_call" | custom-call | tf_op jit(solution)/shard_map/prepare/pallas_call | solution.py:68
  4.2 2.6 %collective-permute-start = (bf16[256,512]{1,0:T(8,128)(2,1)S(1)}, bf16[256,512]{1,0:T(8,128)(2,1)S(1)}, u32[]{:S(2)}, u32[]{:S(2)}) collective-permute-start(bf16[256,512]{1,0:T(8,128)(2,1)S(1)} %get-tuple-element.32.refs_0_), channel_id=1, source_target_pairs={{0,8},{8,0},{16,24},{24,16},{1,9},{9,1},{17,25},{25,17},{2,10},{10... | collective-permute-start | bytes 786440 | tf_op jit(solution)/shard_map/ppermute | solution.py:15
  6.8 1.5 %collective-permute-start.5 = (bf16[256,512]{1,0:T(8,128)(2,1)S(1)}, bf16[256,512]{1,0:T(8,128)(2,1)S(1)}, u32[]{:S(2)}, u32[]{:S(2)}) collective-permute-start(bf16[256,512]{1,0:T(8,128)(2,1)S(1)} %get-tuple-element.33.refs_4_.refs_1_), channel_id=1, source_target_pairs={{0,16},{8,24},{16,0},{24,8},{1,17},{9,25},{17,1},{25,9},{2,18},{10... | collective-permute-start | bytes 786440 | tf_op jit(solution)/shard_map/ppermute | solution.py:15
  9.0 2.2 %collective-permute-start.4 = (bf16[4,256,256]{2,1,0:T(8,128)(2,1)S(1)}, bf16[4,256,256]{2,1,0:T(8,128)(2,1)S(1)}, u32[]{:S(2)}, u32[]{:S(2)}) collective-permute-start(bf16[4,256,256]{2,1,0:T(8,128)(2,1)S(1)} %pair.5.refs_0_), channel_id=1, source_target_pairs={{0,2},{1,3},{2,0},{3,1},{4,6},{5,7},{6,4},{7,5},{8,10},{9,11},{10,... | collective-permute-start | bytes 1572872 | tf_op jit(solution)/shard_map/ppermute | solution.py:15
  11.9 1.6 %collective-permute-start.11 = (bf16[2,512,256]{2,1,0:T(8,128)(2,1)S(1)}, bf16[2,512,256]{2,1,0:T(8,128)(2,1)S(1)}, u32[]{:S(2)}, u32[]{:S(2)}) collective-permute-start(bf16[2,512,256]{2,1,0:T(8,128)(2,1)S(1)} %pair.7.refs_0_), channel_id=1, source_target_pairs={{0,8},{8,0},{16,24},{24,16},{1,9},{9,1},{17,25},{25,17},{2,10},{10... | collective-permute-start | bytes 1572872 | tf_op jit(solution)/shard_map/ppermute | solution.py:15
  13.7 1.5 %collective-permute-done.5.refs_2_.refs_5_.refs_7_ = bf16[256,512]{1,0:T(8,128)(2,1)S(1)} collective-permute-done((bf16[256,512]{1,0:T(8,128)(2,1)S(1)}, bf16[256,512]{1,0:T(8,128)(2,1)S(1)}, u32[]{:S(2)}, u32[]{:S(2)}) %collective-permute-start.5) | collective-permute-done | bytes 262176 | tf_op jit(solution)/shard_map/ppermute | solution.py:15
  15.9 1.6 %collective-permute-start.12 = (bf16[2,512,256]{2,1,0:T(8,128)(2,1)S(1)}, bf16[2,512,256]{2,1,0:T(8,128)(2,1)S(1)}, u32[]{:S(2)}, u32[]{:S(2)}) collective-permute-start(bf16[2,512,256]{2,1,0:T(8,128)(2,1)S(1)} %pair.8.refs_1_), channel_id=1, source_target_pairs={{0,16},{8,24},{16,0},{24,8},{1,17},{9,25},{17,1},{25,9},{2,18},{10... | collective-permute-start | bytes 1572872 | tf_op jit(solution)/shard_map/ppermute | solution.py:15
  18.2 1.6 %collective-permute-start.6 = (bf16[4,256,256]{2,1,0:T(8,128)(2,1)S(1)}, bf16[4,256,256]{2,1,0:T(8,128)(2,1)S(1)}, u32[]{:S(2)}, u32[]{:S(2)}) collective-permute-start(bf16[4,256,256]{2,1,0:T(8,128)(2,1)S(1)} %pair.9), channel_id=1, source_target_pairs={{0,2},{1,3},{2,0},{3,1},{4,6},{5,7},{6,4},{7,5},{8,10},{9,11},{10,... | collective-permute-start | bytes 1572872 | tf_op jit(solution)/shard_map/ppermute | solution.py:15
  19.8 4.1 %collective-permute-done.4.refs_0_.refs_1_ = bf16[4,256,256]{2,1,0:T(8,128)(2,1)S(1)} collective-permute-done((bf16[4,256,256]{2,1,0:T(8,128)(2,1)S(1)}, bf16[4,256,256]{2,1,0:T(8,128)(2,1)S(1)}, u32[]{:S(2)}, u32[]{:S(2)}) %collective-permute-start.4) | collective-permute-done | bytes 524320 | tf_op jit(solution)/shard_map/ppermute | solution.py:15
  25.7 3.4 %collective-permute-done.12.refs_3_.refs_1_ = bf16[2,512,256]{2,1,0:T(8,128)(2,1)S(1)} collective-permute-done((bf16[2,512,256]{2,1,0:T(8,128)(2,1)S(1)}, bf16[2,512,256]{2,1,0:T(8,128)(2,1)S(1)}, u32[]{:S(2)}, u32[]{:S(2)}) %collective-permute-start.12) | collective-permute-done | bytes 524320 | tf_op jit(solution)/shard_map/ppermute | solution.py:15
  29.2 1.6 %collective-permute-start.13 = (bf16[1,512,256]{2,1,0:T(8,128)(2,1)S(1)}, bf16[1,512,256]{2,1,0:T(8,128)(2,1)S(1)}, u32[]{:S(2)}, u32[]{:S(2)}) collective-permute-start(bf16[1,512,256]{2,1,0:T(8,128)(2,1)S(1)} %get-tuple-element.47), channel_id=1, source_target_pairs={{0,16},{8,24},{16,0},{24,8},{1,17},{9,25},{17,1},{25,9},{2,18},{10... | collective-permute-start | bytes 786440 | tf_op jit(solution)/shard_map/ppermute | solution.py:15
  34.8 3.6 %collective-permute-done.13.refs_3_.refs_2_ = bf16[1,512,256]{2,1,0:T(8,128)(2,1)S(1)} collective-permute-done((bf16[1,512,256]{2,1,0:T(8,128)(2,1)S(1)}, bf16[1,512,256]{2,1,0:T(8,128)(2,1)S(1)}, u32[]{:S(2)}, u32[]{:S(2)}) %collective-permute-start.13) | collective-permute-done | bytes 262176 | tf_op jit(solution)/shard_map/ppermute | solution.py:15
  38.4 1.5 %collective-permute-done.14.refs_2_ = bf16[1,512,256]{2,1,0:T(8,128)(2,1)S(1)} collective-permute-done((bf16[1,512,256]{2,1,0:T(8,128)(2,1)S(1)}, bf16[1,512,256]{2,1,0:T(8,128)(2,1)S(1)}, u32[]{:S(2)}, u32[]{:S(2)}) %collective-permute-start.14) | collective-permute-done | bytes 262176 | tf_op jit(solution)/shard_map/ppermute | solution.py:15
  40.1 1.6 %collective-permute-start.15 = (bf16[1,512,256]{2,1,0:T(8,128)(2,1)S(1)}, bf16[1,512,256]{2,1,0:T(8,128)(2,1)S(1)}, u32[]{:S(2)}, u32[]{:S(2)}) collective-permute-start(bf16[1,512,256]{2,1,0:T(8,128)(2,1)S(1)} %merge.9), channel_id=1, source_target_pairs={{0,2},{1,3},{2,0},{3,1},{4,6},{5,7},{6,4},{7,5},{8,10},{9,11},{10,... | collective-permute-start | bytes 786440 | tf_op jit(solution)/shard_map/ppermute | solution.py:15
  51.9 2.6 %collective-permute-start.20 = (bf16[1,256,256]{2,1,0:T(8,128)(2,1)S(1)}, bf16[1,256,256]{2,1,0:T(8,128)(2,1)}, u32[]{:S(2)}, u32[]{:S(2)}) collective-permute-start(bf16[1,256,256]{2,1,0:T(8,128)(2,1)S(1)} %get-tuple-element.49.refs_6_), channel_id=1, source_target_pairs={{0,4},{1,5},{2,6},{3,7},{4,0},{5,1},{6,2},{7,3},{8,12},{9,13},{10,... | collective-permute-start | bytes 393224 | tf_op jit(solution)/shard_map/ppermute | solution.py:15
  56.9 2.9 %collective-permute-done.20.refs_1_ = bf16[1,256,256]{2,1,0:T(8,128)(2,1)} collective-permute-done((bf16[1,256,256]{2,1,0:T(8,128)(2,1)S(1)}, bf16[1,256,256]{2,1,0:T(8,128)(2,1)}, u32[]{:S(2)}, u32[]{:S(2)}) %collective-permute-start.20) | collective-permute-done | bytes 131104 | tf_op jit(solution)/shard_map/ppermute | solution.py:15
  59.8 2.8 %collective-permute-done.21.refs_3_ = bf16[1,256,256]{2,1,0:T(8,128)(2,1)} collective-permute-done((bf16[1,256,256]{2,1,0:T(8,128)(2,1)}, bf16[1,256,256]{2,1,0:T(8,128)(2,1)}, u32[]{:S(2)}, u32[]{:S(2)}) %collective-permute-start.21) | collective-permute-done | bytes 131104 | tf_op jit(solution)/shard_map/ppermute | solution.py:15
  65.9 6.8 %collective-permute-start.23 = (bf16[2,256,256]{2,1,0:T(8,128)(2,1)S(1)}, bf16[2,256,256]{2,1,0:T(8,128)(2,1)S(1)}, u32[]{:S(2)}, u32[]{:S(2)}) collective-permute-start(bf16[2,256,256]{2,1,0:T(8,128)(2,1)S(1)} %amplitude.1.refs_10_.refs_0_), channel_id=1, source_target_pairs={{0,2},{1,3},{2,0},{3,1},{4,6},{5,7},{6,4},{7,5},{8,10},{9,11},{10,... | collective-permute-start | bytes 786440 | tf_op jit(solution)/shard_map/ppermute | solution.py:15
  72.8 2.1 %collective-permute-done.17.refs_1_.refs_6_ = bf16[4,256,512]{2,1,0:T(8,128)(2,1)S(1)} collective-permute-done((bf16[4,256,512]{2,1,0:T(8,128)(2,1)}, bf16[4,256,512]{2,1,0:T(8,128)(2,1)S(1)}, u32[]{:S(2)}, u32[]{:S(2)}) %collective-permute-start.17) | collective-permute-done | bytes 1048608 | tf_op jit(solution)/shard_map/ppermute | solution.py:15
  77.7 1.7 %collective-permute-done.23.refs_12_.refs_2_ = bf16[2,256,256]{2,1,0:T(8,128)(2,1)S(1)} collective-permute-done((bf16[2,256,256]{2,1,0:T(8,128)(2,1)S(1)}, bf16[2,256,256]{2,1,0:T(8,128)(2,1)S(1)}, u32[]{:S(2)}, u32[]{:S(2)}) %collective-permute-start.23) | collective-permute-done | bytes 262176 | tf_op jit(solution)/shard_map/ppermute | solution.py:15
  79.4 1.9 %collective-permute-done.18.refs_8_ = bf16[1,256,512]{2,1,0:T(8,128)(2,1)S(1)} collective-permute-done((bf16[1,256,512]{2,1,0:T(8,128)(2,1)S(1)}, bf16[1,256,512]{2,1,0:T(8,128)(2,1)S(1)}, u32[]{:S(2)}, u32[]{:S(2)}) %collective-permute-start.18) | collective-permute-done | bytes 262176 | tf_op jit(solution)/shard_map/ppermute | solution.py:15
  82.5 1.8 %density_first.1.refs_4_.refs_15_ = f32[4,512,512]{2,1,0:T(8,128)S(1)} custom-call(bf16[256,512]{1,0:T(8,128)(2,1)S(1)} %get-tuple-element.32.refs_0_, bf16[256,512]{1,0:T(8,128)(2,1)S(1)} %get-tuple-element.33.refs_4_.refs_1_, bf16[256,512]{1,0:T(8,128)(2,1)S(1)} %get-tuple-element.34.refs_2_, bf16[256,512]{1,0:T(8,128)(2,1)S(1)} %copy-done.1, ...), custom_call_target="tpu_custom_call" | custom-call | tf_op jit(solution)/shard_map/density_first/pallas_call | solution.py:312
  84.5 2.6 %collective-permute-done.25.refs_14_ = bf16[8,256,256]{2,1,0:T(8,128)(2,1)S(1)} collective-permute-done((bf16[8,256,256]{2,1,0:T(8,128)(2,1)S(1)}, bf16[8,256,256]{2,1,0:T(8,128)(2,1)S(1)}, u32[]{:S(2)}, u32[]{:S(2)}) %collective-permute-start.25) | collective-permute-done | bytes 1048608 | tf_op jit(solution)/shard_map/ppermute | solution.py:15
  87.2 5.8 %density_last.1 = bf16[2048,4,256]{2,1,0:T(4,128)(2,1)} custom-call(bf16[256,512]{1,0:T(8,128)(2,1)S(1)} %get-tuple-element.32.refs_0_, bf16[256,512]{1,0:T(8,128)(2,1)S(1)} %get-tuple-element.33.refs_4_.refs_1_, bf16[256,512]{1,0:T(8,128)(2,1)S(1)} %get-tuple-element.34.refs_2_, bf16[256,512]{1,0:T(8,128)(2,1)S(1)} %copy-done.1, ...), custom_call_target="tpu_custom_call" | custom-call | tf_op jit(solution)/shard_map/density_last/pallas_call | solution.py:327
  (64 shorter events, 28.8 us)
Async XLA Ops:
  3.2 5.1 %collective-permute-start.2 = (bf16[4,512,256]{2,1,0:T(8,128)(2,1)S(1)}, bf16[4,512,256]{2,1,0:T(8,128)(2,1)S(1)}, u32[]{:S(2)}, u32[]{:S(2)}) collective-permute-start(bf16[4,512,256]{2,1,0:T(8,128)(2,1)S(1)} %get-tuple-element.38), channel_id=1, source_target_pairs={{0,1},{1,0},{2,3},{3,2},{4,5},{5,4},{6,7},{7,6},{8,9},{9,8},{10,11... | collective-permute-start | bytes 3145736 | tf_op jit(solution)/shard_map/ppermute | solution.py:15
  3.8 7.4 %collective-permute-start.3 = (bf16[4,512,256]{2,1,0:T(8,128)(2,1)S(1)}, bf16[4,512,256]{2,1,0:T(8,128)(2,1)S(1)}, u32[]{:S(2)}, u32[]{:S(2)}) collective-permute-start(bf16[4,512,256]{2,1,0:T(8,128)(2,1)S(1)} %get-tuple-element.40), channel_id=1, source_target_pairs={{0,1},{1,0},{2,3},{3,2},{4,5},{5,4},{6,7},{7,6},{8,9},{9,8},{10,11... | collective-permute-start | bytes 3145736 | tf_op jit(solution)/shard_map/ppermute | solution.py:15
  4.2 9.5 %collective-permute-start = (bf16[256,512]{1,0:T(8,128)(2,1)S(1)}, bf16[256,512]{1,0:T(8,128)(2,1)S(1)}, u32[]{:S(2)}, u32[]{:S(2)}) collective-permute-start(bf16[256,512]{1,0:T(8,128)(2,1)S(1)} %get-tuple-element.32.refs_0_), channel_id=1, source_target_pairs={{0,8},{8,0},{16,24},{24,16},{1,9},{9,1},{17,25},{25,17},{2,10},{10... | collective-permute-start | bytes 786440 | tf_op jit(solution)/shard_map/ppermute | solution.py:15
  6.8 8.4 %collective-permute-start.5 = (bf16[256,512]{1,0:T(8,128)(2,1)S(1)}, bf16[256,512]{1,0:T(8,128)(2,1)S(1)}, u32[]{:S(2)}, u32[]{:S(2)}) collective-permute-start(bf16[256,512]{1,0:T(8,128)(2,1)S(1)} %get-tuple-element.33.refs_4_.refs_1_), channel_id=1, source_target_pairs={{0,16},{8,24},{16,0},{24,8},{1,17},{9,25},{17,1},{25,9},{2,18},{10... | collective-permute-start | bytes 786440 | tf_op jit(solution)/shard_map/ppermute | solution.py:15
  9.0 14.9 %collective-permute-start.4 = (bf16[4,256,256]{2,1,0:T(8,128)(2,1)S(1)}, bf16[4,256,256]{2,1,0:T(8,128)(2,1)S(1)}, u32[]{:S(2)}, u32[]{:S(2)}) collective-permute-start(bf16[4,256,256]{2,1,0:T(8,128)(2,1)S(1)} %pair.5.refs_0_), channel_id=1, source_target_pairs={{0,2},{1,3},{2,0},{3,1},{4,6},{5,7},{6,4},{7,5},{8,10},{9,11},{10,... | collective-permute-start | bytes 1572872 | tf_op jit(solution)/shard_map/ppermute | solution.py:15
  11.9 13.8 %collective-permute-start.11 = (bf16[2,512,256]{2,1,0:T(8,128)(2,1)S(1)}, bf16[2,512,256]{2,1,0:T(8,128)(2,1)S(1)}, u32[]{:S(2)}, u32[]{:S(2)}) collective-permute-start(bf16[2,512,256]{2,1,0:T(8,128)(2,1)S(1)} %pair.7.refs_0_), channel_id=1, source_target_pairs={{0,8},{8,0},{16,24},{24,16},{1,9},{9,1},{17,25},{25,17},{2,10},{10... | collective-permute-start | bytes 1572872 | tf_op jit(solution)/shard_map/ppermute | solution.py:15
  15.9 13.2 %collective-permute-start.12 = (bf16[2,512,256]{2,1,0:T(8,128)(2,1)S(1)}, bf16[2,512,256]{2,1,0:T(8,128)(2,1)S(1)}, u32[]{:S(2)}, u32[]{:S(2)}) collective-permute-start(bf16[2,512,256]{2,1,0:T(8,128)(2,1)S(1)} %pair.8.refs_1_), channel_id=1, source_target_pairs={{0,16},{8,24},{16,0},{24,8},{1,17},{9,25},{17,1},{25,9},{2,18},{10... | collective-permute-start | bytes 1572872 | tf_op jit(solution)/shard_map/ppermute | solution.py:15
  18.2 23.5 %collective-permute-start.6 = (bf16[4,256,256]{2,1,0:T(8,128)(2,1)S(1)}, bf16[4,256,256]{2,1,0:T(8,128)(2,1)S(1)}, u32[]{:S(2)}, u32[]{:S(2)}) collective-permute-start(bf16[4,256,256]{2,1,0:T(8,128)(2,1)S(1)} %pair.9), channel_id=1, source_target_pairs={{0,2},{1,3},{2,0},{3,1},{4,6},{5,7},{6,4},{7,5},{8,10},{9,11},{10,... | collective-permute-start | bytes 1572872 | tf_op jit(solution)/shard_map/ppermute | solution.py:15
  29.2 9.2 %collective-permute-start.13 = (bf16[1,512,256]{2,1,0:T(8,128)(2,1)S(1)}, bf16[1,512,256]{2,1,0:T(8,128)(2,1)S(1)}, u32[]{:S(2)}, u32[]{:S(2)}) collective-permute-start(bf16[1,512,256]{2,1,0:T(8,128)(2,1)S(1)} %get-tuple-element.47), channel_id=1, source_target_pairs={{0,16},{8,24},{16,0},{24,8},{1,17},{9,25},{17,1},{25,9},{2,18},{10... | collective-permute-start | bytes 786440 | tf_op jit(solution)/shard_map/ppermute | solution.py:15
  30.8 9.2 %collective-permute-start.14 = (bf16[1,512,256]{2,1,0:T(8,128)(2,1)S(1)}, bf16[1,512,256]{2,1,0:T(8,128)(2,1)S(1)}, u32[]{:S(2)}, u32[]{:S(2)}) collective-permute-start(bf16[1,512,256]{2,1,0:T(8,128)(2,1)S(1)} %get-tuple-element.48), channel_id=1, source_target_pairs={{0,8},{8,0},{16,24},{24,16},{1,9},{9,1},{17,25},{25,17},{2,10},{10... | collective-permute-start | bytes 786440 | tf_op jit(solution)/shard_map/ppermute | solution.py:15
  32.8 8.9 %collective-permute-start.7 = (bf16[2,256,256]{2,1,0:T(8,128)(2,1)S(1)}, bf16[2,256,256]{2,1,0:T(8,128)(2,1)S(1)}, u32[]{:S(2)}, u32[]{:S(2)}) collective-permute-start(bf16[2,256,256]{2,1,0:T(8,128)(2,1)S(1)} %get-tuple-element.43), channel_id=1, source_target_pairs={{0,16},{8,24},{16,0},{24,8},{1,17},{9,25},{17,1},{25,9},{2,18},{10... | collective-permute-start | bytes 786440 | tf_op jit(solution)/shard_map/ppermute | solution.py:15
  33.4 9.4 %collective-permute-start.8 = (bf16[2,256,256]{2,1,0:T(8,128)(2,1)S(1)}, bf16[2,256,256]{2,1,0:T(8,128)(2,1)S(1)}, u32[]{:S(2)}, u32[]{:S(2)}) collective-permute-start(bf16[2,256,256]{2,1,0:T(8,128)(2,1)S(1)} %get-tuple-element.44), channel_id=1, source_target_pairs={{0,8},{8,0},{16,24},{24,16},{1,9},{9,1},{17,25},{25,17},{2,10},{10... | collective-permute-start | bytes 786440 | tf_op jit(solution)/shard_map/ppermute | solution.py:15
  40.1 6.4 %collective-permute-start.15 = (bf16[1,512,256]{2,1,0:T(8,128)(2,1)S(1)}, bf16[1,512,256]{2,1,0:T(8,128)(2,1)S(1)}, u32[]{:S(2)}, u32[]{:S(2)}) collective-permute-start(bf16[1,512,256]{2,1,0:T(8,128)(2,1)S(1)} %merge.9), channel_id=1, source_target_pairs={{0,2},{1,3},{2,0},{3,1},{4,6},{5,7},{6,4},{7,5},{8,10},{9,11},{10,... | collective-permute-start | bytes 786440 | tf_op jit(solution)/shard_map/ppermute | solution.py:15
  42.9 5.0 %collective-permute-start.9 = (bf16[1,256,256]{2,1,0:T(8,128)(2,1)S(1)}, bf16[1,256,256]{2,1,0:T(8,128)(2,1)S(1)}, u32[]{:S(2)}, u32[]{:S(2)}) collective-permute-start(bf16[1,256,256]{2,1,0:T(8,128)(2,1)S(1)} %get-tuple-element.45), channel_id=1, source_target_pairs={{0,8},{8,0},{16,24},{24,16},{1,9},{9,1},{17,25},{25,17},{2,10},{10... | collective-permute-start | bytes 393224 | tf_op jit(solution)/shard_map/ppermute | solution.py:15
  43.7 5.0 %collective-permute-start.10 = (bf16[1,256,256]{2,1,0:T(8,128)(2,1)S(1)}, bf16[1,256,256]{2,1,0:T(8,128)(2,1)S(1)}, u32[]{:S(2)}, u32[]{:S(2)}) collective-permute-start(bf16[1,256,256]{2,1,0:T(8,128)(2,1)S(1)} %get-tuple-element.46), channel_id=1, source_target_pairs={{0,16},{8,24},{16,0},{24,8},{1,17},{9,25},{17,1},{25,9},{2,18},{10... | collective-permute-start | bytes 393224 | tf_op jit(solution)/shard_map/ppermute | solution.py:15
  50.1 22.7 %collective-permute-start.16 = (bf16[4,256,512]{2,1,0:T(8,128)(2,1)}, bf16[4,256,512]{2,1,0:T(8,128)(2,1)S(1)}, u32[]{:S(2)}, u32[]{:S(2)}) collective-permute-start(bf16[4,256,512]{2,1,0:T(8,128)(2,1)} %get-tuple-element.52), channel_id=1, source_target_pairs={{0,8},{8,0},{16,24},{24,16},{1,9},{9,1},{17,25},{25,17},{2,10},{10... | collective-permute-start | bytes 3145736 | tf_op jit(solution)/shard_map/ppermute | solution.py:15
  51.4 23.4 %collective-permute-start.17 = (bf16[4,256,512]{2,1,0:T(8,128)(2,1)}, bf16[4,256,512]{2,1,0:T(8,128)(2,1)S(1)}, u32[]{:S(2)}, u32[]{:S(2)}) collective-permute-start(bf16[4,256,512]{2,1,0:T(8,128)(2,1)} %get-tuple-element.53), channel_id=1, source_target_pairs={{0,16},{8,24},{16,0},{24,8},{1,17},{9,25},{17,1},{25,9},{2,18},{10... | collective-permute-start | bytes 3145736 | tf_op jit(solution)/shard_map/ppermute | solution.py:15
  51.9 7.9 %collective-permute-start.20 = (bf16[1,256,256]{2,1,0:T(8,128)(2,1)S(1)}, bf16[1,256,256]{2,1,0:T(8,128)(2,1)}, u32[]{:S(2)}, u32[]{:S(2)}) collective-permute-start(bf16[1,256,256]{2,1,0:T(8,128)(2,1)S(1)} %get-tuple-element.49.refs_6_), channel_id=1, source_target_pairs={{0,4},{1,5},{2,6},{3,7},{4,0},{5,1},{6,2},{7,3},{8,12},{9,13},{10,... | collective-permute-start | bytes 393224 | tf_op jit(solution)/shard_map/ppermute | solution.py:15
  54.5 8.1 %collective-permute-start.21 = (bf16[1,256,256]{2,1,0:T(8,128)(2,1)}, bf16[1,256,256]{2,1,0:T(8,128)(2,1)}, u32[]{:S(2)}, u32[]{:S(2)}) collective-permute-start(bf16[1,256,256]{2,1,0:T(8,128)(2,1)} %get-tuple-element.58), channel_id=1, source_target_pairs={{0,4},{1,5},{2,6},{3,7},{4,0},{5,1},{6,2},{7,3},{8,12},{9,13},{10,... | collective-permute-start | bytes 393224 | tf_op jit(solution)/shard_map/ppermute | solution.py:15
  65.8 10.6 %collective-permute-start.22 = (bf16[2,256,256]{2,1,0:T(8,128)(2,1)S(1)}, bf16[2,256,256]{2,1,0:T(8,128)(2,1)S(1)}, u32[]{:S(2)}, u32[]{:S(2)}) collective-permute-start(bf16[2,256,256]{2,1,0:T(8,128)(2,1)S(1)} %amplitude.1.refs_10_.refs_0_), channel_id=1, source_target_pairs={{0,4},{1,5},{2,6},{3,7},{4,0},{5,1},{6,2},{7,3},{8,12},{9,13},{10,... | collective-permute-start | bytes 786440 | tf_op jit(solution)/shard_map/ppermute | solution.py:15
  65.9 13.5 %collective-permute-start.23 = (bf16[2,256,256]{2,1,0:T(8,128)(2,1)S(1)}, bf16[2,256,256]{2,1,0:T(8,128)(2,1)S(1)}, u32[]{:S(2)}, u32[]{:S(2)}) collective-permute-start(bf16[2,256,256]{2,1,0:T(8,128)(2,1)S(1)} %amplitude.1.refs_10_.refs_0_), channel_id=1, source_target_pairs={{0,2},{1,3},{2,0},{3,1},{4,6},{5,7},{6,4},{7,5},{8,10},{9,11},{10,... | collective-permute-start | bytes 786440 | tf_op jit(solution)/shard_map/ppermute | solution.py:15
  74.9 6.4 %collective-permute-start.18 = (bf16[1,256,512]{2,1,0:T(8,128)(2,1)S(1)}, bf16[1,256,512]{2,1,0:T(8,128)(2,1)S(1)}, u32[]{:S(2)}, u32[]{:S(2)}) collective-permute-start(bf16[1,256,512]{2,1,0:T(8,128)(2,1)S(1)} %get-tuple-element.54), channel_id=1, source_target_pairs={{0,16},{8,24},{16,0},{24,8},{1,17},{9,25},{17,1},{25,9},{2,18},{10... | collective-permute-start | bytes 786440 | tf_op jit(solution)/shard_map/ppermute | solution.py:15
  75.2 6.4 %collective-permute-start.19 = (bf16[1,256,512]{2,1,0:T(8,128)(2,1)S(1)}, bf16[1,256,512]{2,1,0:T(8,128)(2,1)S(1)}, u32[]{:S(2)}, u32[]{:S(2)}) collective-permute-start(bf16[1,256,512]{2,1,0:T(8,128)(2,1)S(1)} %get-tuple-element.55), channel_id=1, source_target_pairs={{0,8},{8,0},{16,24},{24,16},{1,9},{9,1},{17,25},{25,17},{2,10},{10... | collective-permute-start | bytes 786440 | tf_op jit(solution)/shard_map/ppermute | solution.py:15
  76.4 7.9 %collective-permute-start.24 = (bf16[2,256,256]{2,1,0:T(8,128)(2,1)S(1)}, bf16[2,256,256]{2,1,0:T(8,128)(2,1)S(1)}, u32[]{:S(2)}, u32[]{:S(2)}) collective-permute-start(bf16[2,256,256]{2,1,0:T(8,128)(2,1)S(1)} %collective-permute-done.22.refs_11_.refs_1_), channel_id=1, source_target_pairs={{0,2},{1,3},{2,0},{3,1},{4,6},{5,7},{6,4},{7,5},{8,10},{9,11},{10,... | collective-permute-start | bytes 786440 | tf_op jit(solution)/shard_map/ppermute | solution.py:15
  (10 other events, 96.4 us)

commit v7 on v6

--- a/solution.py
+++ b/solution.py
@@ -268,34 +268,33 @@
             out[k, pl.ds(part * rows, rows), pl.ds(i * width, width)] = total
 
 
-def density_last_kernel(chunks, plan, early, *refs):
+def density_last_kernel(chunks, plan, *refs):
     keys, spots, amp_keys = plan
     arrays, first, (out, gathered, turned) = refs[:-4], refs[-4], refs[-3:]
     step = pl.program_id(0)
     depth, width = gathered.shape[1:]
-    rows = out.shape[0] // 2
     my_core = lax.axis_index("aux") % 2
 
     @pl.when(step == 0)
     def _():
         gather_amplitudes(arrays, amp_keys, spots[2 * len(keys) :], chunks, gathered)
 
-    for place, (k, part) in enumerate(keys):
+    for k in range(len(keys) // 2):
 
         @pl.when(step == k)
-        def _(place=place, k=k, part=part):
-            halves = [take(arrays, spot) for spot in spots[2 * place : 2 * place + 2]]
-            sources = jnp.concatenate(halves, axis=1)
-            mine = slice(part * rows, (part + 1) * rows)
+        def _(k=k):
+            quarters = [take(arrays, spot) for spot in spots[4 * k : 4 * k + 4]]
+            halves = [jnp.concatenate(quarters[2 * part : 2 * part + 2], axis=1) for part in range(2)]
+            sources = jnp.concatenate(halves, axis=0)
             for core in range(2):
                 for chunk in range(chunks):
-                    done = depth - width if core == 0 and (k, part) in early else 0
+                    done = depth - width if core == 0 else 0
                     amps = gathered[core * chunks + chunk, done:]
                     total = jnp.dot(sources[:, done:], amps, preferred_element_type=F32)
                     if done:
-                        total += first[k, mine, chunk * width : (chunk + 1) * width]
+                        total += first[k, :, chunk * width : (chunk + 1) * width]
                     turned[(my_core if core == 0 else 1 - my_core) * chunks + chunk] = total.astype(BF16)
-            out[mine] = jnp.swapaxes(turned[...], 0, 1)
+            out[...] = jnp.swapaxes(turned[...], 0, 1)
 
 
 def density_plan(sources, amps):
@@ -320,18 +319,18 @@
     )(*arrays)
 
 
-def density_last(sources, early, amps, first, n_occ, chunks):
+def density_last(sources, amps, first, n_occ, chunks):
     arrays, plan, rows, columns = density_plan(sources, amps)
     width = cut(*amps[0, 0, 0])[1]
     vmem = pl.BlockSpec(memory_space=pltpu.VMEM)
     return pl.pallas_call(
-        functools.partial(density_last_kernel, chunks, plan, early),
+        functools.partial(density_last_kernel, chunks, plan),
         grid=(n_occ,),
         in_specs=[vmem] * (len(arrays) + 1),
         out_specs=pl.BlockSpec((rows, 2 * chunks, width), lambda k: (k ^ lax.axis_index("occ"), 0, 0)),
         scratch_shapes=[
             pltpu.VMEM((2 * chunks, columns, width), BF16),
-            pltpu.VMEM((2 * chunks, rows // 2, width), BF16),
+            pltpu.VMEM((2 * chunks, rows, width), BF16),
         ],
         out_shape=jax.ShapeDtypeStruct((n_occ * rows, 2 * chunks, width), BF16),
         compiler_params=pltpu.CompilerParams(vmem_limit_bytes=20 * MIB),
@@ -474,7 +473,7 @@
         arrived = swap(packed, "aux", n_aux, 1)
         for j, (_, step, c) in enumerate(own):
             amps[1, step, c] = (arrived, (j,))
-        return density_last(sources, set(early), amps, first, n_occ, chunks)
+        return density_last(sources, amps, first, n_occ, chunks)
 
     in_specs = (P(("aux", "occ"), None, None), P(), P(), P(), P(), P())
     out_specs = P("aux", "occ", None)

time: 93.2 us -> 93.3 us (level)
  no operation moved by 1% of the time
where the time goes in v7:
time: 93.3 us; the launch traced here: 93 us
  starting transfers between devices  34.1 us (37%)
  waiting for transfers between devices  32.8 us (35%)
  Pallas kernels  20.2 us (22%)
  local copies, waits for them, and re-layouts  4.35 us (5%)
  between operations  1.49 us (2%)
    ppermute x26, starting transfers between devices, swap(): return lax.ppermute(value, axis, [(d, d ^ mask) for d in range(size)])  34.1 us
    ppermute x26, waiting for transfers between devices, swap(): return lax.ppermute(value, axis, [(d, d ^ mask) for d in range(size)])  32.8 us
    pallas_call x1, Pallas kernels, density_last(): pl.pallas_call(functools.partial(density_last_kernel, chunks, plan), grid...  5.82 us
    pallas_call x5, Pallas kernels, pair(): pl.pallas_call(functools.partial(pair_kernel, pieces), in_specs=[vmem] *...  4.07 us
    unnamed x16, local copies, waits for them, and re-layouts  3.57 us
    pallas_call x1, Pallas kernels, prepare(): pl.pallas_call(functools.partial(prepare_kernel, n_occ, chunks, src_count...  3.18 us
    pallas_call x7, Pallas kernels, merge(): pl.pallas_call(kernel, in_specs=[vmem] * len(arrays) + [vmem, smem, smem,...  2.57 us
  transfers between devices with their start and end apart: 26, of which 18 were waited for; matrix products, arithmetic and copies ran while one was open for 1% of the time, Pallas kernels for 11%

profile of v7, /device:TPU:0, one launch (start us, length us, event | category | flops | bytes accessed | tf_op | source)
XLA Modules:
  0.0 93.0 jit_solution(13072887859512954979)
XLA Ops:
  0.0 3.2 %prepare.1 = (bf16[256,512]{1,0:T(8,128)(2,1)S(1)}, bf16[256,512]{1,0:T(8,128)(2,1)S(1)}, bf16[256,512]{1,0:T(8,128)(2,1)S(1)}, bf16[256,512]{1,0:T(8,128)(2,1)S...) custom-call(s32[4]{0:T(128)} %refs_7_.1, ...), custom_call_target="tpu_custom_call" | custom-call | tf_op jit(solution)/shard_map/prepare/pallas_call | solution.py:68
  4.2 2.6 %collective-permute-start = (bf16[256,512]{1,0:T(8,128)(2,1)S(1)}, bf16[256,512]{1,0:T(8,128)(2,1)S(1)}, u32[]{:S(2)}, u32[]{:S(2)}) collective-permute-start(bf16[256,512]{1,0:T(8,128)(2,1)S(1)} %get-tuple-element.32.refs_0_), channel_id=1, source_target_pairs={{0,8},{8,0},{16,24},{24,16},{1,9},{9,1},{17,25},{25,17},{2,10},{10... | collective-permute-start | bytes 786440 | tf_op jit(solution)/shard_map/ppermute | solution.py:15
  6.8 1.5 %collective-permute-start.5 = (bf16[256,512]{1,0:T(8,128)(2,1)S(1)}, bf16[256,512]{1,0:T(8,128)(2,1)S(1)}, u32[]{:S(2)}, u32[]{:S(2)}) collective-permute-start(bf16[256,512]{1,0:T(8,128)(2,1)S(1)} %get-tuple-element.33.refs_4_.refs_1_), channel_id=1, source_target_pairs={{0,16},{8,24},{16,0},{24,8},{1,17},{9,25},{17,1},{25,9},{2,18},{10... | collective-permute-start | bytes 786440 | tf_op jit(solution)/shard_map/ppermute | solution.py:15
  9.0 2.2 %collective-permute-start.4 = (bf16[4,256,256]{2,1,0:T(8,128)(2,1)S(1)}, bf16[4,256,256]{2,1,0:T(8,128)(2,1)S(1)}, u32[]{:S(2)}, u32[]{:S(2)}) collective-permute-start(bf16[4,256,256]{2,1,0:T(8,128)(2,1)S(1)} %pair.5.refs_0_), channel_id=1, source_target_pairs={{0,2},{1,3},{2,0},{3,1},{4,6},{5,7},{6,4},{7,5},{8,10},{9,11},{10,... | collective-permute-start | bytes 1572872 | tf_op jit(solution)/shard_map/ppermute | solution.py:15
  11.9 1.6 %collective-permute-start.11 = (bf16[2,512,256]{2,1,0:T(8,128)(2,1)S(1)}, bf16[2,512,256]{2,1,0:T(8,128)(2,1)S(1)}, u32[]{:S(2)}, u32[]{:S(2)}) collective-permute-start(bf16[2,512,256]{2,1,0:T(8,128)(2,1)S(1)} %pair.7.refs_0_), channel_id=1, source_target_pairs={{0,8},{8,0},{16,24},{24,16},{1,9},{9,1},{17,25},{25,17},{2,10},{10... | collective-permute-start | bytes 1572872 | tf_op jit(solution)/shard_map/ppermute | solution.py:15
  13.7 1.5 %collective-permute-done.5.refs_2_.refs_5_.refs_7_ = bf16[256,512]{1,0:T(8,128)(2,1)S(1)} collective-permute-done((bf16[256,512]{1,0:T(8,128)(2,1)S(1)}, bf16[256,512]{1,0:T(8,128)(2,1)S(1)}, u32[]{:S(2)}, u32[]{:S(2)}) %collective-permute-start.5) | collective-permute-done | bytes 262176 | tf_op jit(solution)/shard_map/ppermute | solution.py:15
  15.9 1.6 %collective-permute-start.12 = (bf16[2,512,256]{2,1,0:T(8,128)(2,1)S(1)}, bf16[2,512,256]{2,1,0:T(8,128)(2,1)S(1)}, u32[]{:S(2)}, u32[]{:S(2)}) collective-permute-start(bf16[2,512,256]{2,1,0:T(8,128)(2,1)S(1)} %pair.8.refs_1_), channel_id=1, source_target_pairs={{0,16},{8,24},{16,0},{24,8},{1,17},{9,25},{17,1},{25,9},{2,18},{10... | collective-permute-start | bytes 1572872 | tf_op jit(solution)/shard_map/ppermute | solution.py:15
  18.2 1.6 %collective-permute-start.6 = (bf16[4,256,256]{2,1,0:T(8,128)(2,1)S(1)}, bf16[4,256,256]{2,1,0:T(8,128)(2,1)S(1)}, u32[]{:S(2)}, u32[]{:S(2)}) collective-permute-start(bf16[4,256,256]{2,1,0:T(8,128)(2,1)S(1)} %pair.9), channel_id=1, source_target_pairs={{0,2},{1,3},{2,0},{3,1},{4,6},{5,7},{6,4},{7,5},{8,10},{9,11},{10,... | collective-permute-start | bytes 1572872 | tf_op jit(solution)/shard_map/ppermute | solution.py:15
  19.8 4.1 %collective-permute-done.4.refs_0_.refs_1_ = bf16[4,256,256]{2,1,0:T(8,128)(2,1)S(1)} collective-permute-done((bf16[4,256,256]{2,1,0:T(8,128)(2,1)S(1)}, bf16[4,256,256]{2,1,0:T(8,128)(2,1)S(1)}, u32[]{:S(2)}, u32[]{:S(2)}) %collective-permute-start.4) | collective-permute-done | bytes 524320 | tf_op jit(solution)/shard_map/ppermute | solution.py:15
  25.7 3.4 %collective-permute-done.12.refs_3_.refs_1_ = bf16[2,512,256]{2,1,0:T(8,128)(2,1)S(1)} collective-permute-done((bf16[2,512,256]{2,1,0:T(8,128)(2,1)S(1)}, bf16[2,512,256]{2,1,0:T(8,128)(2,1)S(1)}, u32[]{:S(2)}, u32[]{:S(2)}) %collective-permute-start.12) | collective-permute-done | bytes 524320 | tf_op jit(solution)/shard_map/ppermute | solution.py:15
  29.2 1.6 %collective-permute-start.13 = (bf16[1,512,256]{2,1,0:T(8,128)(2,1)S(1)}, bf16[1,512,256]{2,1,0:T(8,128)(2,1)S(1)}, u32[]{:S(2)}, u32[]{:S(2)}) collective-permute-start(bf16[1,512,256]{2,1,0:T(8,128)(2,1)S(1)} %get-tuple-element.47), channel_id=1, source_target_pairs={{0,16},{8,24},{16,0},{24,8},{1,17},{9,25},{17,1},{25,9},{2,18},{10... | collective-permute-start | bytes 786440 | tf_op jit(solution)/shard_map/ppermute | solution.py:15
  34.8 3.6 %collective-permute-done.13.refs_3_.refs_2_ = bf16[1,512,256]{2,1,0:T(8,128)(2,1)S(1)} collective-permute-done((bf16[1,512,256]{2,1,0:T(8,128)(2,1)S(1)}, bf16[1,512,256]{2,1,0:T(8,128)(2,1)S(1)}, u32[]{:S(2)}, u32[]{:S(2)}) %collective-permute-start.13) | collective-permute-done | bytes 262176 | tf_op jit(solution)/shard_map/ppermute | solution.py:15
  38.4 1.5 %collective-permute-done.14.refs_2_ = bf16[1,512,256]{2,1,0:T(8,128)(2,1)S(1)} collective-permute-done((bf16[1,512,256]{2,1,0:T(8,128)(2,1)S(1)}, bf16[1,512,256]{2,1,0:T(8,128)(2,1)S(1)}, u32[]{:S(2)}, u32[]{:S(2)}) %collective-permute-start.14) | collective-permute-done | bytes 262176 | tf_op jit(solution)/shard_map/ppermute | solution.py:15
  40.1 1.6 %collective-permute-start.15 = (bf16[1,512,256]{2,1,0:T(8,128)(2,1)S(1)}, bf16[1,512,256]{2,1,0:T(8,128)(2,1)S(1)}, u32[]{:S(2)}, u32[]{:S(2)}) collective-permute-start(bf16[1,512,256]{2,1,0:T(8,128)(2,1)S(1)} %merge.9), channel_id=1, source_target_pairs={{0,2},{1,3},{2,0},{3,1},{4,6},{5,7},{6,4},{7,5},{8,10},{9,11},{10,... | collective-permute-start | bytes 786440 | tf_op jit(solution)/shard_map/ppermute | solution.py:15
  51.9 2.6 %collective-permute-start.20 = (bf16[1,256,256]{2,1,0:T(8,128)(2,1)S(1)}, bf16[1,256,256]{2,1,0:T(8,128)(2,1)}, u32[]{:S(2)}, u32[]{:S(2)}) collective-permute-start(bf16[1,256,256]{2,1,0:T(8,128)(2,1)S(1)} %get-tuple-element.49.refs_6_), channel_id=1, source_target_pairs={{0,4},{1,5},{2,6},{3,7},{4,0},{5,1},{6,2},{7,3},{8,12},{9,13},{10,... | collective-permute-start | bytes 393224 | tf_op jit(solution)/shard_map/ppermute | solution.py:15
  56.9 2.9 %collective-permute-done.20.refs_1_ = bf16[1,256,256]{2,1,0:T(8,128)(2,1)} collective-permute-done((bf16[1,256,256]{2,1,0:T(8,128)(2,1)S(1)}, bf16[1,256,256]{2,1,0:T(8,128)(2,1)}, u32[]{:S(2)}, u32[]{:S(2)}) %collective-permute-start.20) | collective-permute-done | bytes 131104 | tf_op jit(solution)/shard_map/ppermute | solution.py:15
  59.8 2.8 %collective-permute-done.21.refs_3_ = bf16[1,256,256]{2,1,0:T(8,128)(2,1)} collective-permute-done((bf16[1,256,256]{2,1,0:T(8,128)(2,1)}, bf16[1,256,256]{2,1,0:T(8,128)(2,1)}, u32[]{:S(2)}, u32[]{:S(2)}) %collective-permute-start.21) | collective-permute-done | bytes 131104 | tf_op jit(solution)/shard_map/ppermute | solution.py:15
  65.9 6.8 %collective-permute-start.23 = (bf16[2,256,256]{2,1,0:T(8,128)(2,1)S(1)}, bf16[2,256,256]{2,1,0:T(8,128)(2,1)S(1)}, u32[]{:S(2)}, u32[]{:S(2)}) collective-permute-start(bf16[2,256,256]{2,1,0:T(8,128)(2,1)S(1)} %amplitude.1.refs_10_.refs_0_), channel_id=1, source_target_pairs={{0,2},{1,3},{2,0},{3,1},{4,6},{5,7},{6,4},{7,5},{8,10},{9,11},{10,... | collective-permute-start | bytes 786440 | tf_op jit(solution)/shard_map/ppermute | solution.py:15
  72.8 2.1 %collective-permute-done.17.refs_1_.refs_6_ = bf16[4,256,512]{2,1,0:T(8,128)(2,1)S(1)} collective-permute-done((bf16[4,256,512]{2,1,0:T(8,128)(2,1)}, bf16[4,256,512]{2,1,0:T(8,128)(2,1)S(1)}, u32[]{:S(2)}, u32[]{:S(2)}) %collective-permute-start.17) | collective-permute-done | bytes 1048608 | tf_op jit(solution)/shard_map/ppermute | solution.py:15
  77.7 1.7 %collective-permute-done.23.refs_12_.refs_2_ = bf16[2,256,256]{2,1,0:T(8,128)(2,1)S(1)} collective-permute-done((bf16[2,256,256]{2,1,0:T(8,128)(2,1)S(1)}, bf16[2,256,256]{2,1,0:T(8,128)(2,1)S(1)}, u32[]{:S(2)}, u32[]{:S(2)}) %collective-permute-start.23) | collective-permute-done | bytes 262176 | tf_op jit(solution)/shard_map/ppermute | solution.py:15
  79.4 1.9 %collective-permute-done.18.refs_8_ = bf16[1,256,512]{2,1,0:T(8,128)(2,1)S(1)} collective-permute-done((bf16[1,256,512]{2,1,0:T(8,128)(2,1)S(1)}, bf16[1,256,512]{2,1,0:T(8,128)(2,1)S(1)}, u32[]{:S(2)}, u32[]{:S(2)}) %collective-permute-start.18) | collective-permute-done | bytes 262176 | tf_op jit(solution)/shard_map/ppermute | solution.py:15
  82.5 1.8 %density_first.1.refs_4_.refs_15_ = f32[4,512,512]{2,1,0:T(8,128)S(1)} custom-call(bf16[256,512]{1,0:T(8,128)(2,1)S(1)} %get-tuple-element.32.refs_0_, bf16[256,512]{1,0:T(8,128)(2,1)S(1)} %get-tuple-element.33.refs_4_.refs_1_, bf16[256,512]{1,0:T(8,128)(2,1)S(1)} %get-tuple-element.34.refs_2_, bf16[256,512]{1,0:T(8,128)(2,1)S(1)} %copy-done.1, ...), custom_call_target="tpu_custom_call" | custom-call | tf_op jit(solution)/shard_map/density_first/pallas_call | solution.py:311
  84.5 2.6 %collective-permute-done.25.refs_14_ = bf16[8,256,256]{2,1,0:T(8,128)(2,1)S(1)} collective-permute-done((bf16[8,256,256]{2,1,0:T(8,128)(2,1)S(1)}, bf16[8,256,256]{2,1,0:T(8,128)(2,1)S(1)}, u32[]{:S(2)}, u32[]{:S(2)}) %collective-permute-start.25) | collective-permute-done | bytes 1048608 | tf_op jit(solution)/shard_map/ppermute | solution.py:15
  87.2 5.8 %density_last.1 = bf16[2048,4,256]{2,1,0:T(4,128)(2,1)} custom-call(bf16[256,512]{1,0:T(8,128)(2,1)S(1)} %get-tuple-element.32.refs_0_, bf16[256,512]{1,0:T(8,128)(2,1)S(1)} %get-tuple-element.33.refs_4_.refs_1_, bf16[256,512]{1,0:T(8,128)(2,1)S(1)} %get-tuple-element.34.refs_2_, bf16[256,512]{1,0:T(8,128)(2,1)S(1)} %copy-done.1, ...), custom_call_target="tpu_custom_call" | custom-call | tf_op jit(solution)/shard_map/density_last/pallas_call | solution.py:326
  (64 shorter events, 28.8 us)
Async XLA Ops:
  3.2 5.1 %collective-permute-start.2 = (bf16[4,512,256]{2,1,0:T(8,128)(2,1)S(1)}, bf16[4,512,256]{2,1,0:T(8,128)(2,1)S(1)}, u32[]{:S(2)}, u32[]{:S(2)}) collective-permute-start(bf16[4,512,256]{2,1,0:T(8,128)(2,1)S(1)} %get-tuple-element.38), channel_id=1, source_target_pairs={{0,1},{1,0},{2,3},{3,2},{4,5},{5,4},{6,7},{7,6},{8,9},{9,8},{10,11... | collective-permute-start | bytes 3145736 | tf_op jit(solution)/shard_map/ppermute | solution.py:15
  3.8 7.4 %collective-permute-start.3 = (bf16[4,512,256]{2,1,0:T(8,128)(2,1)S(1)}, bf16[4,512,256]{2,1,0:T(8,128)(2,1)S(1)}, u32[]{:S(2)}, u32[]{:S(2)}) collective-permute-start(bf16[4,512,256]{2,1,0:T(8,128)(2,1)S(1)} %get-tuple-element.40), channel_id=1, source_target_pairs={{0,1},{1,0},{2,3},{3,2},{4,5},{5,4},{6,7},{7,6},{8,9},{9,8},{10,11... | collective-permute-start | bytes 3145736 | tf_op jit(solution)/shard_map/ppermute | solution.py:15
  4.2 9.5 %collective-permute-start = (bf16[256,512]{1,0:T(8,128)(2,1)S(1)}, bf16[256,512]{1,0:T(8,128)(2,1)S(1)}, u32[]{:S(2)}, u32[]{:S(2)}) collective-permute-start(bf16[256,512]{1,0:T(8,128)(2,1)S(1)} %get-tuple-element.32.refs_0_), channel_id=1, source_target_pairs={{0,8},{8,0},{16,24},{24,16},{1,9},{9,1},{17,25},{25,17},{2,10},{10... | collective-permute-start | bytes 786440 | tf_op jit(solution)/shard_map/ppermute | solution.py:15
  6.8 8.4 %collective-permute-start.5 = (bf16[256,512]{1,0:T(8,128)(2,1)S(1)}, bf16[256,512]{1,0:T(8,128)(2,1)S(1)}, u32[]{:S(2)}, u32[]{:S(2)}) collective-permute-start(bf16[256,512]{1,0:T(8,128)(2,1)S(1)} %get-tuple-element.33.refs_4_.refs_1_), channel_id=1, source_target_pairs={{0,16},{8,24},{16,0},{24,8},{1,17},{9,25},{17,1},{25,9},{2,18},{10... | collective-permute-start | bytes 786440 | tf_op jit(solution)/shard_map/ppermute | solution.py:15
  9.0 14.9 %collective-permute-start.4 = (bf16[4,256,256]{2,1,0:T(8,128)(2,1)S(1)}, bf16[4,256,256]{2,1,0:T(8,128)(2,1)S(1)}, u32[]{:S(2)}, u32[]{:S(2)}) collective-permute-start(bf16[4,256,256]{2,1,0:T(8,128)(2,1)S(1)} %pair.5.refs_0_), channel_id=1, source_target_pairs={{0,2},{1,3},{2,0},{3,1},{4,6},{5,7},{6,4},{7,5},{8,10},{9,11},{10,... | collective-permute-start | bytes 1572872 | tf_op jit(solution)/shard_map/ppermute | solution.py:15
  11.9 13.8 %collective-permute-start.11 = (bf16[2,512,256]{2,1,0:T(8,128)(2,1)S(1)}, bf16[2,512,256]{2,1,0:T(8,128)(2,1)S(1)}, u32[]{:S(2)}, u32[]{:S(2)}) collective-permute-start(bf16[2,512,256]{2,1,0:T(8,128)(2,1)S(1)} %pair.7.refs_0_), channel_id=1, source_target_pairs={{0,8},{8,0},{16,24},{24,16},{1,9},{9,1},{17,25},{25,17},{2,10},{10... | collective-permute-start | bytes 1572872 | tf_op jit(solution)/shard_map/ppermute | solution.py:15
  15.9 13.2 %collective-permute-start.12 = (bf16[2,512,256]{2,1,0:T(8,128)(2,1)S(1)}, bf16[2,512,256]{2,1,0:T(8,128)(2,1)S(1)}, u32[]{:S(2)}, u32[]{:S(2)}) collective-permute-start(bf16[2,512,256]{2,1,0:T(8,128)(2,1)S(1)} %pair.8.refs_1_), channel_id=1, source_target_pairs={{0,16},{8,24},{16,0},{24,8},{1,17},{9,25},{17,1},{25,9},{2,18},{10... | collective-permute-start | bytes 1572872 | tf_op jit(solution)/shard_map/ppermute | solution.py:15
  18.2 23.5 %collective-permute-start.6 = (bf16[4,256,256]{2,1,0:T(8,128)(2,1)S(1)}, bf16[4,256,256]{2,1,0:T(8,128)(2,1)S(1)}, u32[]{:S(2)}, u32[]{:S(2)}) collective-permute-start(bf16[4,256,256]{2,1,0:T(8,128)(2,1)S(1)} %pair.9), channel_id=1, source_target_pairs={{0,2},{1,3},{2,0},{3,1},{4,6},{5,7},{6,4},{7,5},{8,10},{9,11},{10,... | collective-permute-start | bytes 1572872 | tf_op jit(solution)/shard_map/ppermute | solution.py:15
  29.2 9.2 %collective-permute-start.13 = (bf16[1,512,256]{2,1,0:T(8,128)(2,1)S(1)}, bf16[1,512,256]{2,1,0:T(8,128)(2,1)S(1)}, u32[]{:S(2)}, u32[]{:S(2)}) collective-permute-start(bf16[1,512,256]{2,1,0:T(8,128)(2,1)S(1)} %get-tuple-element.47), channel_id=1, source_target_pairs={{0,16},{8,24},{16,0},{24,8},{1,17},{9,25},{17,1},{25,9},{2,18},{10... | collective-permute-start | bytes 786440 | tf_op jit(solution)/shard_map/ppermute | solution.py:15
  30.8 9.2 %collective-permute-start.14 = (bf16[1,512,256]{2,1,0:T(8,128)(2,1)S(1)}, bf16[1,512,256]{2,1,0:T(8,128)(2,1)S(1)}, u32[]{:S(2)}, u32[]{:S(2)}) collective-permute-start(bf16[1,512,256]{2,1,0:T(8,128)(2,1)S(1)} %get-tuple-element.48), channel_id=1, source_target_pairs={{0,8},{8,0},{16,24},{24,16},{1,9},{9,1},{17,25},{25,17},{2,10},{10... | collective-permute-start | bytes 786440 | tf_op jit(solution)/shard_map/ppermute | solution.py:15
  32.8 8.9 %collective-permute-start.7 = (bf16[2,256,256]{2,1,0:T(8,128)(2,1)S(1)}, bf16[2,256,256]{2,1,0:T(8,128)(2,1)S(1)}, u32[]{:S(2)}, u32[]{:S(2)}) collective-permute-start(bf16[2,256,256]{2,1,0:T(8,128)(2,1)S(1)} %get-tuple-element.43), channel_id=1, source_target_pairs={{0,16},{8,24},{16,0},{24,8},{1,17},{9,25},{17,1},{25,9},{2,18},{10... | collective-permute-start | bytes 786440 | tf_op jit(solution)/shard_map/ppermute | solution.py:15
  33.4 9.4 %collective-permute-start.8 = (bf16[2,256,256]{2,1,0:T(8,128)(2,1)S(1)}, bf16[2,256,256]{2,1,0:T(8,128)(2,1)S(1)}, u32[]{:S(2)}, u32[]{:S(2)}) collective-permute-start(bf16[2,256,256]{2,1,0:T(8,128)(2,1)S(1)} %get-tuple-element.44), channel_id=1, source_target_pairs={{0,8},{8,0},{16,24},{24,16},{1,9},{9,1},{17,25},{25,17},{2,10},{10... | collective-permute-start | bytes 786440 | tf_op jit(solution)/shard_map/ppermute | solution.py:15
  40.1 6.4 %collective-permute-start.15 = (bf16[1,512,256]{2,1,0:T(8,128)(2,1)S(1)}, bf16[1,512,256]{2,1,0:T(8,128)(2,1)S(1)}, u32[]{:S(2)}, u32[]{:S(2)}) collective-permute-start(bf16[1,512,256]{2,1,0:T(8,128)(2,1)S(1)} %merge.9), channel_id=1, source_target_pairs={{0,2},{1,3},{2,0},{3,1},{4,6},{5,7},{6,4},{7,5},{8,10},{9,11},{10,... | collective-permute-start | bytes 786440 | tf_op jit(solution)/shard_map/ppermute | solution.py:15
  42.9 5.0 %collective-permute-start.9 = (bf16[1,256,256]{2,1,0:T(8,128)(2,1)S(1)}, bf16[1,256,256]{2,1,0:T(8,128)(2,1)S(1)}, u32[]{:S(2)}, u32[]{:S(2)}) collective-permute-start(bf16[1,256,256]{2,1,0:T(8,128)(2,1)S(1)} %get-tuple-element.45), channel_id=1, source_target_pairs={{0,8},{8,0},{16,24},{24,16},{1,9},{9,1},{17,25},{25,17},{2,10},{10... | collective-permute-start | bytes 393224 | tf_op jit(solution)/shard_map/ppermute | solution.py:15
  43.7 5.0 %collective-permute-start.10 = (bf16[1,256,256]{2,1,0:T(8,128)(2,1)S(1)}, bf16[1,256,256]{2,1,0:T(8,128)(2,1)S(1)}, u32[]{:S(2)}, u32[]{:S(2)}) collective-permute-start(bf16[1,256,256]{2,1,0:T(8,128)(2,1)S(1)} %get-tuple-element.46), channel_id=1, source_target_pairs={{0,16},{8,24},{16,0},{24,8},{1,17},{9,25},{17,1},{25,9},{2,18},{10... | collective-permute-start | bytes 393224 | tf_op jit(solution)/shard_map/ppermute | solution.py:15
  50.1 22.7 %collective-permute-start.16 = (bf16[4,256,512]{2,1,0:T(8,128)(2,1)}, bf16[4,256,512]{2,1,0:T(8,128)(2,1)S(1)}, u32[]{:S(2)}, u32[]{:S(2)}) collective-permute-start(bf16[4,256,512]{2,1,0:T(8,128)(2,1)} %get-tuple-element.52), channel_id=1, source_target_pairs={{0,8},{8,0},{16,24},{24,16},{1,9},{9,1},{17,25},{25,17},{2,10},{10... | collective-permute-start | bytes 3145736 | tf_op jit(solution)/shard_map/ppermute | solution.py:15
  51.4 23.4 %collective-permute-start.17 = (bf16[4,256,512]{2,1,0:T(8,128)(2,1)}, bf16[4,256,512]{2,1,0:T(8,128)(2,1)S(1)}, u32[]{:S(2)}, u32[]{:S(2)}) collective-permute-start(bf16[4,256,512]{2,1,0:T(8,128)(2,1)} %get-tuple-element.53), channel_id=1, source_target_pairs={{0,16},{8,24},{16,0},{24,8},{1,17},{9,25},{17,1},{25,9},{2,18},{10... | collective-permute-start | bytes 3145736 | tf_op jit(solution)/shard_map/ppermute | solution.py:15
  51.9 7.9 %collective-permute-start.20 = (bf16[1,256,256]{2,1,0:T(8,128)(2,1)S(1)}, bf16[1,256,256]{2,1,0:T(8,128)(2,1)}, u32[]{:S(2)}, u32[]{:S(2)}) collective-permute-start(bf16[1,256,256]{2,1,0:T(8,128)(2,1)S(1)} %get-tuple-element.49.refs_6_), channel_id=1, source_target_pairs={{0,4},{1,5},{2,6},{3,7},{4,0},{5,1},{6,2},{7,3},{8,12},{9,13},{10,... | collective-permute-start | bytes 393224 | tf_op jit(solution)/shard_map/ppermute | solution.py:15
  54.5 8.1 %collective-permute-start.21 = (bf16[1,256,256]{2,1,0:T(8,128)(2,1)}, bf16[1,256,256]{2,1,0:T(8,128)(2,1)}, u32[]{:S(2)}, u32[]{:S(2)}) collective-permute-start(bf16[1,256,256]{2,1,0:T(8,128)(2,1)} %get-tuple-element.58), channel_id=1, source_target_pairs={{0,4},{1,5},{2,6},{3,7},{4,0},{5,1},{6,2},{7,3},{8,12},{9,13},{10,... | collective-permute-start | bytes 393224 | tf_op jit(solution)/shard_map/ppermute | solution.py:15
  65.8 10.6 %collective-permute-start.22 = (bf16[2,256,256]{2,1,0:T(8,128)(2,1)S(1)}, bf16[2,256,256]{2,1,0:T(8,128)(2,1)S(1)}, u32[]{:S(2)}, u32[]{:S(2)}) collective-permute-start(bf16[2,256,256]{2,1,0:T(8,128)(2,1)S(1)} %amplitude.1.refs_10_.refs_0_), channel_id=1, source_target_pairs={{0,4},{1,5},{2,6},{3,7},{4,0},{5,1},{6,2},{7,3},{8,12},{9,13},{10,... | collective-permute-start | bytes 786440 | tf_op jit(solution)/shard_map/ppermute | solution.py:15
  65.9 13.5 %collective-permute-start.23 = (bf16[2,256,256]{2,1,0:T(8,128)(2,1)S(1)}, bf16[2,256,256]{2,1,0:T(8,128)(2,1)S(1)}, u32[]{:S(2)}, u32[]{:S(2)}) collective-permute-start(bf16[2,256,256]{2,1,0:T(8,128)(2,1)S(1)} %amplitude.1.refs_10_.refs_0_), channel_id=1, source_target_pairs={{0,2},{1,3},{2,0},{3,1},{4,6},{5,7},{6,4},{7,5},{8,10},{9,11},{10,... | collective-permute-start | bytes 786440 | tf_op jit(solution)/shard_map/ppermute | solution.py:15
  74.9 6.4 %collective-permute-start.18 = (bf16[1,256,512]{2,1,0:T(8,128)(2,1)S(1)}, bf16[1,256,512]{2,1,0:T(8,128)(2,1)S(1)}, u32[]{:S(2)}, u32[]{:S(2)}) collective-permute-start(bf16[1,256,512]{2,1,0:T(8,128)(2,1)S(1)} %get-tuple-element.54), channel_id=1, source_target_pairs={{0,16},{8,24},{16,0},{24,8},{1,17},{9,25},{17,1},{25,9},{2,18},{10... | collective-permute-start | bytes 786440 | tf_op jit(solution)/shard_map/ppermute | solution.py:15
  75.2 6.4 %collective-permute-start.19 = (bf16[1,256,512]{2,1,0:T(8,128)(2,1)S(1)}, bf16[1,256,512]{2,1,0:T(8,128)(2,1)S(1)}, u32[]{:S(2)}, u32[]{:S(2)}) collective-permute-start(bf16[1,256,512]{2,1,0:T(8,128)(2,1)S(1)} %get-tuple-element.55), channel_id=1, source_target_pairs={{0,8},{8,0},{16,24},{24,16},{1,9},{9,1},{17,25},{25,17},{2,10},{10... | collective-permute-start | bytes 786440 | tf_op jit(solution)/shard_map/ppermute | solution.py:15
  76.4 7.9 %collective-permute-start.24 = (bf16[2,256,256]{2,1,0:T(8,128)(2,1)S(1)}, bf16[2,256,256]{2,1,0:T(8,128)(2,1)S(1)}, u32[]{:S(2)}, u32[]{:S(2)}) collective-permute-start(bf16[2,256,256]{2,1,0:T(8,128)(2,1)S(1)} %collective-permute-done.22.refs_11_.refs_1_), channel_id=1, source_target_pairs={{0,2},{1,3},{2,0},{3,1},{4,6},{5,7},{6,4},{7,5},{8,10},{9,11},{10,... | collective-permute-start | bytes 786440 | tf_op jit(solution)/shard_map/ppermute | solution.py:15
  (10 other events, 96.4 us)
